TPU v7x, 32 devices: a whole 2x2x4 slice. The times are simulated.
32 devices in a mesh: groups: 2 (over x), gx: 16 (over z, y, core).
Axes of the slice: x: 2, y: 2, z: 4, core: 2. Of those that a mesh axis runs over, the one named last changes fastest.
Arguments:
- permeability: float32 [512, 1024], P(('groups', 'gx')), parts along dimension 0, may hold values from 0.05 to 20
- storage: float32 [512, 1024], P(('groups', 'gx')), parts along dimension 0, may hold values from 0.02 to 0.5
- support_mask: int32 [32, 2, 2, 32, 32], P(('groups', 'gx')), parts along dimension 0, may hold values from 0 to 262143
- prev_basis: float32 [32, 2, 2, 32, 1024], P(('groups', 'gx')), parts along dimension 0, may hold values from 0 to 1
Outputs:
- basis: float32 [32, 2, 2, 32, 1024], P(('groups', 'gx')), parts along dimension 0
- coarse_matrix: float32 [32, 2, 2, 27], P(('groups', 'gx')), parts along dimension 0
There are 2 independent parts, one for each index of `groups`. A program takes and returns all parts, laid end to end along the dimension named above; each array names one. Nothing has to cross between parts.
All inputs are finite; a program needn't handle non-finite values.
Results may differ from a plain program's by a relative error of at most 0.0003.
Values sent between devices are 32-bit elements; how exact they have to be, the bound alone decides.
No kernel may reach another device: no remote copies, remote signals or barrier semaphores. Data moves between devices by JAX's collectives and lax.ppermute only.
A program may use at most 128 MiB of HBM per device.

v0:
```python
import functools

import jax
import jax.numpy as jnp
from jax import lax
from jax.experimental import pallas as pl
from jax.experimental.pallas import tpu as pltpu
from jax.sharding import PartitionSpec as P

ITERS = 2
SUM_FLOOR = 0.5
TINY = 1e-30
F32 = jnp.float32


BLOCKS = 4
LANE_TILES = 8
USED = 6

PERM_AT = 2 * BLOCKS * USED
STOR_AT = PERM_AT + LANE_TILES
MASK_AT = STOR_AT + LANE_TILES
REST_AT = MASK_AT + 2
REST = BLOCKS * USED + 2 * LANE_TILES + 1
REST_SLOTS = (REST + 1) // 2
MESSAGE = REST_AT + REST_SLOTS
THIN = BLOCKS * USED + 1
THIN_SLOTS = (THIN + 1) // 2


def box_tile(by, u):
    return u + 2 * (1 - by)


def lanes_of(tile):
    return pl.ds(128 * tile, 128)


def half_rows(upper):
    rows = lax.broadcasted_iota(jnp.int32, (8, 128), 0)
    return rows // 4 == upper


def joined_mask(mask_ref):
    parts = [mask_ref[0, by, bz] for by in range(2) for bz in range(2)]
    return jnp.concatenate(parts, axis=1)


def pack_kernel(perm_ref, stor_ref, mask_ref, prev_ref, near_ref, far_ref, far2_ref, near2_ref, mask_buf):
    odd = lax.rem(lax.axis_index("gx"), 2)
    mask_buf[...] = joined_mask(mask_ref).astype(F32)

    def rows_of(ref, tile, *rest):
        return ref[(*rest[:-1], pl.ds(pl.multiple_of(8 * tile, 8), 8), rest[-1])]

    def put_pairs(out_ref, at, slots, pieces, upper):
        keep = half_rows(upper)
        for s in range(slots):
            tile = pieces[s]()
            if s + slots < len(pieces):
                tile = jnp.where(keep, tile, pltpu.roll(pieces[s + slots](), 4, 0))
            out_ref[at + s] = tile

    def message(out_ref, leftward):
        first = 2 - 2 * leftward
        for xt in range(2):
            for blk in range(BLOCKS):
                by, bz = divmod(blk, 2)
                for u in range(USED):
                    out_ref[(xt * BLOCKS + blk) * USED + u] = rows_of(
                        prev_ref, first + xt, 0, by, bz, lanes_of(box_tile(by, u))
                    )
            out_ref[MASK_AT + xt] = rows_of(mask_buf, first + xt, lanes_of(0))
        for t in range(LANE_TILES):
            out_ref[PERM_AT + t] = rows_of(perm_ref, 1 - leftward, lanes_of(t))
            out_ref[STOR_AT + t] = rows_of(stor_ref, 1 - leftward, lanes_of(t))
        rest = 1 + leftward
        pieces = [
            functools.partial(rows_of, prev_ref, rest, 0, blk // 2, blk % 2, lanes_of(box_tile(blk // 2, u)))
            for blk in range(BLOCKS)
            for u in range(USED)
        ]
        pieces += [functools.partial(rows_of, perm_ref, leftward, lanes_of(t)) for t in range(LANE_TILES)]
        pieces += [functools.partial(rows_of, stor_ref, leftward, lanes_of(t)) for t in range(LANE_TILES)]
        pieces += [functools.partial(rows_of, mask_buf, rest, lanes_of(0))]
        put_pairs(out_ref, REST_AT, REST_SLOTS, pieces, 1 - leftward)

    def thin(out_ref, leftward):
        edge = 3 - 3 * leftward
        pieces = [
            functools.partial(rows_of, prev_ref, edge, 0, blk // 2, blk % 2, lanes_of(box_tile(blk // 2, u)))
            for blk in range(BLOCKS)
            for u in range(USED)
        ]
        pieces += [functools.partial(rows_of, mask_buf, edge, lanes_of(0))]
        put_pairs(out_ref, 0, THIN_SLOTS, pieces, 1 - leftward)

    message(far_ref, 1 - odd)
    message(near_ref, odd)
    thin(far2_ref, odd)
    thin(near2_ref, 1 - odd)


def main_kernel(
    perm_ref, stor_ref, mask_ref, prev_ref, near_ref, far_ref, far2_ref, near2_ref,
    basis_ref, coarse_ref,
    kbuf, cbuf, wbuf, gbuf, mown, mring, mtwo, sup, pbuf, qbuf, own_mask, sums,
):
    here = lax.axis_index("gx")
    last = lax.axis_size("gx") - 1
    odd = lax.rem(here, 2) == 1
    rows = lax.broadcasted_iota(jnp.int32, (8, 128), 0)
    lanes = lax.broadcasted_iota(jnp.int32, (8, 128), 1)
    heights = lax.rem(lanes, 32)
    low_rows = rows < 4
    zero = jnp.zeros((8, 128), F32)

    def left_big(i):
        return jnp.where(odd, near_ref[i], far_ref[i])

    def right_big(i):
        return jnp.where(odd, far_ref[i], near_ref[i])

    def left_thin(i):
        return jnp.where(odd, near2_ref[i], far2_ref[i])

    def right_thin(i):
        return jnp.where(odd, far2_ref[i], near2_ref[i])

    def paired(left, right, at, slots, index):
        slot = index % slots
        tile = jnp.where(low_rows, right(at + slot), left(at + slot))
        if index >= slots:
            other = jnp.where(low_rows, left(at + slot), right(at + slot))
            tile = pltpu.roll(other, 4, 0)
        return tile

    def rest_tile(index):
        return paired(left_big, right_big, REST_AT, REST_SLOTS, index)

    def thin_tile(index):
        return paired(left_thin, right_thin, 0, THIN_SLOTS, index)

    for t in range(LANE_TILES):
        for buf, ref, bulk, rest in (
            (kbuf, perm_ref, PERM_AT, BLOCKS * USED),
            (cbuf, stor_ref, STOR_AT, BLOCKS * USED + LANE_TILES),
        ):
            buf[t, 0:8] = left_big(bulk + t)
            buf[t, 8:16] = ref[0:8, 128 * t : 128 * t + 128]
            buf[t, 16:24] = ref[8:16, 128 * t : 128 * t + 128]
            buf[t, 24:32] = right_big(bulk + t)
            buf[t, 32:40] = rest_tile(rest + t)
    kbuf[LANE_TILES] = jnp.zeros((40, 128), F32)

    own_mask[...] = joined_mask(mask_ref)
    block = lanes // 32
    inner = (heights >= 8) & (heights < 24)
    core_bits = jnp.where(inner, jnp.where(lax.rem(block, 2) == 0, 0xFFFF, 0xFFFF00), 0)
    for k in range(4):
        tile = own_mask[8 * k : 8 * k + 8]
        if k in (1, 2):
            tile = tile | core_bits
        if k == 0:
            tile = jnp.where(here == 0, 0, tile)
        if k == 3:
            tile = jnp.where(here == last, 0, tile)
        mown[k] = tile
    mring[0] = left_big(MASK_AT).astype(jnp.int32) | core_bits
    mring[1] = left_big(MASK_AT + 1).astype(jnp.int32)
    mring[2] = right_big(MASK_AT).astype(jnp.int32)
    mring[3] = right_big(MASK_AT + 1).astype(jnp.int32) | core_bits
    mring[4] = rest_tile(REST - 1).astype(jnp.int32) | core_bits
    mtwo[...] = thin_tile(THIN - 1).astype(jnp.int32)

    lane_bits = []
    for bz in range(2):
        offset = heights - 8 * bz
        valid = (offset >= 0) & (offset < (18, 24)[bz])
        lane_bits.append(jnp.where(valid, jnp.left_shift(1, jnp.clip(offset, 0, 23)), 0))

    def support_of(tile, by, bz, u):
        index = 32 * (2 * by + bz) + 4 * u + 8 * (1 - by) + lanes // 32
        spread = jnp.take_along_axis(tile, index, axis=1, mode="promise_in_bounds")
        return jnp.where((spread & lane_bits[bz]) != 0, 1.0, 0.0)

    blank = jnp.zeros((40, 128), F32)
    for e in range(2):
        for by in range(2):
            for bz in range(2):
                for slot in range(LANE_TILES + 2):
                    if not 1 + 2 * by <= slot <= USED + 2 * by:
                        pbuf[e, by, bz, slot] = blank
                        qbuf[e, by, bz, slot] = blank
                for u in range(USED):
                    t = u + 2 * by
                    blk = 2 * by + bz
                    cell = blk * USED + u

                    def put(e, k, tile, bits):
                        s = support_of(bits, by, bz, u)
                        sup[e, by, bz, u, 8 * k : 8 * k + 8] = s
                        pbuf[e, by, bz, t + 1, 8 * k : 8 * k + 8] = s * tile

                    if e == 0:
                        for k in range(4):
                            at = 128 * box_tile(by, u)
                            put(0, k, prev_ref[0, by, bz, 8 * k : 8 * k + 8, at : at + 128], mown[k])
                        put(0, 4, thin_tile(cell), mtwo[...])
                    else:
                        put(1, 0, left_big(cell), mring[0])
                        put(1, 1, left_big(BLOCKS * USED + cell), mring[1])
                        put(1, 2, right_big(cell), mring[2])
                        put(1, 3, right_big(BLOCKS * USED + cell), mring[3])
                        put(1, 4, rest_tile(cell), mring[4])

    def up_x(tiles, ends):
        turned = [pltpu.roll(v, 7, 0) for v in tiles]
        return [jnp.where(rows < 7, turned[i], ends[i] if not isinstance(ends[i], int) else turned[ends[i]]) for i in range(len(tiles))]

    def down_x(tiles, ends):
        turned = [pltpu.roll(v, 1, 0) for v in tiles]
        return [jnp.where(rows > 0, turned[i], ends[i] if not isinstance(ends[i], int) else turned[ends[i]]) for i in range(len(tiles))]

    def up_y(here_, next_):
        return pltpu.roll(jnp.where(lanes >= 32, here_, next_), 96, 1)

    def down_y(here_, before):
        return pltpu.roll(jnp.where(lanes < 96, here_, before), 32, 1)

    def up_z(v):
        return pltpu.roll(v, 127, 1)

    def down_z(v):
        return pltpu.roll(v, 1, 1)

    def harmonic(a, b):
        return 2.0 * a * b / jnp.maximum(a + b, TINY)

    def faces(t, carry):
        k = [kbuf[t, 8 * i : 8 * i + 8] for i in range(5)]
        kn = [kbuf[t + 1, 8 * i : 8 * i + 8] for i in range(5)]
        east = [harmonic(a, b) for a, b in zip(k, up_x(k, [1, 2, 3, 4, 0]))]
        west = down_x(east, [4, 0, 1, 2, 3])
        for i in range(5):
            north = harmonic(k[i], up_y(k[i], kn[i]))
            upper = jnp.where(heights < 31, harmonic(k[i], up_z(k[i])), 0.0)
            lower = down_z(upper)
            south = down_y(north, carry[i])
            diag = cbuf[t, 8 * i : 8 * i + 8] + east[i] + west[i] + north + south + upper + lower
            scale = (2.0 / 3.0) / jnp.maximum(diag, TINY)
            for d, face in enumerate((east[i], west[i], north, south, upper, lower)):
                wbuf[d, t, 8 * i : 8 * i + 8] = face * scale
            gbuf[t, 8 * i : 8 * i + 8] = 1.5 * diag
            carry = carry[:i] + (north,) + carry[i + 1 :]
        return carry

    lax.fori_loop(0, LANE_TILES, faces, (zero,) * 5)

    def stencil(e, by, bz, t, tiles, ups, downs, which, weights):
        out = []
        for n, i in enumerate(which):
            v = tiles[n]
            above = pbuf[e, by, bz, t + 2, 8 * i : 8 * i + 8]
            below = pbuf[e, by, bz, t, 8 * i : 8 * i + 8]
            w = weights[i]
            total = w[0] * ups[n] + w[1] * downs[n]
            total += w[2] * up_y(v, above) + w[3] * down_y(v, below)
            total += w[4] * up_z(v) + w[5] * down_z(v)
            out.append(total)
        return out

    def load_weights(t):
        return [[wbuf[d, t, 8 * i : 8 * i + 8] for d in range(6)] for i in range(5)]

    def groups(e):
        if e == 0:
            return (((0, 1, 2, 3), [1, 2, 3, zero], [zero, 0, 1, 2]), ((4,), [zero], [zero]))
        return (((0, 1, 2, 3, 4), [1, zero, 3, 4, 0], [4, 0, zero, 2, 3]),)

    def relax(step, carry):
        by = step // USED
        u = step - by * USED
        t = u + 2 * by
        weights = load_weights(t)
        for bz in range(2):
            for e in range(2):
                for which, ups, downs in groups(e):
                    tiles = [pbuf[e, by, bz, t + 1, 8 * i : 8 * i + 8] for i in which]
                    near = stencil(e, by, bz, t, tiles, up_x(tiles, ups), down_x(tiles, downs), which, weights)
                    for n, i in enumerate(which):
                        s = sup[e, by, bz, u, 8 * i : 8 * i + 8]
                        kept = s * jnp.maximum(tiles[n] * (1.0 / 3.0) + near[n], 0.0)
                        qbuf[e, by, bz, t + 1, 8 * i : 8 * i + 8] = kept
        return carry

    def normalise(t, carry):
        for i in range(5):
            at = pl.ds(8 * i, 8)
            kept = [qbuf[e, by, bz, t + 1, at] for e in range(2) for by in range(2) for bz in range(2)]
            total = functools.reduce(lambda a, b: a + b, kept)
            scale = 1.0 / jnp.maximum(total, SUM_FLOOR)
            for n, v in enumerate(kept):
                pbuf[n // 4, (n // 2) % 2, n % 2, t + 1, at] = v * scale
        return carry

    def sweep(_, carry):
        lax.fori_loop(0, 2 * USED, relax, 0)
        lax.fori_loop(0, LANE_TILES, normalise, 0)
        return carry

    lax.fori_loop(0, ITERS, sweep, 0)

    for by in range(2):
        for bz in range(2):
            for u in range(USED):
                at = 128 * box_tile(by, u)
                basis_ref[0, by, bz, :, at : at + 128] = pbuf[0, by, bz, u + 2 * by + 1, 0:32]
            at = 0 if by == 0 else 768
            basis_ref[0, by, bz, :, at : at + 256] = jnp.zeros((32, 256), F32)

    for by in range(2):

        def couple(step, acc):
            t = step + by
            weights = load_weights(t)
            scale = [gbuf[t, 8 * i : 8 * i + 8] for i in range(5)]
            acc = list(acc)
            images = []
            for bz in range(2):
                tiles = [pbuf[0, by, bz, t + 1, 8 * i : 8 * i + 8] for i in range(4)]
                ups, downs = up_x(tiles, [1, 2, 3, zero]), down_x(tiles, [zero, 0, 1, 2])
                near = stencil(0, by, bz, t, tiles, ups, downs, (0, 1, 2, 3), weights)
                image = [scale[i] * (tiles[i] * (2.0 / 3.0) - near[i]) for i in range(4)]
                beyond = jnp.where(rows == 0, pltpu.roll(tiles[3], 1, 0), 0.0) * weights[4][1]
                before = jnp.where(rows == 7, pltpu.roll(tiles[0], 7, 0), 0.0) * weights[4][0]
                images.append((image, -scale[4] * before, -scale[4] * beyond))
            for partner in range(BLOCKS):
                by2, bz2 = divmod(partner, 2)
                own = [pbuf[0, by2, bz2, t + 1, 8 * i : 8 * i + 8] for i in range(4)]
                side = [pbuf[1, by2, bz2, t + 1, 8 * i : 8 * i + 8] for i in range(5)]
                for bz in range(2):
                    image, before, beyond = images[bz]
                    at = bz * 12 + partner
                    acc[at] += image[0] * side[0] + image[1] * side[1] + before * side[4]
                    acc[at + 4] += image[0] * own[0] + image[1] * own[1] + image[2] * own[2] + image[3] * own[3]
                    acc[at + 8] += image[2] * side[2] + image[3] * side[3] + beyond * side[4]
            return tuple(acc)

        acc = lax.fori_loop(0, USED + 1, couple, (zero,) * 24)
        for bz in range(2):
            for n in range(12):
                sums[2 * by + bz, n] = jnp.sum(acc[bz * 12 + n], axis=0)

    entry = lax.broadcasted_iota(jnp.int32, (16, 128), 0)
    column = lax.broadcasted_iota(jnp.int32, (16, 128), 1)
    for by in range(2):
        for bz in range(2):
            values = jnp.sum(sums[2 * by + bz], axis=1, keepdims=True)
            target = 9 * (entry // 4) + 3 * (lax.rem(entry // 2, 2) - by + 1) + (lax.rem(entry, 2) - bz + 1)
            placed = jnp.where((column == target) & (entry < 12), values, 0.0)
            coarse_ref[0, by, bz, :] = jnp.sum(placed, axis=0)[:27]


def shards(permeability, storage, support_mask, prev_basis):
    vmem = pl.BlockSpec(memory_space=pltpu.VMEM)
    near, far, far2, near2 = pl.pallas_call(
        pack_kernel,
        in_specs=[vmem] * 4,
        out_specs=[vmem] * 4,
        out_shape=[jax.ShapeDtypeStruct((n, 8, 128), F32) for n in (MESSAGE, MESSAGE, THIN_SLOTS, THIN_SLOTS)],
        scratch_shapes=[pltpu.VMEM((32, 128), F32)],
        name="pack",
    )(permeability, storage, support_mask, prev_basis)

    size = lax.axis_size("gx")

    def move(x, step_even, step_odd):
        pairs = [(i, i + (step_odd if i % 2 else step_even)) for i in range(size)]
        return lax.ppermute(x, "gx", [(i, j) for i, j in pairs if 0 <= j < size])

    far = move(far, -1, 1)
    far2 = move(far2, 2, -2)
    near2 = move(near2, -2, 2)
    near = move(near, 1, -1)

    ring = (2, 2, 2, LANE_TILES + 2, 40, 128)
    return pl.pallas_call(
        main_kernel,
        in_specs=[vmem] * 8,
        out_specs=[vmem] * 2,
        out_shape=[
            jax.ShapeDtypeStruct(prev_basis.shape, F32),
            jax.ShapeDtypeStruct((*prev_basis.shape[:3], 27), F32),
        ],
        scratch_shapes=[
            pltpu.VMEM((LANE_TILES + 1, 40, 128), F32),
            pltpu.VMEM((LANE_TILES, 40, 128), F32),
            pltpu.VMEM((6, LANE_TILES, 40, 128), F32),
            pltpu.VMEM((LANE_TILES, 40, 128), F32),
            pltpu.VMEM((4, 8, 128), jnp.int32),
            pltpu.VMEM((5, 8, 128), jnp.int32),
            pltpu.VMEM((8, 128), jnp.int32),
            pltpu.VMEM((2, 2, 2, USED, 40, 128), F32),
            pltpu.VMEM(ring, F32),
            pltpu.VMEM(ring, F32),
            pltpu.VMEM((32, 128), jnp.int32),
            pltpu.VMEM((4, 16, 128), F32),
        ],
        compiler_params=pltpu.CompilerParams(vmem_limit_bytes=32 * 1024 * 1024),
        name="smooth",
    )(permeability, storage, support_mask, prev_basis, near, far, far2, near2)


def solution(mesh):
    placed = (
        P(("groups", "gx"), None),
        P(("groups", "gx"), None),
        P(("groups", "gx"), None, None, None, None),
        P(("groups", "gx"), None, None, None, None),
    )
    return jax.shard_map(
        shards,
        mesh=mesh,
        in_specs=placed,
        out_specs=(
            P(("groups", "gx"), None, None, None, None),
            P(("groups", "gx"), None, None, None),
        ),
        check_vma=False,
    )
```

profile of v0, /device:TPU:8, one launch (start us, length us, event | category | flops | bytes accessed | tf_op | source)
XLA Modules:
  0.0 27.5 jit_solution(14698299700999189102)
XLA Ops:
  0.6 0.0 copy-start
  0.6 0.0 copy-start.3
  0.7 0.0 copy-start.2
  0.7 0.0 copy-start.1
  0.7 2.2 %pack.1 = (f32[87,8,128]{2,1,0:T(8,128)}, f32[87,8,128]{2,1,0:T(8,128)}, f32[13,8,128]{2,1,0:T(8,128)}, f32[13,8,128]{2,1,0:T(8,128)}) custom-call(f32[16,1024]{1,0:T(8,128)} %perm_ref.3, f32[16,1024]{1,0:T(8,128)} %stor_ref.3, s32[1,2,2,32,32]{4,3,2,1,0:T(8,128)} %mask_ref.3, f32[1,2,2,32,1024]{4,3,2,1,0:T(8,128)} %prev_ref.3), custom_call_target="tpu_custom_call" | custom-call | tf_op jit(solution)/shard_map/pack/pallas_call | solution.py:367
  2.8 0.0 collective-permute-start
  2.8 3.4 %collective-permute-start.1 = (f32[87,8,128]{2,1,0:T(8,128)}, f32[87,8,128]{2,1,0:T(8,128)S(1)}, u32[]{:S(2)}, u32[]{:S(2)}) collective-permute-start(f32[87,8,128]{2,1,0:T(8,128)} %get-tuple-element.7), channel_id=1, source_target_pairs={{1,2},{2,1},{3,4},{4,3},{5,6},{6,5},{7,8},{8,7},{9,10},{10,9},{11,... | collective-permute-start | bytes 1069064 | tf_op jit(solution)/shard_map/ppermute | solution.py:380
  6.3 2.5 %collective-permute-start.2 = (f32[13,8,128]{2,1,0:T(8,128)}, f32[13,8,128]{2,1,0:T(8,128)S(1)}, u32[]{:S(2)}, u32[]{:S(2)}) collective-permute-start(f32[13,8,128]{2,1,0:T(8,128)} %get-tuple-element.8), channel_id=1, source_target_pairs={{0,2},{2,4},{3,1},{4,6},{5,3},{6,8},{7,5},{8,10},{9,7},{10,12},{11... | collective-permute-start | bytes 159752 | tf_op jit(solution)/shard_map/ppermute | solution.py:380
  8.8 4.2 %collective-permute-start.3 = (f32[13,8,128]{2,1,0:T(8,128)}, f32[13,8,128]{2,1,0:T(8,128)S(1)}, u32[]{:S(2)}, u32[]{:S(2)}) collective-permute-start(f32[13,8,128]{2,1,0:T(8,128)} %get-tuple-element.9), channel_id=1, source_target_pairs={{1,3},{2,0},{3,5},{4,2},{5,7},{6,4},{7,9},{8,6},{9,11},{10,8},{11,... | collective-permute-start | bytes 159752 | tf_op jit(solution)/shard_map/ppermute | solution.py:380
  13.0 1.3 %collective-permute-done.2.far2_ref = f32[13,8,128]{2,1,0:T(8,128)S(1)} collective-permute-done((f32[13,8,128]{2,1,0:T(8,128)}, f32[13,8,128]{2,1,0:T(8,128)S(1)}, u32[]{:S(2)}, u32[]{:S(2)}) %collective-permute-start.2) | collective-permute-done | bytes 53280 | tf_op jit(solution)/shard_map/ppermute | solution.py:380
  14.3 4.2 %collective-permute-done.3.near2_ref = f32[13,8,128]{2,1,0:T(8,128)S(1)} collective-permute-done((f32[13,8,128]{2,1,0:T(8,128)}, f32[13,8,128]{2,1,0:T(8,128)S(1)}, u32[]{:S(2)}, u32[]{:S(2)}) %collective-permute-start.3) | collective-permute-done | bytes 53280 | tf_op jit(solution)/shard_map/ppermute | solution.py:380
  18.5 0.0 collective-permute-done.near_ref
  18.5 0.0 collective-permute-done.1.far_ref
  18.5 0.0 copy-done
  18.5 0.0 copy-done.3
  18.5 0.0 copy-done.2
  18.6 0.0 copy-done.1
  18.6 8.9 %smooth.1 = (f32[1,2,2,32,1024]{4,3,2,1,0:T(8,128)}, f32[1,2,2,27]{3,2,1,0:T(2,128)}) custom-call(f32[16,1024]{1,0:T(8,128)S(1)} %copy-done.1, f32[16,1024]{1,0:T(8,128)S(1)} %copy-done.2, s32[1,2,2,32,32]{4,3,2,1,0:T(8,128)S(1)} %copy-done.3, f32[1,2,2,32,1024]{4,3,2,1,0:T(8,128)S(1)} %copy-done, f32[87,8,128]{2,1,0:T(8,128)S(1)} %collective-permute-done.near_ref, ...), custom_call_target="tpu_custom_call" | custom-call | tf_op jit(solution)/shard_map/smooth/pallas_call | solution.py:388
Async XLA Ops:
  0.6 17.9 %copy-start = (f32[1,2,2,32,1024]{4,3,2,1,0:T(8,128)S(1)}, f32[1,2,2,32,1024]{4,3,2,1,0:T(8,128)}, u32[]{:S(2)}) copy-start(f32[1,2,2,32,1024]{4,3,2,1,0:T(8,128)} %prev_ref.3) | copy-start | bytes 1572868
  0.6 17.9 %copy-start.3 = (s32[1,2,2,32,32]{4,3,2,1,0:T(8,128)S(1)}, s32[1,2,2,32,32]{4,3,2,1,0:T(8,128)}, u32[]{:S(2)}) copy-start(s32[1,2,2,32,32]{4,3,2,1,0:T(8,128)} %mask_ref.3) | copy-start | bytes 49156
  0.7 17.9 %copy-start.2 = (f32[16,1024]{1,0:T(8,128)S(1)}, f32[16,1024]{1,0:T(8,128)}, u32[]{:S(2)}) copy-start(f32[16,1024]{1,0:T(8,128)} %stor_ref.3) | copy-start | bytes 196612
  0.7 17.9 %copy-start.1 = (f32[16,1024]{1,0:T(8,128)S(1)}, f32[16,1024]{1,0:T(8,128)}, u32[]{:S(2)}) copy-start(f32[16,1024]{1,0:T(8,128)} %perm_ref.3) | copy-start | bytes 196612
  2.8 15.7 %collective-permute-start = (f32[87,8,128]{2,1,0:T(8,128)}, f32[87,8,128]{2,1,0:T(8,128)S(1)}, u32[]{:S(2)}, u32[]{:S(2)}) collective-permute-start(f32[87,8,128]{2,1,0:T(8,128)} %get-tuple-element.6), channel_id=1, source_target_pairs={{0,1},{1,0},{2,3},{3,2},{4,5},{5,4},{6,7},{7,6},{8,9},{9,8},{10,11... | collective-permute-start | bytes 1069064 | tf_op jit(solution)/shard_map/ppermute | solution.py:380
  2.8 15.7 %collective-permute-start.1 = (f32[87,8,128]{2,1,0:T(8,128)}, f32[87,8,128]{2,1,0:T(8,128)S(1)}, u32[]{:S(2)}, u32[]{:S(2)}) collective-permute-start(f32[87,8,128]{2,1,0:T(8,128)} %get-tuple-element.7), channel_id=1, source_target_pairs={{1,2},{2,1},{3,4},{4,3},{5,6},{6,5},{7,8},{8,7},{9,10},{10,9},{11,... | collective-permute-start | bytes 1069064 | tf_op jit(solution)/shard_map/ppermute | solution.py:380
  6.3 8.1 %collective-permute-start.2 = (f32[13,8,128]{2,1,0:T(8,128)}, f32[13,8,128]{2,1,0:T(8,128)S(1)}, u32[]{:S(2)}, u32[]{:S(2)}) collective-permute-start(f32[13,8,128]{2,1,0:T(8,128)} %get-tuple-element.8), channel_id=1, source_target_pairs={{0,2},{2,4},{3,1},{4,6},{5,3},{6,8},{7,5},{8,10},{9,7},{10,12},{11... | collective-permute-start | bytes 159752 | tf_op jit(solution)/shard_map/ppermute | solution.py:380
  8.8 9.7 %collective-permute-start.3 = (f32[13,8,128]{2,1,0:T(8,128)}, f32[13,8,128]{2,1,0:T(8,128)S(1)}, u32[]{:S(2)}, u32[]{:S(2)}) collective-permute-start(f32[13,8,128]{2,1,0:T(8,128)} %get-tuple-element.9), channel_id=1, source_target_pairs={{1,3},{2,0},{3,5},{4,2},{5,7},{6,4},{7,9},{8,6},{9,11},{10,8},{11,... | collective-permute-start | bytes 159752 | tf_op jit(solution)/shard_map/ppermute | solution.py:380
where the time goes:
time: 27.7 us; the launch traced here: 27.5 us
  Pallas kernels  11.1 us (40%)
  starting transfers between devices  10.2 us (37%)
  waiting for transfers between devices  5.51 us (20%)
  between operations  0.72 us (3%)
    ppermute x4, starting transfers between devices, move(): return lax.ppermute(x, 'gx', [(i, j) for i, j in pairs if 0 <= j < size])  10.2 us
    pallas_call x1, Pallas kernels, shards(): pl.pallas_call(main_kernel, in_specs=[vmem] * 8, out_specs=[vmem] * 2, ou...  8.9 us
    ppermute x4, waiting for transfers between devices, move(): return lax.ppermute(x, 'gx', [(i, j) for i, j in pairs if 0 <= j < size])  5.51 us
    pallas_call x1, Pallas kernels, shards(): pl.pallas_call(pack_kernel, in_specs=[vmem] * 4, out_specs=[vmem] * 4, ou...  2.16 us
  transfers between devices with their start and end apart: 4, of which 2 were waited for; matrix products, arithmetic and copies ran while one was open for 0% of the time, Pallas kernels for 0%

commit v1 on v0

v1 whole, which is shorter than its diff:
```python
import functools

import jax
import jax.numpy as jnp
from jax import lax
from jax.experimental import pallas as pl
from jax.experimental.pallas import tpu as pltpu
from jax.sharding import PartitionSpec as P

ITERS = 2
SUM_FLOOR = 0.5
TINY = 1e-30
F32 = jnp.float32


BLOCKS = 4
LANE_TILES = 8
USED = 6

PERM_AT = 2 * BLOCKS * USED
STOR_AT = PERM_AT + LANE_TILES
MASK_AT = STOR_AT + LANE_TILES
REST_AT = MASK_AT + 2
REST = BLOCKS * USED + 2 * LANE_TILES + 1
REST_SLOTS = (REST + 1) // 2
MESSAGE = REST_AT + REST_SLOTS
THIN = BLOCKS * USED + 1
THIN_SLOTS = (THIN + 1) // 2


OWN, TWO, SIDE, STRIP = 8, 48, 64, 112
PADS = (0, 40, 56, 104)
TILES = tuple((OWN + 8 * k, k) for k in range(4)) + ((TWO, 4),) + tuple((SIDE + 8 * n, (n + 2) % 5) for n in range(5))


def box_tile(by, u):
    return u + 2 * (1 - by)


def lanes_of(tile):
    return pl.ds(128 * tile, 128)


def half_rows(upper):
    rows = lax.broadcasted_iota(jnp.int32, (8, 128), 0)
    return rows // 4 == upper


def joined_mask(mask_ref):
    parts = [mask_ref[0, by, bz] for by in range(2) for bz in range(2)]
    return jnp.concatenate(parts, axis=1)


def pack_kernel(perm_ref, stor_ref, mask_ref, prev_ref, near_ref, far_ref, far2_ref, near2_ref, mask_buf):
    odd = lax.rem(lax.axis_index("gx"), 2)
    mask_buf[...] = joined_mask(mask_ref).astype(F32)

    def rows_of(ref, tile, *rest):
        return ref[(*rest[:-1], pl.ds(pl.multiple_of(8 * tile, 8), 8), rest[-1])]

    def put_pairs(out_ref, at, slots, pieces, upper):
        keep = half_rows(upper)
        for s in range(slots):
            tile = pieces[s]()
            if s + slots < len(pieces):
                tile = jnp.where(keep, tile, pltpu.roll(pieces[s + slots](), 4, 0))
            out_ref[at + s] = tile

    def message(out_ref, leftward):
        first = 2 - 2 * leftward
        for xt in range(2):
            for blk in range(BLOCKS):
                by, bz = divmod(blk, 2)
                for u in range(USED):
                    out_ref[(xt * BLOCKS + blk) * USED + u] = rows_of(
                        prev_ref, first + xt, 0, by, bz, lanes_of(box_tile(by, u))
                    )
            out_ref[MASK_AT + xt] = rows_of(mask_buf, first + xt, lanes_of(0))
        for t in range(LANE_TILES):
            out_ref[PERM_AT + t] = rows_of(perm_ref, 1 - leftward, lanes_of(t))
            out_ref[STOR_AT + t] = rows_of(stor_ref, 1 - leftward, lanes_of(t))
        rest = 1 + leftward
        pieces = [
            functools.partial(rows_of, prev_ref, rest, 0, blk // 2, blk % 2, lanes_of(box_tile(blk // 2, u)))
            for blk in range(BLOCKS)
            for u in range(USED)
        ]
        pieces += [functools.partial(rows_of, perm_ref, leftward, lanes_of(t)) for t in range(LANE_TILES)]
        pieces += [functools.partial(rows_of, stor_ref, leftward, lanes_of(t)) for t in range(LANE_TILES)]
        pieces += [functools.partial(rows_of, mask_buf, rest, lanes_of(0))]
        put_pairs(out_ref, REST_AT, REST_SLOTS, pieces, 1 - leftward)

    def thin(out_ref, leftward):
        edge = 3 - 3 * leftward
        pieces = [
            functools.partial(rows_of, prev_ref, edge, 0, blk // 2, blk % 2, lanes_of(box_tile(blk // 2, u)))
            for blk in range(BLOCKS)
            for u in range(USED)
        ]
        pieces += [functools.partial(rows_of, mask_buf, edge, lanes_of(0))]
        put_pairs(out_ref, 0, THIN_SLOTS, pieces, 1 - leftward)

    message(far_ref, 1 - odd)
    message(near_ref, odd)
    thin(far2_ref, odd)
    thin(near2_ref, 1 - odd)


def main_kernel(
    perm_ref, stor_ref, mask_ref, prev_ref, near_ref, far_ref, far2_ref, near2_ref,
    basis_ref, coarse_ref,
    kbuf, cbuf, wbuf, gbuf, sup, pbuf, qbuf, own_mask, sums,
):
    here = lax.axis_index("gx")
    last = lax.axis_size("gx") - 1
    odd = lax.rem(here, 2) == 1
    rows = lax.broadcasted_iota(jnp.int32, (8, 128), 0)
    lanes = lax.broadcasted_iota(jnp.int32, (8, 128), 1)
    heights = lax.rem(lanes, 32)
    low_rows = rows < 4
    zero = jnp.zeros((8, 128), F32)

    def left_big(i):
        return jnp.where(odd, near_ref[i], far_ref[i])

    def right_big(i):
        return jnp.where(odd, far_ref[i], near_ref[i])

    def left_thin(i):
        return jnp.where(odd, near2_ref[i], far2_ref[i])

    def right_thin(i):
        return jnp.where(odd, far2_ref[i], near2_ref[i])

    def paired(left, right, at, slots, index):
        slot = index % slots
        tile = jnp.where(low_rows, right(at + slot), left(at + slot))
        if index >= slots:
            other = jnp.where(low_rows, left(at + slot), right(at + slot))
            tile = pltpu.roll(other, 4, 0)
        return tile

    def rest_tile(index):
        return paired(left_big, right_big, REST_AT, REST_SLOTS, index)

    def thin_tile(index):
        return paired(left_thin, right_thin, 0, THIN_SLOTS, index)

    for t in range(LANE_TILES):
        for buf, ref, bulk, rest in (
            (kbuf, perm_ref, PERM_AT, BLOCKS * USED),
            (cbuf, stor_ref, STOR_AT, BLOCKS * USED + LANE_TILES),
        ):
            buf[t, 0:8] = left_big(bulk + t)
            buf[t, 8:16] = ref[0:8, 128 * t : 128 * t + 128]
            buf[t, 16:24] = ref[8:16, 128 * t : 128 * t + 128]
            buf[t, 24:32] = right_big(bulk + t)
            buf[t, 32:40] = rest_tile(rest + t)

    own_mask[...] = joined_mask(mask_ref)
    block = lanes // 32
    inner = (heights >= 8) & (heights < 24)
    core_bits = jnp.where(inner, jnp.where(lax.rem(block, 2) == 0, 0xFFFF, 0xFFFF00), 0)
    own_bits = [own_mask[8 * k : 8 * k + 8] for k in range(4)]
    own_bits[0] = jnp.where(here == 0, 0, own_bits[0])
    own_bits[1] |= core_bits
    own_bits[2] |= core_bits
    own_bits[3] = jnp.where(here == last, 0, own_bits[3])
    two_bits = thin_tile(THIN - 1).astype(jnp.int32)
    side_bits = [
        right_big(MASK_AT).astype(jnp.int32),
        right_big(MASK_AT + 1).astype(jnp.int32) | core_bits,
        rest_tile(REST - 1).astype(jnp.int32) | core_bits,
        left_big(MASK_AT).astype(jnp.int32) | core_bits,
        left_big(MASK_AT + 1).astype(jnp.int32),
    ]

    lane_bits = []
    for bz in range(2):
        offset = heights - 8 * bz
        valid = (offset >= 0) & (offset < (18, 24)[bz])
        lane_bits.append(jnp.where(valid, jnp.left_shift(1, jnp.clip(offset, 0, 23)), 0))

    def support_of(tile, by, bz, u):
        index = 32 * (2 * by + bz) + 4 * u + 8 * (1 - by) + lanes // 32
        spread = jnp.take_along_axis(tile, index, axis=1, mode="promise_in_bounds")
        return jnp.where((spread & lane_bits[bz]) != 0, 1.0, 0.0)

    for by in range(2):
        for bz in range(2):
            for u in range(USED):
                cell = (2 * by + bz) * USED + u
                for row in PADS:
                    pbuf[by, bz, u, row : row + 8] = zero

                def put(row, tile, bits):
                    s = support_of(bits, by, bz, u)
                    sup[by, bz, u, row : row + 8] = s
                    pbuf[by, bz, u, row : row + 8] = s * tile

                for k in range(4):
                    at = 128 * box_tile(by, u)
                    put(OWN + 8 * k, prev_ref[0, by, bz, 8 * k : 8 * k + 8, at : at + 128], own_bits[k])
                put(TWO, thin_tile(cell), two_bits)
                put(SIDE, right_big(cell), side_bits[0])
                put(SIDE + 8, right_big(BLOCKS * USED + cell), side_bits[1])
                put(SIDE + 16, rest_tile(cell), side_bits[2])
                put(SIDE + 24, left_big(cell), side_bits[3])
                put(SIDE + 32, left_big(BLOCKS * USED + cell), side_bits[4])

    def up_y(here_, next_):
        return pltpu.roll(jnp.where(lanes >= 32, here_, next_), 96, 1)

    def down_y(here_, before):
        return pltpu.roll(jnp.where(lanes < 96, here_, before), 32, 1)

    def up_z(v):
        return pltpu.roll(v, 127, 1)

    def down_z(v):
        return pltpu.roll(v, 1, 1)

    def inverse(v):
        first = pl.reciprocal(v, approx=True)
        return first * (2.0 - v * first)

    def harmonic(a, b):
        return 2.0 * (a * b) * inverse(jnp.maximum(a + b, TINY))

    south = [zero] * 5
    for t in range(LANE_TILES):
        k = [kbuf[t, 8 * i : 8 * i + 8] for i in range(5)]
        turned = [pltpu.roll(v, 7, 0) for v in k]
        east = [harmonic(k[i], jnp.where(rows < 7, turned[i], turned[(i + 1) % 5])) for i in range(5)]
        turned = [pltpu.roll(v, 1, 0) for v in east]
        west = [jnp.where(rows > 0, turned[i], turned[i - 1]) for i in range(5)]
        for i in range(5):
            above = kbuf[t + 1, 8 * i : 8 * i + 8] if t + 1 < LANE_TILES else zero
            north = harmonic(k[i], up_y(k[i], above))
            upper = jnp.where(heights < 31, harmonic(k[i], up_z(k[i])), 0.0)
            lower = down_z(upper)
            below = down_y(north, south[i])
            south[i] = north
            diag = cbuf[t, 8 * i : 8 * i + 8] + east[i] + west[i] + north + below + upper + lower
            scale = (2.0 / 3.0) * inverse(jnp.maximum(diag, TINY))
            for d, face in enumerate((east[i], west[i], north, below, upper, lower)):
                wbuf[t, d, 8 * i : 8 * i + 8] = face * scale
            gbuf[t, 8 * i : 8 * i + 8] = 1.5 * diag

    def weights_of(t):
        return [[wbuf[t, d, 8 * i : 8 * i + 8] for d in range(6)] for i in range(5)]

    def tile_of(by, bz, u, row):
        if 0 <= u < USED:
            return pbuf[by, bz, u, row : row + 8]
        return zero

    def stencil(by, bz, u, row, v, w):
        near = w[0] * pbuf[by, bz, u, row + 1 : row + 9] + w[1] * pbuf[by, bz, u, row - 1 : row + 7]
        near += w[2] * up_y(v, tile_of(by, bz, u + 1, row)) + w[3] * down_y(v, tile_of(by, bz, u - 1, row))
        return near + (w[4] * up_z(v) + w[5] * down_z(v))

    def relax(by, carry):
        for u in range(USED):
            weights = weights_of(u + 2 * by)
            for bz in range(2):
                for row, i in TILES:
                    v = tile_of(by, bz, u, row)
                    near = stencil(by, bz, u, row, v, weights[i])
                    s = sup[by, bz, u, row : row + 8]
                    qbuf[by, bz, u, row : row + 8] = s * jnp.maximum(v * (1.0 / 3.0) + near, 0.0)
        return carry

    def normalise(final):
        for t in range(LANE_TILES):
            blocks = [(by, bz, t - 2 * by) for by in range(2) for bz in range(2) if 0 <= t - 2 * by < USED]
            for i in range(5):
                at = [(b, row) for b in blocks for row, ring in TILES if ring == i]
                kept = [qbuf[by, bz, u, row : row + 8] for (by, bz, u), row in at]
                total = functools.reduce(lambda a, b: a + b, kept)
                scale = inverse(jnp.maximum(total, SUM_FLOOR))
                for ((by, bz, u), row), v in zip(at, kept):
                    v = v * scale
                    pbuf[by, bz, u, row : row + 8] = v
                    if final and row < TWO:
                        lane = 128 * box_tile(by, u)
                        basis_ref[0, by, bz, row - OWN : row - OWN + 8, lane : lane + 128] = v

    for sweep in range(ITERS):
        lax.fori_loop(0, 2, relax, 0)
        normalise(sweep == ITERS - 1)

    for by in range(2):
        for bz in range(2):
            at = 0 if by == 0 else 768
            basis_ref[0, by, bz, :, at : at + 256] = jnp.zeros((32, 256), F32)

    for by in range(2):
        acc = [[] for _ in range(24)]
        for t in range(by, by + USED + 1):
            u = t - 2 * by
            weights = weights_of(t)
            scale = [gbuf[t, 8 * i : 8 * i + 8] for i in range(5)]
            images = []
            for bz in range(2):
                image = []
                for k in range(4):
                    row = OWN + 8 * k
                    if 0 <= u < USED:
                        v = tile_of(by, bz, u, row)
                        image.append(scale[k] * (v * (2.0 / 3.0) - stencil(by, bz, u, row, v, weights[k])))
                    elif u < 0:
                        image.append(-scale[k] * (weights[k][2] * up_y(zero, tile_of(by, bz, u + 1, row))))
                    else:
                        image.append(-scale[k] * (weights[k][3] * down_y(zero, tile_of(by, bz, u - 1, row))))
                before = beyond = None
                if 0 <= u < USED:
                    edge = pbuf[by, bz, u, OWN + 31 : OWN + 39]
                    beyond = -scale[4] * (weights[4][1] * edge)
                    edge = pbuf[by, bz, u, OWN - 7 : OWN + 1]
                    before = -scale[4] * (weights[4][0] * edge)
                images.append((image, before, beyond))
            for partner in range(BLOCKS):
                by2, bz2 = divmod(partner, 2)
                u2 = t - 2 * by2
                if not 0 <= u2 < USED:
                    continue
                own = [tile_of(by2, bz2, u2, OWN + 8 * k) for k in range(4)]
                side = [tile_of(by2, bz2, u2, SIDE + 8 * k) for k in range(5)]
                for bz in range(2):
                    image, before, beyond = images[bz]
                    at = bz * 12 + partner
                    acc[at] += [image[0] * side[3], image[1] * side[4]]
                    acc[at + 4] += [image[k] * own[k] for k in range(4)]
                    acc[at + 8] += [image[2] * side[0], image[3] * side[1]]
                    if before is not None:
                        acc[at] += [before * side[2]]
                        acc[at + 8] += [beyond * side[2]]
            acc = [[functools.reduce(lambda a, b: a + b, terms)] if terms else [] for terms in acc]
        for bz in range(2):
            for n in range(12):
                sums[2 * by + bz, n] = jnp.sum(acc[bz * 12 + n][0], axis=0)

    entry = lax.broadcasted_iota(jnp.int32, (16, 128), 0)
    column = lax.broadcasted_iota(jnp.int32, (16, 128), 1)
    for by in range(2):
        for bz in range(2):
            values = jnp.sum(sums[2 * by + bz], axis=1, keepdims=True)
            target = 9 * (entry // 4) + 3 * (lax.rem(entry // 2, 2) - by + 1) + (lax.rem(entry, 2) - bz + 1)
            placed = jnp.where((column == target) & (entry < 12), values, 0.0)
            coarse_ref[0, by, bz, :] = jnp.sum(placed, axis=0)[:27]


def shards(permeability, storage, support_mask, prev_basis):
    vmem = pl.BlockSpec(memory_space=pltpu.VMEM)
    near, far, far2, near2 = pl.pallas_call(
        pack_kernel,
        in_specs=[vmem] * 4,
        out_specs=[vmem] * 4,
        out_shape=[jax.ShapeDtypeStruct((n, 8, 128), F32) for n in (MESSAGE, MESSAGE, THIN_SLOTS, THIN_SLOTS)],
        scratch_shapes=[pltpu.VMEM((32, 128), F32)],
        name="pack",
    )(permeability, storage, support_mask, prev_basis)

    size = lax.axis_size("gx")

    def move(x, step_even, step_odd):
        pairs = [(i, i + (step_odd if i % 2 else step_even)) for i in range(size)]
        return lax.ppermute(x, "gx", [(i, j) for i, j in pairs if 0 <= j < size])

    far = move(far, -1, 1)
    far2 = move(far2, 2, -2)
    near2 = move(near2, -2, 2)
    near = move(near, 1, -1)

    strips = (2, 2, USED, STRIP, 128)
    return pl.pallas_call(
        main_kernel,
        in_specs=[vmem] * 8,
        out_specs=[vmem] * 2,
        out_shape=[
            jax.ShapeDtypeStruct(prev_basis.shape, F32),
            jax.ShapeDtypeStruct((*prev_basis.shape[:3], 27), F32),
        ],
        scratch_shapes=[
            pltpu.VMEM((LANE_TILES, 40, 128), F32),
            pltpu.VMEM((LANE_TILES, 40, 128), F32),
            pltpu.VMEM((LANE_TILES, 6, 40, 128), F32),
            pltpu.VMEM((LANE_TILES, 40, 128), F32),
            pltpu.VMEM(strips, F32),
            pltpu.VMEM(strips, F32),
            pltpu.VMEM(strips, F32),
            pltpu.VMEM((32, 128), jnp.int32),
            pltpu.VMEM((4, 16, 128), F32),
        ],
        compiler_params=pltpu.CompilerParams(vmem_limit_bytes=32 * 1024 * 1024),
        name="smooth",
    )(permeability, storage, support_mask, prev_basis, near, far, far2, near2)


def solution(mesh):
    placed = (
        P(("groups", "gx"), None),
        P(("groups", "gx"), None),
        P(("groups", "gx"), None, None, None, None),
        P(("groups", "gx"), None, None, None, None),
    )
    return jax.shard_map(
        shards,
        mesh=mesh,
        in_specs=placed,
        out_specs=(
            P(("groups", "gx"), None, None, None, None),
            P(("groups", "gx"), None, None, None),
        ),
        check_vma=False,
    )
```

time: 27.7 us -> 24.6 us (0.89)
  Pallas kernels: 11.1 us -> 7.98 us
    pallas_call x1, Pallas kernels: 8.9 us -> 5.82 us  [shards(): pl.pallas_call(main_kernel, in_specs=[vmem] * 8, out_specs=[vmem] * 2, ou...]
where the time goes in v1:
time: 24.6 us; the launch traced here: 24.4 us
  starting transfers between devices  10.2 us (41%)
  Pallas kernels  7.98 us (32%)
  waiting for transfers between devices  5.51 us (22%)
  between operations  0.72 us (3%)
    ppermute x4, starting transfers between devices, move(): return lax.ppermute(x, 'gx', [(i, j) for i, j in pairs if 0 <= j < size])  10.2 us
    pallas_call x1, Pallas kernels, shards(): pl.pallas_call(main_kernel, in_specs=[vmem] * 8, out_specs=[vmem] * 2, ou...  5.82 us
    ppermute x4, waiting for transfers between devices, move(): return lax.ppermute(x, 'gx', [(i, j) for i, j in pairs if 0 <= j < size])  5.51 us
    pallas_call x1, Pallas kernels, shards(): pl.pallas_call(pack_kernel, in_specs=[vmem] * 4, out_specs=[vmem] * 4, ou...  2.16 us
  transfers between devices with their start and end apart: 4, of which 2 were waited for; matrix products, arithmetic and copies ran while one was open for 0% of the time, Pallas kernels for 0%

profile of v1, /device:TPU:8, one launch (start us, length us, event | category | flops | bytes accessed | tf_op | source)
XLA Modules:
  0.0 24.4 jit_solution(17600504539191559576)
XLA Ops:
  0.6 0.0 copy-start
  0.6 0.0 copy-start.3
  0.7 0.0 copy-start.2
  0.7 0.0 copy-start.1
  0.7 2.2 %pack.1 = (f32[87,8,128]{2,1,0:T(8,128)}, f32[87,8,128]{2,1,0:T(8,128)}, f32[13,8,128]{2,1,0:T(8,128)}, f32[13,8,128]{2,1,0:T(8,128)}) custom-call(f32[16,1024]{1,0:T(8,128)} %perm_ref.3, f32[16,1024]{1,0:T(8,128)} %stor_ref.3, s32[1,2,2,32,32]{4,3,2,1,0:T(8,128)} %mask_ref.3, f32[1,2,2,32,1024]{4,3,2,1,0:T(8,128)} %prev_ref.3), custom_call_target="tpu_custom_call" | custom-call | tf_op jit(solution)/shard_map/pack/pallas_call | solution.py:356
  2.8 0.0 collective-permute-start
  2.8 3.4 %collective-permute-start.1 = (f32[87,8,128]{2,1,0:T(8,128)}, f32[87,8,128]{2,1,0:T(8,128)S(1)}, u32[]{:S(2)}, u32[]{:S(2)}) collective-permute-start(f32[87,8,128]{2,1,0:T(8,128)} %get-tuple-element.7), channel_id=1, source_target_pairs={{1,2},{2,1},{3,4},{4,3},{5,6},{6,5},{7,8},{8,7},{9,10},{10,9},{11,... | collective-permute-start | bytes 1069064 | tf_op jit(solution)/shard_map/ppermute | solution.py:369
  6.3 2.5 %collective-permute-start.2 = (f32[13,8,128]{2,1,0:T(8,128)}, f32[13,8,128]{2,1,0:T(8,128)S(1)}, u32[]{:S(2)}, u32[]{:S(2)}) collective-permute-start(f32[13,8,128]{2,1,0:T(8,128)} %get-tuple-element.8), channel_id=1, source_target_pairs={{0,2},{2,4},{3,1},{4,6},{5,3},{6,8},{7,5},{8,10},{9,7},{10,12},{11... | collective-permute-start | bytes 159752 | tf_op jit(solution)/shard_map/ppermute | solution.py:369
  8.8 4.2 %collective-permute-start.3 = (f32[13,8,128]{2,1,0:T(8,128)}, f32[13,8,128]{2,1,0:T(8,128)S(1)}, u32[]{:S(2)}, u32[]{:S(2)}) collective-permute-start(f32[13,8,128]{2,1,0:T(8,128)} %get-tuple-element.9), channel_id=1, source_target_pairs={{1,3},{2,0},{3,5},{4,2},{5,7},{6,4},{7,9},{8,6},{9,11},{10,8},{11,... | collective-permute-start | bytes 159752 | tf_op jit(solution)/shard_map/ppermute | solution.py:369
  13.0 1.3 %collective-permute-done.2.far2_ref = f32[13,8,128]{2,1,0:T(8,128)S(1)} collective-permute-done((f32[13,8,128]{2,1,0:T(8,128)}, f32[13,8,128]{2,1,0:T(8,128)S(1)}, u32[]{:S(2)}, u32[]{:S(2)}) %collective-permute-start.2) | collective-permute-done | bytes 53280 | tf_op jit(solution)/shard_map/ppermute | solution.py:369
  14.3 4.2 %collective-permute-done.3.near2_ref = f32[13,8,128]{2,1,0:T(8,128)S(1)} collective-permute-done((f32[13,8,128]{2,1,0:T(8,128)}, f32[13,8,128]{2,1,0:T(8,128)S(1)}, u32[]{:S(2)}, u32[]{:S(2)}) %collective-permute-start.3) | collective-permute-done | bytes 53280 | tf_op jit(solution)/shard_map/ppermute | solution.py:369
  18.5 0.0 collective-permute-done.near_ref
  18.5 0.0 collective-permute-done.1.far_ref
  18.5 0.0 copy-done
  18.5 0.0 copy-done.3
  18.5 0.0 copy-done.2
  18.6 0.0 copy-done.1
  18.6 5.8 %smooth.1 = (f32[1,2,2,32,1024]{4,3,2,1,0:T(8,128)}, f32[1,2,2,27]{3,2,1,0:T(2,128)}) custom-call(f32[16,1024]{1,0:T(8,128)S(1)} %copy-done.1, f32[16,1024]{1,0:T(8,128)S(1)} %copy-done.2, s32[1,2,2,32,32]{4,3,2,1,0:T(8,128)S(1)} %copy-done.3, f32[1,2,2,32,1024]{4,3,2,1,0:T(8,128)S(1)} %copy-done, f32[87,8,128]{2,1,0:T(8,128)S(1)} %collective-permute-done.near_ref, ...), custom_call_target="tpu_custom_call" | custom-call | tf_op jit(solution)/shard_map/smooth/pallas_call | solution.py:377
Async XLA Ops:
  0.6 17.9 %copy-start = (f32[1,2,2,32,1024]{4,3,2,1,0:T(8,128)S(1)}, f32[1,2,2,32,1024]{4,3,2,1,0:T(8,128)}, u32[]{:S(2)}) copy-start(f32[1,2,2,32,1024]{4,3,2,1,0:T(8,128)} %prev_ref.3) | copy-start | bytes 1572868
  0.6 17.9 %copy-start.3 = (s32[1,2,2,32,32]{4,3,2,1,0:T(8,128)S(1)}, s32[1,2,2,32,32]{4,3,2,1,0:T(8,128)}, u32[]{:S(2)}) copy-start(s32[1,2,2,32,32]{4,3,2,1,0:T(8,128)} %mask_ref.3) | copy-start | bytes 49156
  0.7 17.9 %copy-start.2 = (f32[16,1024]{1,0:T(8,128)S(1)}, f32[16,1024]{1,0:T(8,128)}, u32[]{:S(2)}) copy-start(f32[16,1024]{1,0:T(8,128)} %stor_ref.3) | copy-start | bytes 196612
  0.7 17.9 %copy-start.1 = (f32[16,1024]{1,0:T(8,128)S(1)}, f32[16,1024]{1,0:T(8,128)}, u32[]{:S(2)}) copy-start(f32[16,1024]{1,0:T(8,128)} %perm_ref.3) | copy-start | bytes 196612
  2.8 15.7 %collective-permute-start = (f32[87,8,128]{2,1,0:T(8,128)}, f32[87,8,128]{2,1,0:T(8,128)S(1)}, u32[]{:S(2)}, u32[]{:S(2)}) collective-permute-start(f32[87,8,128]{2,1,0:T(8,128)} %get-tuple-element.6), channel_id=1, source_target_pairs={{0,1},{1,0},{2,3},{3,2},{4,5},{5,4},{6,7},{7,6},{8,9},{9,8},{10,11... | collective-permute-start | bytes 1069064 | tf_op jit(solution)/shard_map/ppermute | solution.py:369
  2.8 15.7 %collective-permute-start.1 = (f32[87,8,128]{2,1,0:T(8,128)}, f32[87,8,128]{2,1,0:T(8,128)S(1)}, u32[]{:S(2)}, u32[]{:S(2)}) collective-permute-start(f32[87,8,128]{2,1,0:T(8,128)} %get-tuple-element.7), channel_id=1, source_target_pairs={{1,2},{2,1},{3,4},{4,3},{5,6},{6,5},{7,8},{8,7},{9,10},{10,9},{11,... | collective-permute-start | bytes 1069064 | tf_op jit(solution)/shard_map/ppermute | solution.py:369
  6.3 8.1 %collective-permute-start.2 = (f32[13,8,128]{2,1,0:T(8,128)}, f32[13,8,128]{2,1,0:T(8,128)S(1)}, u32[]{:S(2)}, u32[]{:S(2)}) collective-permute-start(f32[13,8,128]{2,1,0:T(8,128)} %get-tuple-element.8), channel_id=1, source_target_pairs={{0,2},{2,4},{3,1},{4,6},{5,3},{6,8},{7,5},{8,10},{9,7},{10,12},{11... | collective-permute-start | bytes 159752 | tf_op jit(solution)/shard_map/ppermute | solution.py:369
  8.8 9.7 %collective-permute-start.3 = (f32[13,8,128]{2,1,0:T(8,128)}, f32[13,8,128]{2,1,0:T(8,128)S(1)}, u32[]{:S(2)}, u32[]{:S(2)}) collective-permute-start(f32[13,8,128]{2,1,0:T(8,128)} %get-tuple-element.9), channel_id=1, source_target_pairs={{1,3},{2,0},{3,5},{4,2},{5,7},{6,4},{7,9},{8,6},{9,11},{10,8},{11,... | collective-permute-start | bytes 159752 | tf_op jit(solution)/shard_map/ppermute | solution.py:369

commit v2 on v1

--- a/solution.py
+++ b/solution.py
@@ -17,16 +17,25 @@
 LANE_TILES = 8
 USED = 6
 
-PERM_AT = 2 * BLOCKS * USED
+LEVELS = 16
+BULK = 2 * USED * 3
+PERM_AT = BULK
 STOR_AT = PERM_AT + LANE_TILES
 MASK_AT = STOR_AT + LANE_TILES
-REST_AT = MASK_AT + 2
-REST = BLOCKS * USED + 2 * LANE_TILES + 1
-REST_SLOTS = (REST + 1) // 2
-MESSAGE = REST_AT + REST_SLOTS
-THIN = BLOCKS * USED + 1
-THIN_SLOTS = (THIN + 1) // 2
-
+REST_AT = 8 * (MASK_AT + 2)
+HALF = USED // 2
+CELLS = 2 * (HALF + USED)
+REST = CELLS + 2 * LANE_TILES + 1
+THIN = CELLS + 1
+EDGE = 3
+
+
+def whole_tiles(rows):
+    return 8 * ((rows + 7) // 8)
+
+
+MESSAGE = whole_tiles(REST_AT + EDGE * REST + 8 - EDGE)
+THIN_MESSAGE = whole_tiles(EDGE * THIN + 8 - EDGE)
 
 OWN, TWO, SIDE, STRIP = 8, 48, 64, 112
 PADS = (0, 40, 56, 104)
@@ -41,69 +50,126 @@
     return pl.ds(128 * tile, 128)
 
 
-def half_rows(upper):
-    rows = lax.broadcasted_iota(jnp.int32, (8, 128), 0)
-    return rows // 4 == upper
-
-
 def joined_mask(mask_ref):
     parts = [mask_ref[0, by, bz] for by in range(2) for bz in range(2)]
     return jnp.concatenate(parts, axis=1)
 
 
-def pack_kernel(perm_ref, stor_ref, mask_ref, prev_ref, near_ref, far_ref, far2_ref, near2_ref, mask_buf):
+def height_of_lane():
+    return lax.rem(lax.broadcasted_iota(jnp.int32, (8, 128), 1), 32)
+
+
+def share(first, second):
+    heights = height_of_lane()
+    first_up, second_up = pltpu.roll(first, LEVELS, 1), pltpu.roll(second, LEVELS, 1)
+    return jnp.where(heights < LEVELS, first, second_up), first_up, second_up
+
+
+def unshare(common, first_rest, second_rest):
+    heights = height_of_lane()
+    first = jnp.where(heights < LEVELS, common, pltpu.roll(first_rest, 128 - LEVELS, 1))
+    second = pltpu.roll(jnp.where(heights >= LEVELS, common, second_rest), 128 - LEVELS, 1)
+    return first, second
+
+
+def put_edges(out_ref, at, pieces, rightward):
+    for n, tile in enumerate(pieces):
+        tile = jnp.where(rightward == 1, pltpu.roll(tile, EDGE, 0), tile)
+        out_ref[at + EDGE * n : at + EDGE * (n + 1)] = tile[:EDGE]
+
+
+def cells(tile):
+    low = height_of_lane() < 2
+    pieces = []
+    for by in range(2):
+        common, rests = [], [None] * USED
+        for u in range(HALF):
+            both, rests[u], rests[u + HALF] = share(tile(by, 0, u), tile(by, 0, u + HALF))
+            common.append(both)
+        pieces += common + [jnp.where(low, rests[u], tile(by, 1, u)) for u in range(USED)]
+    return pieces
+
+
+def put_message(out_ref, leftward, prev_tile, perm_tile, stor_tile, mask_tile):
+    low = height_of_lane() < 2
+    def put_tile(n, tile):
+        out_ref[8 * n : 8 * n + 8] = tile
+
+    for by in range(2):
+        for u in range(USED):
+            common, first_up, second_up = share(prev_tile(0, by, 0, u), prev_tile(1, by, 0, u))
+            at = 24 * (by * USED + u)
+            out_ref[at : at + 8] = common
+            out_ref[at + 8 : at + 16] = jnp.where(low, first_up, prev_tile(0, by, 1, u))
+            out_ref[at + 16 : at + 24] = jnp.where(low, second_up, prev_tile(1, by, 1, u))
+    for n in range(2):
+        put_tile(MASK_AT + n, mask_tile(n))
+    for t in range(LANE_TILES):
+        put_tile(PERM_AT + t, perm_tile(1 - leftward, t))
+        put_tile(STOR_AT + t, stor_tile(1 - leftward, t))
+    pieces = cells(functools.partial(prev_tile, 2))
+    pieces += [perm_tile(leftward, t) for t in range(LANE_TILES)]
+    pieces += [stor_tile(leftward, t) for t in range(LANE_TILES)]
+    pieces += [mask_tile(2)]
+    put_edges(out_ref, REST_AT, pieces, 1 - leftward)
+    tail = REST_AT + EDGE * REST
+    out_ref[tail:MESSAGE] = jnp.zeros((MESSAGE - tail, 128), F32)
+
+
+def eight(tile):
+    return pl.ds(pl.multiple_of(8 * tile, 8), 8)
+
+
+def put_thin(out_ref, leftward, prev_tile, mask_tile):
+    edge = 3 - 3 * leftward
+    pieces = cells(functools.partial(prev_tile, edge)) + [mask_tile(edge)]
+    put_edges(out_ref, 0, pieces, 1 - leftward)
+    tail = EDGE * THIN
+    out_ref[tail:THIN_MESSAGE] = jnp.zeros((THIN_MESSAGE - tail, 128), F32)
+
+
+def pack_kernel(
+    perm_ref, stor_ref, mask_ref, prev_ref, far_ref, far2_ref, near2_ref, near_ref, perm, stor, mask, prev, mask_buf, sems
+):
     odd = lax.rem(lax.axis_index("gx"), 2)
-    mask_buf[...] = joined_mask(mask_ref).astype(F32)
-
-    def rows_of(ref, tile, *rest):
-        return ref[(*rest[:-1], pl.ds(pl.multiple_of(8 * tile, 8), 8), rest[-1])]
-
-    def put_pairs(out_ref, at, slots, pieces, upper):
-        keep = half_rows(upper)
-        for s in range(slots):
-            tile = pieces[s]()
-            if s + slots < len(pieces):
-                tile = jnp.where(keep, tile, pltpu.roll(pieces[s + slots](), 4, 0))
-            out_ref[at + s] = tile
+    copies = []
+    for by in range(2):
+        for bz in range(2):
+            blk = 2 * by + bz
+            lanes = pl.ds(128 * box_tile(by, 0), 128 * USED)
+            copies.append((prev_ref.at[0, by, bz, :, lanes], prev.at[blk]))
+            copies.append((mask_ref.at[0, by, bz], mask.at[blk]))
+    copies += [(perm_ref, perm), (stor_ref, stor)]
+    copies = [pltpu.make_async_copy(src, dst, sems.at[n]) for n, (src, dst) in enumerate(copies)]
+    for copy in copies:
+        copy.start()
+    for copy in copies:
+        copy.wait()
+    mask_buf[...] = jnp.concatenate([mask[blk] for blk in range(BLOCKS)], axis=1).astype(F32)
+
+    def prev_tile(tile, by, bz, u):
+        return prev[2 * by + bz, eight(tile), lanes_of(u)]
+
+    def mask_tile(tile):
+        return mask_buf[eight(tile), lanes_of(0)]
 
     def message(out_ref, leftward):
-        first = 2 - 2 * leftward
-        for xt in range(2):
-            for blk in range(BLOCKS):
-                by, bz = divmod(blk, 2)
-                for u in range(USED):
-                    out_ref[(xt * BLOCKS + blk) * USED + u] = rows_of(
-                        prev_ref, first + xt, 0, by, bz, lanes_of(box_tile(by, u))
-                    )
-            out_ref[MASK_AT + xt] = rows_of(mask_buf, first + xt, lanes_of(0))
-        for t in range(LANE_TILES):
-            out_ref[PERM_AT + t] = rows_of(perm_ref, 1 - leftward, lanes_of(t))
-            out_ref[STOR_AT + t] = rows_of(stor_ref, 1 - leftward, lanes_of(t))
-        rest = 1 + leftward
-        pieces = [
-            functools.partial(rows_of, prev_ref, rest, 0, blk // 2, blk % 2, lanes_of(box_tile(blk // 2, u)))
-            for blk in range(BLOCKS)
-            for u in range(USED)
-        ]
-        pieces += [functools.partial(rows_of, perm_ref, leftward, lanes_of(t)) for t in range(LANE_TILES)]
-        pieces += [functools.partial(rows_of, stor_ref, leftward, lanes_of(t)) for t in range(LANE_TILES)]
-        pieces += [functools.partial(rows_of, mask_buf, rest, lanes_of(0))]
-        put_pairs(out_ref, REST_AT, REST_SLOTS, pieces, 1 - leftward)
-
-    def thin(out_ref, leftward):
-        edge = 3 - 3 * leftward
-        pieces = [
-            functools.partial(rows_of, prev_ref, edge, 0, blk // 2, blk % 2, lanes_of(box_tile(blk // 2, u)))
-            for blk in range(BLOCKS)
-            for u in range(USED)
-        ]
-        pieces += [functools.partial(rows_of, mask_buf, edge, lanes_of(0))]
-        put_pairs(out_ref, 0, THIN_SLOTS, pieces, 1 - leftward)
+        def tile_at(n):
+            return jnp.where(leftward == 1, n, (2, 3, 1)[n])
+
+        put_message(
+            out_ref,
+            leftward,
+            lambda n, by, bz, u: prev_tile(tile_at(n), by, bz, u),
+            lambda n, t: perm[eight(n), lanes_of(t)],
+            lambda n, t: stor[eight(n), lanes_of(t)],
+            lambda n: mask_tile(tile_at(n)),
+        )
 
     message(far_ref, 1 - odd)
+    put_thin(far2_ref, odd, prev_tile, mask_tile)
+    put_thin(near2_ref, 1 - odd, prev_tile, mask_tile)
     message(near_ref, odd)
-    thin(far2_ref, odd)
-    thin(near2_ref, 1 - odd)
 
 
 def main_kernel(
@@ -121,35 +187,34 @@
     zero = jnp.zeros((8, 128), F32)
 
     def left_big(i):
-        return jnp.where(odd, near_ref[i], far_ref[i])
+        at = pl.ds(8 * i, 8)
+        return jnp.where(odd, near_ref[at], far_ref[at])
 
     def right_big(i):
-        return jnp.where(odd, far_ref[i], near_ref[i])
-
-    def left_thin(i):
-        return jnp.where(odd, near2_ref[i], far2_ref[i])
-
-    def right_thin(i):
-        return jnp.where(odd, far2_ref[i], near2_ref[i])
-
-    def paired(left, right, at, slots, index):
-        slot = index % slots
-        tile = jnp.where(low_rows, right(at + slot), left(at + slot))
-        if index >= slots:
-            other = jnp.where(low_rows, left(at + slot), right(at + slot))
-            tile = pltpu.roll(other, 4, 0)
-        return tile
+        at = pl.ds(8 * i, 8)
+        return jnp.where(odd, far_ref[at], near_ref[at])
+
+    def edges(ref, at, left):
+        start = at - (8 - EDGE) if left else at
+        tile = ref[max(start, 0) : max(start, 0) + 8]
+        return pltpu.roll(tile, -start, 0) if start < 0 else tile
 
     def rest_tile(index):
-        return paired(left_big, right_big, REST_AT, REST_SLOTS, index)
+        at = REST_AT + EDGE * index
+        right = jnp.where(odd, edges(far_ref, at, False), edges(near_ref, at, False))
+        left = jnp.where(odd, edges(near_ref, at, True), edges(far_ref, at, True))
+        return jnp.where(low_rows, right, left)
 
     def thin_tile(index):
-        return paired(left_thin, right_thin, 0, THIN_SLOTS, index)
+        at = EDGE * index
+        right = jnp.where(odd, edges(far2_ref, at, False), edges(near2_ref, at, False))
+        left = jnp.where(odd, edges(near2_ref, at, True), edges(far2_ref, at, True))
+        return jnp.where(low_rows, right, left)
 
     for t in range(LANE_TILES):
         for buf, ref, bulk, rest in (
-            (kbuf, perm_ref, PERM_AT, BLOCKS * USED),
-            (cbuf, stor_ref, STOR_AT, BLOCKS * USED + LANE_TILES),
+            (kbuf, perm_ref, PERM_AT, CELLS),
+            (cbuf, stor_ref, STOR_AT, CELLS + LANE_TILES),
         ):
             buf[t, 0:8] = left_big(bulk + t)
             buf[t, 8:16] = ref[0:8, 128 * t : 128 * t + 128]
@@ -186,10 +251,27 @@
         spread = jnp.take_along_axis(tile, index, axis=1, mode="promise_in_bounds")
         return jnp.where((spread & lane_bits[bz]) != 0, 1.0, 0.0)
 
+    side = [{} for _ in range(5)]
+    two = {}
+    for by in range(2):
+        for u in range(USED):
+            at = 3 * (by * USED + u)
+            for side_tile, first in ((right_big, 0), (left_big, 3)):
+                common, first_top, second_top = [side_tile(at + n) for n in range(3)]
+                low, high = unshare(common, first_top, second_top)
+                side[first][by, 0, u], side[first + 1][by, 0, u] = low, high
+                side[first][by, 1, u], side[first + 1][by, 1, u] = first_top, second_top
+        base = by * (HALF + USED)
+        for fetch, cells_of in ((rest_tile, side[2]), (thin_tile, two)):
+            for u in range(HALF):
+                tops = [fetch(base + HALF + u), fetch(base + HALF + u + HALF)]
+                low, high = unshare(fetch(base + u), *tops)
+                cells_of[by, 0, u], cells_of[by, 0, u + HALF] = low, high
+                cells_of[by, 1, u], cells_of[by, 1, u + HALF] = tops
+
     for by in range(2):
         for bz in range(2):
             for u in range(USED):
-                cell = (2 * by + bz) * USED + u
                 for row in PADS:
                     pbuf[by, bz, u, row : row + 8] = zero
 
@@ -201,12 +283,9 @@
                 for k in range(4):
                     at = 128 * box_tile(by, u)
                     put(OWN + 8 * k, prev_ref[0, by, bz, 8 * k : 8 * k + 8, at : at + 128], own_bits[k])
-                put(TWO, thin_tile(cell), two_bits)
-                put(SIDE, right_big(cell), side_bits[0])
-                put(SIDE + 8, right_big(BLOCKS * USED + cell), side_bits[1])
-                put(SIDE + 16, rest_tile(cell), side_bits[2])
-                put(SIDE + 24, left_big(cell), side_bits[3])
-                put(SIDE + 32, left_big(BLOCKS * USED + cell), side_bits[4])
+                put(TWO, two[by, bz, u], two_bits)
+                for n in range(5):
+                    put(SIDE + 8 * n, side[n][by, bz, u], side_bits[n])
 
     def up_y(here_, next_):
         return pltpu.roll(jnp.where(lanes >= 32, here_, next_), 96, 1)
@@ -353,15 +432,22 @@
 
 def shards(permeability, storage, support_mask, prev_basis):
     vmem = pl.BlockSpec(memory_space=pltpu.VMEM)
-    near, far, far2, near2 = pl.pallas_call(
+    arguments = (permeability, storage, support_mask, prev_basis)
+    far, far2, near2, near = pl.pallas_call(
         pack_kernel,
-        in_specs=[vmem] * 4,
+        in_specs=[pl.BlockSpec(memory_space=pl.ANY)] * 4,
         out_specs=[vmem] * 4,
-        out_shape=[jax.ShapeDtypeStruct((n, 8, 128), F32) for n in (MESSAGE, MESSAGE, THIN_SLOTS, THIN_SLOTS)],
-        scratch_shapes=[pltpu.VMEM((32, 128), F32)],
+        out_shape=[pltpu.VMEM((n, 128), F32) for n in (MESSAGE, THIN_MESSAGE, THIN_MESSAGE, MESSAGE)],
+        scratch_shapes=[
+            pltpu.VMEM(permeability.shape, F32),
+            pltpu.VMEM(storage.shape, F32),
+            pltpu.VMEM((BLOCKS, 32, 32), jnp.int32),
+            pltpu.VMEM((BLOCKS, 32, 128 * USED), F32),
+            pltpu.VMEM((32, 128), F32),
+            pltpu.SemaphoreType.DMA((2 * BLOCKS + 2,)),
+        ],
         name="pack",
-    )(permeability, storage, support_mask, prev_basis)
-
+    )(*arguments)
     size = lax.axis_size("gx")
 
     def move(x, step_even, step_odd):
@@ -395,7 +481,7 @@
         ],
         compiler_params=pltpu.CompilerParams(vmem_limit_bytes=32 * 1024 * 1024),
         name="smooth",
-    )(permeability, storage, support_mask, prev_basis, near, far, far2, near2)
+    )(*arguments, near, far, far2, near2)
 
 
 def solution(mesh):

time: 24.6 us -> 21.9 us (0.89)
  the two profiles are of different devices: /device:TPU:8 before, /device:TPU:0 now
where the time goes in v2:
time: 21.9 us; the launch traced here: 21.7 us
  starting transfers between devices  8.16 us (37%)
  Pallas kernels  7.31 us (33%)
  waiting for transfers between devices  5.5 us (25%)
  between operations  0.72 us (3%)
    ppermute x4, starting transfers between devices, move(): return lax.ppermute(x, 'gx', [(i, j) for i, j in pairs if 0 <= j < size])  8.16 us
    pallas_call x1, Pallas kernels, shards(): pl.pallas_call(main_kernel, in_specs=[vmem] * 8, out_specs=[vmem] * 2, ou...  5.86 us
    ppermute x4, waiting for transfers between devices, move(): return lax.ppermute(x, 'gx', [(i, j) for i, j in pairs if 0 <= j < size])  5.5 us
    pallas_call x1, Pallas kernels, shards(): pl.pallas_call(pack_kernel, in_specs=[pl.BlockSpec(memory_space=pl.ANY)]...  1.45 us
  transfers between devices with their start and end apart: 4, of which 2 were waited for; matrix products, arithmetic and copies ran while one was open for 0% of the time, Pallas kernels for 0%

profile of v2, /device:TPU:0, one launch (start us, length us, event | category | flops | bytes accessed | tf_op | source)
XLA Modules:
  0.0 21.7 jit_solution(10519495588972975725)
XLA Ops:
  0.6 0.0 copy-start
  0.6 0.0 copy-start.3
  0.7 0.0 copy-start.2
  0.7 0.0 copy-start.1
  0.7 1.4 %pack.1 = (f32[544,128]{1,0:T(8,128)S(1)}, f32[64,128]{1,0:T(8,128)S(1)}, f32[64,128]{1,0:T(8,128)S(1)}, f32[544,128]{1,0:T(8,128)S(1)}) custom-call(f32[16,1024]{1,0:T(8,128)} %perm_ref.3, f32[16,1024]{1,0:T(8,128)} %stor_ref.3, s32[1,2,2,32,32]{4,3,2,1,0:T(8,128)} %mask_ref.3, f32[1,2,2,32,1024]{4,3,2,1,0:T(8,128)} %prev_ref.3), custom_call_target="tpu_custom_call" | custom-call | tf_op jit(solution)/shard_map/pack/pallas_call | solution.py:436
  2.1 0.5 %collective-permute-start = (f32[544,128]{1,0:T(8,128)S(1)}, f32[544,128]{1,0:T(8,128)S(1)}, u32[]{:S(2)}, u32[]{:S(2)}) collective-permute-start(f32[544,128]{1,0:T(8,128)S(1)} %get-tuple-element.6), channel_id=1, source_target_pairs={{0,1},{1,0},{2,3},{3,2},{4,5},{5,4},{6,7},{7,6},{8,9},{9,8},{10,11... | collective-permute-start | bytes 835592 | tf_op jit(solution)/shard_map/ppermute | solution.py:455
  2.6 0.7 %collective-permute-start.1 = (f32[544,128]{1,0:T(8,128)S(1)}, f32[544,128]{1,0:T(8,128)S(1)}, u32[]{:S(2)}, u32[]{:S(2)}) collective-permute-start(f32[544,128]{1,0:T(8,128)S(1)} %get-tuple-element.7), channel_id=1, source_target_pairs={{1,2},{2,1},{3,4},{4,3},{5,6},{6,5},{7,8},{8,7},{9,10},{10,9},{11,... | collective-permute-start | bytes 835592 | tf_op jit(solution)/shard_map/ppermute | solution.py:455
  3.3 5.7 %collective-permute-start.2 = (f32[64,128]{1,0:T(8,128)S(1)}, f32[64,128]{1,0:T(8,128)S(1)}, u32[]{:S(2)}, u32[]{:S(2)}) collective-permute-start(f32[64,128]{1,0:T(8,128)S(1)} %get-tuple-element.8), channel_id=1, source_target_pairs={{0,2},{2,4},{3,1},{4,6},{5,3},{6,8},{7,5},{8,10},{9,7},{10,12},{11... | collective-permute-start | bytes 98312 | tf_op jit(solution)/shard_map/ppermute | solution.py:455
  9.0 1.3 %collective-permute-start.3 = (f32[64,128]{1,0:T(8,128)S(1)}, f32[64,128]{1,0:T(8,128)S(1)}, u32[]{:S(2)}, u32[]{:S(2)}) collective-permute-start(f32[64,128]{1,0:T(8,128)S(1)} %get-tuple-element.9), channel_id=1, source_target_pairs={{1,3},{2,0},{3,5},{4,2},{5,7},{6,4},{7,9},{8,6},{9,11},{10,8},{11,... | collective-permute-start | bytes 98312 | tf_op jit(solution)/shard_map/ppermute | solution.py:455
  10.3 2.9 %collective-permute-done.2.far2_ref = f32[64,128]{1,0:T(8,128)S(1)} collective-permute-done((f32[64,128]{1,0:T(8,128)S(1)}, f32[64,128]{1,0:T(8,128)S(1)}, u32[]{:S(2)}, u32[]{:S(2)}) %collective-permute-start.2) | collective-permute-done | bytes 32800 | tf_op jit(solution)/shard_map/ppermute | solution.py:455
  13.2 2.6 %collective-permute-done.3.near2_ref = f32[64,128]{1,0:T(8,128)S(1)} collective-permute-done((f32[64,128]{1,0:T(8,128)S(1)}, f32[64,128]{1,0:T(8,128)S(1)}, u32[]{:S(2)}, u32[]{:S(2)}) %collective-permute-start.3) | collective-permute-done | bytes 32800 | tf_op jit(solution)/shard_map/ppermute | solution.py:455
  15.8 0.0 collective-permute-done.near_ref
  15.8 0.0 collective-permute-done.1.far_ref
  15.8 0.0 copy-done
  15.8 0.0 copy-done.3
  15.8 0.0 copy-done.2
  15.8 0.0 copy-done.1
  15.9 5.9 %smooth.1 = (f32[1,2,2,32,1024]{4,3,2,1,0:T(8,128)}, f32[1,2,2,27]{3,2,1,0:T(2,128)}) custom-call(f32[16,1024]{1,0:T(8,128)S(1)} %copy-done.1, f32[16,1024]{1,0:T(8,128)S(1)} %copy-done.2, s32[1,2,2,32,32]{4,3,2,1,0:T(8,128)S(1)} %copy-done.3, f32[1,2,2,32,1024]{4,3,2,1,0:T(8,128)S(1)} %copy-done, f32[544,128]{1,0:T(8,128)S(1)} %collective-permute-done.near_ref, ...), custom_call_target="tpu_custom_call" | custom-call | tf_op jit(solution)/shard_map/smooth/pallas_call | solution.py:463
Async XLA Ops:
  0.6 15.2 %copy-start = (f32[1,2,2,32,1024]{4,3,2,1,0:T(8,128)S(1)}, f32[1,2,2,32,1024]{4,3,2,1,0:T(8,128)}, u32[]{:S(2)}) copy-start(f32[1,2,2,32,1024]{4,3,2,1,0:T(8,128)} %prev_ref.3) | copy-start | bytes 1572868
  0.6 15.2 %copy-start.3 = (s32[1,2,2,32,32]{4,3,2,1,0:T(8,128)S(1)}, s32[1,2,2,32,32]{4,3,2,1,0:T(8,128)}, u32[]{:S(2)}) copy-start(s32[1,2,2,32,32]{4,3,2,1,0:T(8,128)} %mask_ref.3) | copy-start | bytes 49156
  0.7 15.2 %copy-start.2 = (f32[16,1024]{1,0:T(8,128)S(1)}, f32[16,1024]{1,0:T(8,128)}, u32[]{:S(2)}) copy-start(f32[16,1024]{1,0:T(8,128)} %stor_ref.3) | copy-start | bytes 196612
  0.7 15.2 %copy-start.1 = (f32[16,1024]{1,0:T(8,128)S(1)}, f32[16,1024]{1,0:T(8,128)}, u32[]{:S(2)}) copy-start(f32[16,1024]{1,0:T(8,128)} %perm_ref.3) | copy-start | bytes 196612
  2.1 13.7 %collective-permute-start = (f32[544,128]{1,0:T(8,128)S(1)}, f32[544,128]{1,0:T(8,128)S(1)}, u32[]{:S(2)}, u32[]{:S(2)}) collective-permute-start(f32[544,128]{1,0:T(8,128)S(1)} %get-tuple-element.6), channel_id=1, source_target_pairs={{0,1},{1,0},{2,3},{3,2},{4,5},{5,4},{6,7},{7,6},{8,9},{9,8},{10,11... | collective-permute-start | bytes 835592 | tf_op jit(solution)/shard_map/ppermute | solution.py:455
  2.6 13.2 %collective-permute-start.1 = (f32[544,128]{1,0:T(8,128)S(1)}, f32[544,128]{1,0:T(8,128)S(1)}, u32[]{:S(2)}, u32[]{:S(2)}) collective-permute-start(f32[544,128]{1,0:T(8,128)S(1)} %get-tuple-element.7), channel_id=1, source_target_pairs={{1,2},{2,1},{3,4},{4,3},{5,6},{6,5},{7,8},{8,7},{9,10},{10,9},{11,... | collective-permute-start | bytes 835592 | tf_op jit(solution)/shard_map/ppermute | solution.py:455
  3.3 9.9 %collective-permute-start.2 = (f32[64,128]{1,0:T(8,128)S(1)}, f32[64,128]{1,0:T(8,128)S(1)}, u32[]{:S(2)}, u32[]{:S(2)}) collective-permute-start(f32[64,128]{1,0:T(8,128)S(1)} %get-tuple-element.8), channel_id=1, source_target_pairs={{0,2},{2,4},{3,1},{4,6},{5,3},{6,8},{7,5},{8,10},{9,7},{10,12},{11... | collective-permute-start | bytes 98312 | tf_op jit(solution)/shard_map/ppermute | solution.py:455
  9.0 6.8 %collective-permute-start.3 = (f32[64,128]{1,0:T(8,128)S(1)}, f32[64,128]{1,0:T(8,128)S(1)}, u32[]{:S(2)}, u32[]{:S(2)}) collective-permute-start(f32[64,128]{1,0:T(8,128)S(1)} %get-tuple-element.9), channel_id=1, source_target_pairs={{1,3},{2,0},{3,5},{4,2},{5,7},{6,4},{7,9},{8,6},{9,11},{10,8},{11,... | collective-permute-start | bytes 98312 | tf_op jit(solution)/shard_map/ppermute | solution.py:455

commit v3 on v2

--- a/solution.py
+++ b/solution.py
@@ -306,23 +306,25 @@
     def harmonic(a, b):
         return 2.0 * (a * b) * inverse(jnp.maximum(a + b, TINY))
 
-    south = [zero] * 5
+    def edge_k(t, i):
+        return kbuf[t, 8 * i : 8 * i + 8] if 0 <= t < LANE_TILES else zero
+
     for t in range(LANE_TILES):
-        k = [kbuf[t, 8 * i : 8 * i + 8] for i in range(5)]
-        turned = [pltpu.roll(v, 7, 0) for v in k]
-        east = [harmonic(k[i], jnp.where(rows < 7, turned[i], turned[(i + 1) % 5])) for i in range(5)]
-        turned = [pltpu.roll(v, 1, 0) for v in east]
-        west = [jnp.where(rows > 0, turned[i], turned[i - 1]) for i in range(5)]
+        k = [edge_k(t, i) for i in range(5)]
+        ups = [pltpu.roll(v, 7, 0) for v in k]
+        downs = [pltpu.roll(v, 1, 0) for v in k]
         for i in range(5):
-            above = kbuf[t + 1, 8 * i : 8 * i + 8] if t + 1 < LANE_TILES else zero
-            north = harmonic(k[i], up_y(k[i], above))
-            upper = jnp.where(heights < 31, harmonic(k[i], up_z(k[i])), 0.0)
-            lower = down_z(upper)
-            below = down_y(north, south[i])
-            south[i] = north
-            diag = cbuf[t, 8 * i : 8 * i + 8] + east[i] + west[i] + north + below + upper + lower
+            faces = [
+                harmonic(k[i], jnp.where(rows < 7, ups[i], ups[(i + 1) % 5])),
+                harmonic(k[i], jnp.where(rows > 0, downs[i], downs[i - 1])),
+                harmonic(k[i], up_y(k[i], edge_k(t + 1, i))),
+                harmonic(k[i], down_y(k[i], edge_k(t - 1, i))),
+                jnp.where(heights < 31, harmonic(k[i], up_z(k[i])), 0.0),
+                jnp.where(heights > 0, harmonic(k[i], down_z(k[i])), 0.0),
+            ]
+            diag = functools.reduce(lambda a, b: a + b, faces, cbuf[t, 8 * i : 8 * i + 8])
             scale = (2.0 / 3.0) * inverse(jnp.maximum(diag, TINY))
-            for d, face in enumerate((east[i], west[i], north, below, upper, lower)):
+            for d, face in enumerate(faces):
                 wbuf[t, d, 8 * i : 8 * i + 8] = face * scale
             gbuf[t, 8 * i : 8 * i + 8] = 1.5 * diag
 

time: 21.9 us -> 20.8 us (0.950)
  Pallas kernels: 7.31 us -> 6.16 us
    pallas_call x1, Pallas kernels: 5.86 us -> 4.71 us  [shards(): pl.pallas_call(main_kernel, in_specs=[vmem] * 8, out_specs=[vmem] * 2, ou...]
where the time goes in v3:
time: 20.8 us; the launch traced here: 20.6 us
  starting transfers between devices  8.16 us (39%)
  Pallas kernels  6.16 us (30%)
  waiting for transfers between devices  5.5 us (26%)
  between operations  0.72 us (3%)
    ppermute x4, starting transfers between devices, move(): return lax.ppermute(x, 'gx', [(i, j) for i, j in pairs if 0 <= j < size])  8.16 us
    ppermute x4, waiting for transfers between devices, move(): return lax.ppermute(x, 'gx', [(i, j) for i, j in pairs if 0 <= j < size])  5.5 us
    pallas_call x1, Pallas kernels, shards(): pl.pallas_call(main_kernel, in_specs=[vmem] * 8, out_specs=[vmem] * 2, ou...  4.71 us
    pallas_call x1, Pallas kernels, shards(): pl.pallas_call(pack_kernel, in_specs=[pl.BlockSpec(memory_space=pl.ANY)]...  1.45 us
  transfers between devices with their start and end apart: 4, of which 2 were waited for; matrix products, arithmetic and copies ran while one was open for 0% of the time, Pallas kernels for 0%

profile of v3, /device:TPU:0, one launch (start us, length us, event | category | flops | bytes accessed | tf_op | source)
XLA Modules:
  0.0 20.6 jit_solution(7432336256941061249)
XLA Ops:
  0.6 0.0 copy-start
  0.6 0.0 copy-start.3
  0.7 0.0 copy-start.2
  0.7 0.0 copy-start.1
  0.7 1.4 %pack.1 = (f32[544,128]{1,0:T(8,128)S(1)}, f32[64,128]{1,0:T(8,128)S(1)}, f32[64,128]{1,0:T(8,128)S(1)}, f32[544,128]{1,0:T(8,128)S(1)}) custom-call(f32[16,1024]{1,0:T(8,128)} %perm_ref.3, f32[16,1024]{1,0:T(8,128)} %stor_ref.3, s32[1,2,2,32,32]{4,3,2,1,0:T(8,128)} %mask_ref.3, f32[1,2,2,32,1024]{4,3,2,1,0:T(8,128)} %prev_ref.3), custom_call_target="tpu_custom_call" | custom-call | tf_op jit(solution)/shard_map/pack/pallas_call | solution.py:438
  2.1 0.5 %collective-permute-start = (f32[544,128]{1,0:T(8,128)S(1)}, f32[544,128]{1,0:T(8,128)S(1)}, u32[]{:S(2)}, u32[]{:S(2)}) collective-permute-start(f32[544,128]{1,0:T(8,128)S(1)} %get-tuple-element.6), channel_id=1, source_target_pairs={{0,1},{1,0},{2,3},{3,2},{4,5},{5,4},{6,7},{7,6},{8,9},{9,8},{10,11... | collective-permute-start | bytes 835592 | tf_op jit(solution)/shard_map/ppermute | solution.py:457
  2.6 0.7 %collective-permute-start.1 = (f32[544,128]{1,0:T(8,128)S(1)}, f32[544,128]{1,0:T(8,128)S(1)}, u32[]{:S(2)}, u32[]{:S(2)}) collective-permute-start(f32[544,128]{1,0:T(8,128)S(1)} %get-tuple-element.7), channel_id=1, source_target_pairs={{1,2},{2,1},{3,4},{4,3},{5,6},{6,5},{7,8},{8,7},{9,10},{10,9},{11,... | collective-permute-start | bytes 835592 | tf_op jit(solution)/shard_map/ppermute | solution.py:457
  3.3 5.7 %collective-permute-start.2 = (f32[64,128]{1,0:T(8,128)S(1)}, f32[64,128]{1,0:T(8,128)S(1)}, u32[]{:S(2)}, u32[]{:S(2)}) collective-permute-start(f32[64,128]{1,0:T(8,128)S(1)} %get-tuple-element.8), channel_id=1, source_target_pairs={{0,2},{2,4},{3,1},{4,6},{5,3},{6,8},{7,5},{8,10},{9,7},{10,12},{11... | collective-permute-start | bytes 98312 | tf_op jit(solution)/shard_map/ppermute | solution.py:457
  9.0 1.3 %collective-permute-start.3 = (f32[64,128]{1,0:T(8,128)S(1)}, f32[64,128]{1,0:T(8,128)S(1)}, u32[]{:S(2)}, u32[]{:S(2)}) collective-permute-start(f32[64,128]{1,0:T(8,128)S(1)} %get-tuple-element.9), channel_id=1, source_target_pairs={{1,3},{2,0},{3,5},{4,2},{5,7},{6,4},{7,9},{8,6},{9,11},{10,8},{11,... | collective-permute-start | bytes 98312 | tf_op jit(solution)/shard_map/ppermute | solution.py:457
  10.3 2.9 %collective-permute-done.2.far2_ref = f32[64,128]{1,0:T(8,128)S(1)} collective-permute-done((f32[64,128]{1,0:T(8,128)S(1)}, f32[64,128]{1,0:T(8,128)S(1)}, u32[]{:S(2)}, u32[]{:S(2)}) %collective-permute-start.2) | collective-permute-done | bytes 32800 | tf_op jit(solution)/shard_map/ppermute | solution.py:457
  13.2 2.6 %collective-permute-done.3.near2_ref = f32[64,128]{1,0:T(8,128)S(1)} collective-permute-done((f32[64,128]{1,0:T(8,128)S(1)}, f32[64,128]{1,0:T(8,128)S(1)}, u32[]{:S(2)}, u32[]{:S(2)}) %collective-permute-start.3) | collective-permute-done | bytes 32800 | tf_op jit(solution)/shard_map/ppermute | solution.py:457
  15.8 0.0 collective-permute-done.near_ref
  15.8 0.0 collective-permute-done.1.far_ref
  15.8 0.0 copy-done
  15.8 0.0 copy-done.3
  15.8 0.0 copy-done.2
  15.8 0.0 copy-done.1
  15.9 4.7 %smooth.1 = (f32[1,2,2,32,1024]{4,3,2,1,0:T(8,128)}, f32[1,2,2,27]{3,2,1,0:T(2,128)}) custom-call(f32[16,1024]{1,0:T(8,128)S(1)} %copy-done.1, f32[16,1024]{1,0:T(8,128)S(1)} %copy-done.2, s32[1,2,2,32,32]{4,3,2,1,0:T(8,128)S(1)} %copy-done.3, f32[1,2,2,32,1024]{4,3,2,1,0:T(8,128)S(1)} %copy-done, f32[544,128]{1,0:T(8,128)S(1)} %collective-permute-done.near_ref, ...), custom_call_target="tpu_custom_call" | custom-call | tf_op jit(solution)/shard_map/smooth/pallas_call | solution.py:465
Async XLA Ops:
  0.6 15.2 %copy-start = (f32[1,2,2,32,1024]{4,3,2,1,0:T(8,128)S(1)}, f32[1,2,2,32,1024]{4,3,2,1,0:T(8,128)}, u32[]{:S(2)}) copy-start(f32[1,2,2,32,1024]{4,3,2,1,0:T(8,128)} %prev_ref.3) | copy-start | bytes 1572868
  0.6 15.2 %copy-start.3 = (s32[1,2,2,32,32]{4,3,2,1,0:T(8,128)S(1)}, s32[1,2,2,32,32]{4,3,2,1,0:T(8,128)}, u32[]{:S(2)}) copy-start(s32[1,2,2,32,32]{4,3,2,1,0:T(8,128)} %mask_ref.3) | copy-start | bytes 49156
  0.7 15.2 %copy-start.2 = (f32[16,1024]{1,0:T(8,128)S(1)}, f32[16,1024]{1,0:T(8,128)}, u32[]{:S(2)}) copy-start(f32[16,1024]{1,0:T(8,128)} %stor_ref.3) | copy-start | bytes 196612
  0.7 15.2 %copy-start.1 = (f32[16,1024]{1,0:T(8,128)S(1)}, f32[16,1024]{1,0:T(8,128)}, u32[]{:S(2)}) copy-start(f32[16,1024]{1,0:T(8,128)} %perm_ref.3) | copy-start | bytes 196612
  2.1 13.7 %collective-permute-start = (f32[544,128]{1,0:T(8,128)S(1)}, f32[544,128]{1,0:T(8,128)S(1)}, u32[]{:S(2)}, u32[]{:S(2)}) collective-permute-start(f32[544,128]{1,0:T(8,128)S(1)} %get-tuple-element.6), channel_id=1, source_target_pairs={{0,1},{1,0},{2,3},{3,2},{4,5},{5,4},{6,7},{7,6},{8,9},{9,8},{10,11... | collective-permute-start | bytes 835592 | tf_op jit(solution)/shard_map/ppermute | solution.py:457
  2.6 13.2 %collective-permute-start.1 = (f32[544,128]{1,0:T(8,128)S(1)}, f32[544,128]{1,0:T(8,128)S(1)}, u32[]{:S(2)}, u32[]{:S(2)}) collective-permute-start(f32[544,128]{1,0:T(8,128)S(1)} %get-tuple-element.7), channel_id=1, source_target_pairs={{1,2},{2,1},{3,4},{4,3},{5,6},{6,5},{7,8},{8,7},{9,10},{10,9},{11,... | collective-permute-start | bytes 835592 | tf_op jit(solution)/shard_map/ppermute | solution.py:457
  3.3 9.9 %collective-permute-start.2 = (f32[64,128]{1,0:T(8,128)S(1)}, f32[64,128]{1,0:T(8,128)S(1)}, u32[]{:S(2)}, u32[]{:S(2)}) collective-permute-start(f32[64,128]{1,0:T(8,128)S(1)} %get-tuple-element.8), channel_id=1, source_target_pairs={{0,2},{2,4},{3,1},{4,6},{5,3},{6,8},{7,5},{8,10},{9,7},{10,12},{11... | collective-permute-start | bytes 98312 | tf_op jit(solution)/shard_map/ppermute | solution.py:457
  9.0 6.8 %collective-permute-start.3 = (f32[64,128]{1,0:T(8,128)S(1)}, f32[64,128]{1,0:T(8,128)S(1)}, u32[]{:S(2)}, u32[]{:S(2)}) collective-permute-start(f32[64,128]{1,0:T(8,128)S(1)} %get-tuple-element.9), channel_id=1, source_target_pairs={{1,3},{2,0},{3,5},{4,2},{5,7},{6,4},{7,9},{8,6},{9,11},{10,8},{11,... | collective-permute-start | bytes 98312 | tf_op jit(solution)/shard_map/ppermute | solution.py:457

commit v4 on v3

--- a/solution.py
+++ b/solution.py
@@ -132,6 +132,7 @@
     perm_ref, stor_ref, mask_ref, prev_ref, far_ref, far2_ref, near2_ref, near_ref, perm, stor, mask, prev, mask_buf, sems
 ):
     odd = lax.rem(lax.axis_index("gx"), 2)
+    odd_chip = lax.rem(lax.axis_index("gx") // 2, 2)
     copies = []
     for by in range(2):
         for bz in range(2):
@@ -167,19 +168,20 @@
         )
 
     message(far_ref, 1 - odd)
-    put_thin(far2_ref, odd, prev_tile, mask_tile)
-    put_thin(near2_ref, 1 - odd, prev_tile, mask_tile)
+    put_thin(far2_ref, odd_chip, prev_tile, mask_tile)
+    put_thin(near2_ref, 1 - odd_chip, prev_tile, mask_tile)
     message(near_ref, odd)
 
 
 def main_kernel(
-    perm_ref, stor_ref, mask_ref, prev_ref, near_ref, far_ref, far2_ref, near2_ref,
+    perm_ref, stor_ref, mask_ref, prev_ref, far_ref, far2_ref, near2_ref, near_ref,
     basis_ref, coarse_ref,
     kbuf, cbuf, wbuf, gbuf, sup, pbuf, qbuf, own_mask, sums,
 ):
     here = lax.axis_index("gx")
     last = lax.axis_size("gx") - 1
     odd = lax.rem(here, 2) == 1
+    odd_chip = lax.rem(here // 2, 2) == 1
     rows = lax.broadcasted_iota(jnp.int32, (8, 128), 0)
     lanes = lax.broadcasted_iota(jnp.int32, (8, 128), 1)
     heights = lax.rem(lanes, 32)
@@ -207,8 +209,8 @@
 
     def thin_tile(index):
         at = EDGE * index
-        right = jnp.where(odd, edges(far2_ref, at, False), edges(near2_ref, at, False))
-        left = jnp.where(odd, edges(near2_ref, at, True), edges(far2_ref, at, True))
+        right = jnp.where(odd_chip, edges(near2_ref, at, False), edges(far2_ref, at, False))
+        left = jnp.where(odd_chip, edges(far2_ref, at, True), edges(near2_ref, at, True))
         return jnp.where(low_rows, right, left)
 
     for t in range(LANE_TILES):
@@ -452,14 +454,14 @@
     )(*arguments)
     size = lax.axis_size("gx")
 
-    def move(x, step_even, step_odd):
-        pairs = [(i, i + (step_odd if i % 2 else step_even)) for i in range(size)]
+    def move(x, step, width):
+        pairs = [(i, i + (-step if i // width % 2 else step)) for i in range(size)]
         return lax.ppermute(x, "gx", [(i, j) for i, j in pairs if 0 <= j < size])
 
     far = move(far, -1, 1)
-    far2 = move(far2, 2, -2)
+    far2 = move(far2, 2, 2)
     near2 = move(near2, -2, 2)
-    near = move(near, 1, -1)
+    near = move(near, 1, 1)
 
     strips = (2, 2, USED, STRIP, 128)
     return pl.pallas_call(
@@ -483,7 +485,7 @@
         ],
         compiler_params=pltpu.CompilerParams(vmem_limit_bytes=32 * 1024 * 1024),
         name="smooth",
-    )(*arguments, near, far, far2, near2)
+    )(*arguments, far, far2, near2, near)
 
 
 def solution(mesh):

time: 20.8 us -> 19.5 us (0.938)
  the two profiles are of different devices: /device:TPU:0 before, /device:TPU:8 now
where the time goes in v4:
time: 19.5 us; the launch traced here: 19.2 us
  starting transfers between devices  7.41 us (38%)
  Pallas kernels  6.16 us (32%)
  waiting for transfers between devices  4.91 us (25%)
  between operations  0.72 us (4%)
    ppermute x4, starting transfers between devices, move(): return lax.ppermute(x, 'gx', [(i, j) for i, j in pairs if 0 <= j < size])  7.41 us
    ppermute x4, waiting for transfers between devices, move(): return lax.ppermute(x, 'gx', [(i, j) for i, j in pairs if 0 <= j < size])  4.91 us
    pallas_call x1, Pallas kernels, shards(): pl.pallas_call(main_kernel, in_specs=[vmem] * 8, out_specs=[vmem] * 2, ou...  4.71 us
    pallas_call x1, Pallas kernels, shards(): pl.pallas_call(pack_kernel, in_specs=[pl.BlockSpec(memory_space=pl.ANY)]...  1.44 us
  transfers between devices with their start and end apart: 4, of which 1 were waited for; matrix products, arithmetic and copies ran while one was open for 0% of the time, Pallas kernels for 0%

profile of v4, /device:TPU:8, one launch (start us, length us, event | category | flops | bytes accessed | tf_op | source)
XLA Modules:
  0.0 19.2 jit_solution(3862551731014138753)
XLA Ops:
  0.6 0.0 copy-start
  0.6 0.0 copy-start.3
  0.7 0.0 copy-start.2
  0.7 0.0 copy-start.1
  0.7 1.4 %pack.1 = (f32[544,128]{1,0:T(8,128)S(1)}, f32[64,128]{1,0:T(8,128)S(1)}, f32[64,128]{1,0:T(8,128)S(1)}, f32[544,128]{1,0:T(8,128)S(1)}) custom-call(f32[16,1024]{1,0:T(8,128)} %perm_ref.3, f32[16,1024]{1,0:T(8,128)} %stor_ref.3, s32[1,2,2,32,32]{4,3,2,1,0:T(8,128)} %mask_ref.3, f32[1,2,2,32,1024]{4,3,2,1,0:T(8,128)} %prev_ref.3), custom_call_target="tpu_custom_call" | custom-call | tf_op jit(solution)/shard_map/pack/pallas_call | solution.py:440
  2.1 2.8 %collective-permute-start = (f32[544,128]{1,0:T(8,128)S(1)}, f32[544,128]{1,0:T(8,128)S(1)}, u32[]{:S(2)}, u32[]{:S(2)}) collective-permute-start(f32[544,128]{1,0:T(8,128)S(1)} %get-tuple-element.6), channel_id=1, source_target_pairs={{1,2},{2,1},{3,4},{4,3},{5,6},{6,5},{7,8},{8,7},{9,10},{10,9},{11,... | collective-permute-start | bytes 835592 | tf_op jit(solution)/shard_map/ppermute | solution.py:459
  4.9 0.9 %collective-permute-start.3 = (f32[544,128]{1,0:T(8,128)S(1)}, f32[544,128]{1,0:T(8,128)S(1)}, u32[]{:S(2)}, u32[]{:S(2)}) collective-permute-start(f32[544,128]{1,0:T(8,128)S(1)} %get-tuple-element.9), channel_id=1, source_target_pairs={{0,1},{1,0},{2,3},{3,2},{4,5},{5,4},{6,7},{7,6},{8,9},{9,8},{10,11... | collective-permute-start | bytes 835592 | tf_op jit(solution)/shard_map/ppermute | solution.py:459
  5.7 1.5 %collective-permute-start.1 = (f32[64,128]{1,0:T(8,128)S(1)}, f32[64,128]{1,0:T(8,128)S(1)}, u32[]{:S(2)}, u32[]{:S(2)}) collective-permute-start(f32[64,128]{1,0:T(8,128)S(1)} %get-tuple-element.7), channel_id=1, source_target_pairs={{0,2},{1,3},{2,0},{3,1},{4,6},{5,7},{6,4},{7,5},{8,10},{9,11},{10,... | collective-permute-start | bytes 98312 | tf_op jit(solution)/shard_map/ppermute | solution.py:459
  7.3 2.3 %collective-permute-start.2 = (f32[64,128]{1,0:T(8,128)S(1)}, f32[64,128]{1,0:T(8,128)S(1)}, u32[]{:S(2)}, u32[]{:S(2)}) collective-permute-start(f32[64,128]{1,0:T(8,128)S(1)} %get-tuple-element.8), channel_id=1, source_target_pairs={{2,4},{3,5},{4,2},{5,3},{6,8},{7,9},{8,6},{9,7},{10,12},{11,13},{1... | collective-permute-start | bytes 98312 | tf_op jit(solution)/shard_map/ppermute | solution.py:459
  9.6 4.9 %collective-permute-done.1.far2_ref = f32[64,128]{1,0:T(8,128)S(1)} collective-permute-done((f32[64,128]{1,0:T(8,128)S(1)}, f32[64,128]{1,0:T(8,128)S(1)}, u32[]{:S(2)}, u32[]{:S(2)}) %collective-permute-start.1) | collective-permute-done | bytes 32800 | tf_op jit(solution)/shard_map/ppermute | solution.py:459
  14.5 0.0 collective-permute-done.2.near2_ref
  14.5 0.0 collective-permute-done.far_ref
  14.5 0.0 collective-permute-done.3.near_ref
  14.5 0.0 copy-done
  14.5 0.0 copy-done.3
  14.5 0.0 copy-done.2
  14.5 0.0 copy-done.1
  14.5 4.7 %smooth.1 = (f32[1,2,2,32,1024]{4,3,2,1,0:T(8,128)}, f32[1,2,2,27]{3,2,1,0:T(2,128)}) custom-call(f32[16,1024]{1,0:T(8,128)S(1)} %copy-done.1, f32[16,1024]{1,0:T(8,128)S(1)} %copy-done.2, s32[1,2,2,32,32]{4,3,2,1,0:T(8,128)S(1)} %copy-done.3, f32[1,2,2,32,1024]{4,3,2,1,0:T(8,128)S(1)} %copy-done, f32[544,128]{1,0:T(8,128)S(1)} %collective-permute-done.far_ref, ...), custom_call_target="tpu_custom_call" | custom-call | tf_op jit(solution)/shard_map/smooth/pallas_call | solution.py:467
Async XLA Ops:
  0.6 13.8 %copy-start = (f32[1,2,2,32,1024]{4,3,2,1,0:T(8,128)S(1)}, f32[1,2,2,32,1024]{4,3,2,1,0:T(8,128)}, u32[]{:S(2)}) copy-start(f32[1,2,2,32,1024]{4,3,2,1,0:T(8,128)} %prev_ref.3) | copy-start | bytes 1572868
  0.6 13.8 %copy-start.3 = (s32[1,2,2,32,32]{4,3,2,1,0:T(8,128)S(1)}, s32[1,2,2,32,32]{4,3,2,1,0:T(8,128)}, u32[]{:S(2)}) copy-start(s32[1,2,2,32,32]{4,3,2,1,0:T(8,128)} %mask_ref.3) | copy-start | bytes 49156
  0.7 13.8 %copy-start.2 = (f32[16,1024]{1,0:T(8,128)S(1)}, f32[16,1024]{1,0:T(8,128)}, u32[]{:S(2)}) copy-start(f32[16,1024]{1,0:T(8,128)} %stor_ref.3) | copy-start | bytes 196612
  0.7 13.8 %copy-start.1 = (f32[16,1024]{1,0:T(8,128)S(1)}, f32[16,1024]{1,0:T(8,128)}, u32[]{:S(2)}) copy-start(f32[16,1024]{1,0:T(8,128)} %perm_ref.3) | copy-start | bytes 196612
  2.1 12.3 %collective-permute-start = (f32[544,128]{1,0:T(8,128)S(1)}, f32[544,128]{1,0:T(8,128)S(1)}, u32[]{:S(2)}, u32[]{:S(2)}) collective-permute-start(f32[544,128]{1,0:T(8,128)S(1)} %get-tuple-element.6), channel_id=1, source_target_pairs={{1,2},{2,1},{3,4},{4,3},{5,6},{6,5},{7,8},{8,7},{9,10},{10,9},{11,... | collective-permute-start | bytes 835592 | tf_op jit(solution)/shard_map/ppermute | solution.py:459
  4.9 9.6 %collective-permute-start.3 = (f32[544,128]{1,0:T(8,128)S(1)}, f32[544,128]{1,0:T(8,128)S(1)}, u32[]{:S(2)}, u32[]{:S(2)}) collective-permute-start(f32[544,128]{1,0:T(8,128)S(1)} %get-tuple-element.9), channel_id=1, source_target_pairs={{0,1},{1,0},{2,3},{3,2},{4,5},{5,4},{6,7},{7,6},{8,9},{9,8},{10,11... | collective-permute-start | bytes 835592 | tf_op jit(solution)/shard_map/ppermute | solution.py:459
  5.7 8.7 %collective-permute-start.1 = (f32[64,128]{1,0:T(8,128)S(1)}, f32[64,128]{1,0:T(8,128)S(1)}, u32[]{:S(2)}, u32[]{:S(2)}) collective-permute-start(f32[64,128]{1,0:T(8,128)S(1)} %get-tuple-element.7), channel_id=1, source_target_pairs={{0,2},{1,3},{2,0},{3,1},{4,6},{5,7},{6,4},{7,5},{8,10},{9,11},{10,... | collective-permute-start | bytes 98312 | tf_op jit(solution)/shard_map/ppermute | solution.py:459
  7.3 7.2 %collective-permute-start.2 = (f32[64,128]{1,0:T(8,128)S(1)}, f32[64,128]{1,0:T(8,128)S(1)}, u32[]{:S(2)}, u32[]{:S(2)}) collective-permute-start(f32[64,128]{1,0:T(8,128)S(1)} %get-tuple-element.8), channel_id=1, source_target_pairs={{2,4},{3,5},{4,2},{5,3},{6,8},{7,9},{8,6},{9,7},{10,12},{11,13},{1... | collective-permute-start | bytes 98312 | tf_op jit(solution)/shard_map/ppermute | solution.py:459

commit v5 on v4

--- a/solution.py
+++ b/solution.py
@@ -38,6 +38,7 @@
 THIN_MESSAGE = whole_tiles(EDGE * THIN + 8 - EDGE)
 
 OWN, TWO, SIDE, STRIP = 8, 48, 64, 112
+SPAN = 96
 PADS = (0, 40, 56, 104)
 TILES = tuple((OWN + 8 * k, k) for k in range(4)) + ((TWO, 4),) + tuple((SIDE + 8 * n, (n + 2) % 5) for n in range(5))
 
@@ -176,7 +177,7 @@
 def main_kernel(
     perm_ref, stor_ref, mask_ref, prev_ref, far_ref, far2_ref, near2_ref, near_ref,
     basis_ref, coarse_ref,
-    kbuf, cbuf, wbuf, gbuf, sup, pbuf, qbuf, own_mask, sums,
+    kbuf, cbuf, wbuf, gbuf, sup, pbuf, qbuf, own_mask, sums, zbuf, shift,
 ):
     here = lax.axis_index("gx")
     last = lax.axis_size("gx") - 1
@@ -338,18 +339,31 @@
             return pbuf[by, bz, u, row : row + 8]
         return zero
 
-    def stencil(by, bz, u, row, v, w):
+    def stencil(by, bz, u, row, v, w, beside_z=None):
+        upper, lower = beside_z or (up_z(v), down_z(v))
         near = w[0] * pbuf[by, bz, u, row + 1 : row + 9] + w[1] * pbuf[by, bz, u, row - 1 : row + 7]
         near += w[2] * up_y(v, tile_of(by, bz, u + 1, row)) + w[3] * down_y(v, tile_of(by, bz, u - 1, row))
-        return near + (w[4] * up_z(v) + w[5] * down_z(v))
+        return near + (w[4] * upper + w[5] * lower)
+
+    deep = lax.broadcasted_iota(jnp.int32, (256, 256), 0) % 128
+    wide = lax.broadcasted_iota(jnp.int32, (256, 256), 1)
+    source = jnp.where(wide < 128, wide + 1, wide - 129)
+    shift[...] = jnp.where(deep == source, 1.0, 0.0).astype(jnp.bfloat16)
 
     def relax(by, carry):
+        v = pbuf[by, :, :, OWN : OWN + SPAN].reshape(2 * USED * SPAN, 128)
+        high = v.astype(jnp.bfloat16)
+        low = (v - high.astype(F32)).astype(jnp.bfloat16)
+        parts = jnp.concatenate([high, low], axis=1)
+        zbuf[...] = jnp.dot(parts, shift[...], preferred_element_type=F32).reshape(2, USED, SPAN, 256)
         for u in range(USED):
             weights = weights_of(u + 2 * by)
             for bz in range(2):
                 for row, i in TILES:
                     v = tile_of(by, bz, u, row)
-                    near = stencil(by, bz, u, row, v, weights[i])
+                    at = slice(row - OWN, row - OWN + 8)
+                    beside_z = zbuf[bz, u, at, 0:128], zbuf[bz, u, at, 128:256]
+                    near = stencil(by, bz, u, row, v, weights[i], beside_z)
                     s = sup[by, bz, u, row : row + 8]
                     qbuf[by, bz, u, row : row + 8] = s * jnp.maximum(v * (1.0 / 3.0) + near, 0.0)
         return carry
@@ -370,7 +384,8 @@
                         basis_ref[0, by, bz, row - OWN : row - OWN + 8, lane : lane + 128] = v
 
     for sweep in range(ITERS):
-        lax.fori_loop(0, 2, relax, 0)
+        for by in range(2):
+            relax(by, 0)
         normalise(sweep == ITERS - 1)
 
     for by in range(2):
@@ -482,6 +497,8 @@
             pltpu.VMEM(strips, F32),
             pltpu.VMEM((32, 128), jnp.int32),
             pltpu.VMEM((4, 16, 128), F32),
+            pltpu.VMEM((2, USED, SPAN, 256), F32),
+            pltpu.VMEM((256, 256), jnp.bfloat16),
         ],
         compiler_params=pltpu.CompilerParams(vmem_limit_bytes=32 * 1024 * 1024),
         name="smooth",

time: 19.5 us -> 18.9 us (0.969)
  Pallas kernels: 6.16 us -> 5.57 us
    pallas_call x1, Pallas kernels: 4.71 us -> 4.12 us  [shards(): pl.pallas_call(main_kernel, in_specs=[vmem] * 8, out_specs=[vmem] * 2, ou...]
where the time goes in v5:
time: 18.9 us; the launch traced here: 18.6 us
  starting transfers between devices  7.41 us (39%)
  Pallas kernels  5.57 us (29%)
  waiting for transfers between devices  4.91 us (26%)
  between operations  0.72 us (4%)
    ppermute x4, starting transfers between devices, move(): return lax.ppermute(x, 'gx', [(i, j) for i, j in pairs if 0 <= j < size])  7.41 us
    ppermute x4, waiting for transfers between devices, move(): return lax.ppermute(x, 'gx', [(i, j) for i, j in pairs if 0 <= j < size])  4.91 us
    pallas_call x1, Pallas kernels, shards(): pl.pallas_call(main_kernel, in_specs=[vmem] * 8, out_specs=[vmem] * 2, ou...  4.12 us
    pallas_call x1, Pallas kernels, shards(): pl.pallas_call(pack_kernel, in_specs=[pl.BlockSpec(memory_space=pl.ANY)]...  1.44 us
  transfers between devices with their start and end apart: 4, of which 1 were waited for; matrix products, arithmetic and copies ran while one was open for 0% of the time, Pallas kernels for 0%

profile of v5, /device:TPU:8, one launch (start us, length us, event | category | flops | bytes accessed | tf_op | source)
XLA Modules:
  0.0 18.6 jit_solution(17110401705453098857)
XLA Ops:
  0.6 0.0 copy-start
  0.6 0.0 copy-start.3
  0.7 0.0 copy-start.2
  0.7 0.0 copy-start.1
  0.7 1.4 %pack.1 = (f32[544,128]{1,0:T(8,128)S(1)}, f32[64,128]{1,0:T(8,128)S(1)}, f32[64,128]{1,0:T(8,128)S(1)}, f32[544,128]{1,0:T(8,128)S(1)}) custom-call(f32[16,1024]{1,0:T(8,128)} %perm_ref.3, f32[16,1024]{1,0:T(8,128)} %stor_ref.3, s32[1,2,2,32,32]{4,3,2,1,0:T(8,128)} %mask_ref.3, f32[1,2,2,32,1024]{4,3,2,1,0:T(8,128)} %prev_ref.3), custom_call_target="tpu_custom_call" | custom-call | tf_op jit(solution)/shard_map/pack/pallas_call | solution.py:455
  2.1 2.8 %collective-permute-start = (f32[544,128]{1,0:T(8,128)S(1)}, f32[544,128]{1,0:T(8,128)S(1)}, u32[]{:S(2)}, u32[]{:S(2)}) collective-permute-start(f32[544,128]{1,0:T(8,128)S(1)} %get-tuple-element.6), channel_id=1, source_target_pairs={{1,2},{2,1},{3,4},{4,3},{5,6},{6,5},{7,8},{8,7},{9,10},{10,9},{11,... | collective-permute-start | bytes 835592 | tf_op jit(solution)/shard_map/ppermute | solution.py:474
  4.9 0.9 %collective-permute-start.3 = (f32[544,128]{1,0:T(8,128)S(1)}, f32[544,128]{1,0:T(8,128)S(1)}, u32[]{:S(2)}, u32[]{:S(2)}) collective-permute-start(f32[544,128]{1,0:T(8,128)S(1)} %get-tuple-element.9), channel_id=1, source_target_pairs={{0,1},{1,0},{2,3},{3,2},{4,5},{5,4},{6,7},{7,6},{8,9},{9,8},{10,11... | collective-permute-start | bytes 835592 | tf_op jit(solution)/shard_map/ppermute | solution.py:474
  5.7 1.5 %collective-permute-start.1 = (f32[64,128]{1,0:T(8,128)S(1)}, f32[64,128]{1,0:T(8,128)S(1)}, u32[]{:S(2)}, u32[]{:S(2)}) collective-permute-start(f32[64,128]{1,0:T(8,128)S(1)} %get-tuple-element.7), channel_id=1, source_target_pairs={{0,2},{1,3},{2,0},{3,1},{4,6},{5,7},{6,4},{7,5},{8,10},{9,11},{10,... | collective-permute-start | bytes 98312 | tf_op jit(solution)/shard_map/ppermute | solution.py:474
  7.3 2.3 %collective-permute-start.2 = (f32[64,128]{1,0:T(8,128)S(1)}, f32[64,128]{1,0:T(8,128)S(1)}, u32[]{:S(2)}, u32[]{:S(2)}) collective-permute-start(f32[64,128]{1,0:T(8,128)S(1)} %get-tuple-element.8), channel_id=1, source_target_pairs={{2,4},{3,5},{4,2},{5,3},{6,8},{7,9},{8,6},{9,7},{10,12},{11,13},{1... | collective-permute-start | bytes 98312 | tf_op jit(solution)/shard_map/ppermute | solution.py:474
  9.6 4.9 %collective-permute-done.1.far2_ref = f32[64,128]{1,0:T(8,128)S(1)} collective-permute-done((f32[64,128]{1,0:T(8,128)S(1)}, f32[64,128]{1,0:T(8,128)S(1)}, u32[]{:S(2)}, u32[]{:S(2)}) %collective-permute-start.1) | collective-permute-done | bytes 32800 | tf_op jit(solution)/shard_map/ppermute | solution.py:474
  14.5 0.0 collective-permute-done.2.near2_ref
  14.5 0.0 collective-permute-done.far_ref
  14.5 0.0 collective-permute-done.3.near_ref
  14.5 0.0 copy-done
  14.5 0.0 copy-done.3
  14.5 0.0 copy-done.2
  14.5 0.0 copy-done.1
  14.5 4.1 %smooth.1 = (f32[1,2,2,32,1024]{4,3,2,1,0:T(8,128)}, f32[1,2,2,27]{3,2,1,0:T(2,128)}) custom-call(f32[16,1024]{1,0:T(8,128)S(1)} %copy-done.1, f32[16,1024]{1,0:T(8,128)S(1)} %copy-done.2, s32[1,2,2,32,32]{4,3,2,1,0:T(8,128)S(1)} %copy-done.3, f32[1,2,2,32,1024]{4,3,2,1,0:T(8,128)S(1)} %copy-done, f32[544,128]{1,0:T(8,128)S(1)} %collective-permute-done.far_ref, ...), custom_call_target="tpu_custom_call" | custom-call | tf_op jit(solution)/shard_map/smooth/pallas_call | solution.py:482
Async XLA Ops:
  0.6 13.8 %copy-start = (f32[1,2,2,32,1024]{4,3,2,1,0:T(8,128)S(1)}, f32[1,2,2,32,1024]{4,3,2,1,0:T(8,128)}, u32[]{:S(2)}) copy-start(f32[1,2,2,32,1024]{4,3,2,1,0:T(8,128)} %prev_ref.3) | copy-start | bytes 1572868
  0.6 13.8 %copy-start.3 = (s32[1,2,2,32,32]{4,3,2,1,0:T(8,128)S(1)}, s32[1,2,2,32,32]{4,3,2,1,0:T(8,128)}, u32[]{:S(2)}) copy-start(s32[1,2,2,32,32]{4,3,2,1,0:T(8,128)} %mask_ref.3) | copy-start | bytes 49156
  0.7 13.8 %copy-start.2 = (f32[16,1024]{1,0:T(8,128)S(1)}, f32[16,1024]{1,0:T(8,128)}, u32[]{:S(2)}) copy-start(f32[16,1024]{1,0:T(8,128)} %stor_ref.3) | copy-start | bytes 196612
  0.7 13.8 %copy-start.1 = (f32[16,1024]{1,0:T(8,128)S(1)}, f32[16,1024]{1,0:T(8,128)}, u32[]{:S(2)}) copy-start(f32[16,1024]{1,0:T(8,128)} %perm_ref.3) | copy-start | bytes 196612
  2.1 12.3 %collective-permute-start = (f32[544,128]{1,0:T(8,128)S(1)}, f32[544,128]{1,0:T(8,128)S(1)}, u32[]{:S(2)}, u32[]{:S(2)}) collective-permute-start(f32[544,128]{1,0:T(8,128)S(1)} %get-tuple-element.6), channel_id=1, source_target_pairs={{1,2},{2,1},{3,4},{4,3},{5,6},{6,5},{7,8},{8,7},{9,10},{10,9},{11,... | collective-permute-start | bytes 835592 | tf_op jit(solution)/shard_map/ppermute | solution.py:474
  4.9 9.6 %collective-permute-start.3 = (f32[544,128]{1,0:T(8,128)S(1)}, f32[544,128]{1,0:T(8,128)S(1)}, u32[]{:S(2)}, u32[]{:S(2)}) collective-permute-start(f32[544,128]{1,0:T(8,128)S(1)} %get-tuple-element.9), channel_id=1, source_target_pairs={{0,1},{1,0},{2,3},{3,2},{4,5},{5,4},{6,7},{7,6},{8,9},{9,8},{10,11... | collective-permute-start | bytes 835592 | tf_op jit(solution)/shard_map/ppermute | solution.py:474
  5.7 8.7 %collective-permute-start.1 = (f32[64,128]{1,0:T(8,128)S(1)}, f32[64,128]{1,0:T(8,128)S(1)}, u32[]{:S(2)}, u32[]{:S(2)}) collective-permute-start(f32[64,128]{1,0:T(8,128)S(1)} %get-tuple-element.7), channel_id=1, source_target_pairs={{0,2},{1,3},{2,0},{3,1},{4,6},{5,7},{6,4},{7,5},{8,10},{9,11},{10,... | collective-permute-start | bytes 98312 | tf_op jit(solution)/shard_map/ppermute | solution.py:474
  7.3 7.2 %collective-permute-start.2 = (f32[64,128]{1,0:T(8,128)S(1)}, f32[64,128]{1,0:T(8,128)S(1)}, u32[]{:S(2)}, u32[]{:S(2)}) collective-permute-start(f32[64,128]{1,0:T(8,128)S(1)} %get-tuple-element.8), channel_id=1, source_target_pairs={{2,4},{3,5},{4,2},{5,3},{6,8},{7,9},{8,6},{9,7},{10,12},{11,13},{1... | collective-permute-start | bytes 98312 | tf_op jit(solution)/shard_map/ppermute | solution.py:474

commit v6 on v4

v6 whole, which is shorter than its diff:
```python
import functools

import jax
import jax.numpy as jnp
from jax import lax
from jax.experimental import pallas as pl
from jax.experimental.pallas import tpu as pltpu
from jax.sharding import PartitionSpec as P

ITERS = 2
SUM_FLOOR = 0.5
TINY = 1e-30
F32 = jnp.float32


BLOCKS = 4
LANE_TILES = 8
USED = 6

LEVELS = 16
BULK = 2 * USED * 3
PERM_AT = BULK
STOR_AT = PERM_AT + LANE_TILES
MASK_AT = STOR_AT + LANE_TILES
REST_AT = 8 * (MASK_AT + 2)
HALF = USED // 2
CELLS = 2 * (HALF + USED)
REST = CELLS + 2 * LANE_TILES + 1
THIN = CELLS + 1
EDGE = 3


def whole_tiles(rows):
    return 8 * ((rows + 7) // 8)


MESSAGE = whole_tiles(REST_AT + EDGE * REST + 8 - EDGE)
THIN_MESSAGE = whole_tiles(EDGE * THIN + 8 - EDGE)

OWN, TWO, SIDE, STRIP = 8, 48, 64, 112
SPAN = 96
PADS = (0, 40, 56, 104)
TILES = tuple((OWN + 8 * k, k) for k in range(4)) + ((TWO, 4),) + tuple((SIDE + 8 * n, (n + 2) % 5) for n in range(5))


def box_tile(by, u):
    return u + 2 * (1 - by)


def lanes_of(tile):
    return pl.ds(128 * tile, 128)


def height_of_lane():
    return lax.rem(lax.broadcasted_iota(jnp.int32, (8, 128), 1), 32)


def share(first, second):
    heights = height_of_lane()
    first_up, second_up = pltpu.roll(first, LEVELS, 1), pltpu.roll(second, LEVELS, 1)
    return jnp.where(heights < LEVELS, first, second_up), first_up, second_up


def unshare(common, first_rest, second_rest):
    heights = height_of_lane()
    first = jnp.where(heights < LEVELS, common, pltpu.roll(first_rest, 128 - LEVELS, 1))
    second = pltpu.roll(jnp.where(heights >= LEVELS, common, second_rest), 128 - LEVELS, 1)
    return first, second


def put_edges(out_ref, at, pieces, rightward):
    for n, tile in enumerate(pieces):
        tile = jnp.where(rightward == 1, pltpu.roll(tile, EDGE, 0), tile)
        out_ref[at + EDGE * n : at + EDGE * (n + 1)] = tile[:EDGE]


def cells(tile):
    low = height_of_lane() < 2
    pieces = []
    for by in range(2):
        common, rests = [], [None] * USED
        for u in range(HALF):
            both, rests[u], rests[u + HALF] = share(tile(by, 0, u), tile(by, 0, u + HALF))
            common.append(both)
        pieces += common + [jnp.where(low, rests[u], tile(by, 1, u)) for u in range(USED)]
    return pieces


def put_message(out_ref, rest_ref, rest_at, leftward, prev_tile, perm_tile, stor_tile, mask_tile):
    low = height_of_lane() < 2
    def put_tile(n, tile):
        out_ref[8 * n : 8 * n + 8] = tile

    for by in range(2):
        for u in range(USED):
            common, first_up, second_up = share(prev_tile(0, by, 0, u), prev_tile(1, by, 0, u))
            at = 24 * (by * USED + u)
            out_ref[at : at + 8] = common
            out_ref[at + 8 : at + 16] = jnp.where(low, first_up, prev_tile(0, by, 1, u))
            out_ref[at + 16 : at + 24] = jnp.where(low, second_up, prev_tile(1, by, 1, u))
    for n in range(2):
        put_tile(MASK_AT + n, mask_tile(n))
    for t in range(LANE_TILES):
        put_tile(PERM_AT + t, perm_tile(1 - leftward, t))
        put_tile(STOR_AT + t, stor_tile(1 - leftward, t))
    pieces = cells(functools.partial(prev_tile, 2))
    pieces += [perm_tile(leftward, t) for t in range(LANE_TILES)]
    pieces += [stor_tile(leftward, t) for t in range(LANE_TILES)]
    pieces += [mask_tile(2)]
    put_edges(rest_ref, rest_at, pieces, 1 - leftward)
    tail, end = rest_at + EDGE * REST, rest_at + MESSAGE - REST_AT
    rest_ref[tail:end] = jnp.zeros((end - tail, 128), F32)


def eight(tile):
    return pl.ds(pl.multiple_of(8 * tile, 8), 8)


def put_thin(out_ref, leftward, prev_tile, mask_tile):
    edge = 3 - 3 * leftward
    pieces = cells(functools.partial(prev_tile, edge)) + [mask_tile(edge)]
    put_edges(out_ref, 0, pieces, 1 - leftward)
    tail = EDGE * THIN
    out_ref[tail:THIN_MESSAGE] = jnp.zeros((THIN_MESSAGE - tail, 128), F32)


def pack_kernel(
    perm_ref, stor_ref, mask_ref, prev_ref,
    far_ref, far2_ref, near2_ref, near_ref, rest_ref, perm, stor, mask_buf, prev, mask, sems,
):
    odd = lax.rem(lax.axis_index("gx"), 2)
    odd_chip = lax.rem(lax.axis_index("gx") // 2, 2)
    copies = []
    for by in range(2):
        for bz in range(2):
            blk = 2 * by + bz
            lanes = pl.ds(128 * box_tile(by, 0), 128 * USED)
            copies.append((prev_ref.at[0, by, bz, :, lanes], prev.at[blk]))
            copies.append((mask_ref.at[0, by, bz], mask.at[blk]))
    copies += [(perm_ref, perm), (stor_ref, stor)]
    copies = [pltpu.make_async_copy(src, dst, sems.at[n]) for n, (src, dst) in enumerate(copies)]
    for copy in copies:
        copy.start()
    for copy in copies:
        copy.wait()
    mask_buf[...] = jnp.concatenate([mask[blk] for blk in range(BLOCKS)], axis=1).astype(F32)

    def prev_tile(tile, by, bz, u):
        return prev[2 * by + bz, eight(tile), lanes_of(u)]

    def mask_tile(tile):
        return mask_buf[eight(tile), lanes_of(0)]

    def message(out_ref, rest_ref, rest_at, leftward):
        def tile_at(n):
            return jnp.where(leftward == 1, n, (2, 3, 1)[n])

        put_message(
            out_ref,
            rest_ref,
            rest_at,
            leftward,
            lambda n, by, bz, u: prev_tile(tile_at(n), by, bz, u),
            lambda n, t: perm[eight(n), lanes_of(t)],
            lambda n, t: stor[eight(n), lanes_of(t)],
            lambda n: mask_tile(tile_at(n)),
        )

    message(far_ref, far_ref, REST_AT, 1 - odd)
    put_thin(far2_ref, odd_chip, prev_tile, mask_tile)
    put_thin(near2_ref, 1 - odd_chip, prev_tile, mask_tile)
    message(near_ref, rest_ref, 0, odd)


def tile_rows(n):
    return slice(8 * n, 8 * n + 8)


def lane_index():
    return lax.broadcasted_iota(jnp.int32, (8, 128), 1)


def zeros():
    return jnp.zeros((8, 128), F32)


def up_y(here, after):
    return pltpu.roll(jnp.where(lane_index() >= 32, here, after), 96, 1)


def down_y(here, before):
    return pltpu.roll(jnp.where(lane_index() < 96, here, before), 32, 1)


def up_z(v):
    return pltpu.roll(v, 127, 1)


def down_z(v):
    return pltpu.roll(v, 1, 1)


def inverse(v):
    first = pl.reciprocal(v, approx=True)
    return first * (2.0 - v * first)


def harmonic(a, b):
    return 2.0 * (a * b) * inverse(jnp.maximum(a + b, TINY))


def edges(ref, at, index, left):
    start = at + EDGE * index - (8 - EDGE) * left
    tile = ref[max(start, 0) : max(start, 0) + 8]
    return pltpu.roll(tile, -start, 0) if start < 0 else tile


def fill_coefficients(rings, buf, own_ref, bulk, rest, sides):
    low = lax.broadcasted_iota(jnp.int32, (8, 128), 0) < 4
    for t in range(LANE_TILES):
        for i in rings:
            if i in (1, 2):
                tile = own_ref[tile_rows(i - 1), lanes_of(t)]
            elif i < 4:
                tile = sides[i // 3][0][tile_rows(bulk + t)]
            else:
                ends = [edges(*ref[1:], rest + t, n == 0) if ref is not None else None for n, ref in enumerate(sides)]
                tile = ends[0] if ends[1] is None else ends[1] if ends[0] is None else jnp.where(low, ends[1], ends[0])
            buf[t, tile_rows(i)] = tile


def fill_weights(rings, kbuf, cbuf, wbuf, gbuf):
    rows = lax.broadcasted_iota(jnp.int32, (8, 128), 0)
    heights = height_of_lane()

    def k_of(t, i):
        return kbuf[t, tile_rows(i % 5)] if 0 <= t < LANE_TILES else zeros()

    for t in range(LANE_TILES):
        for i in rings:
            k = k_of(t, i)
            east = jnp.where(rows < 7, pltpu.roll(k, 7, 0), pltpu.roll(k_of(t, i + 1), 7, 0))
            west = jnp.where(rows > 0, pltpu.roll(k, 1, 0), pltpu.roll(k_of(t, i + 4), 1, 0))
            faces = [
                harmonic(k, east),
                harmonic(k, west),
                harmonic(k, up_y(k, k_of(t + 1, i))),
                harmonic(k, down_y(k, k_of(t - 1, i))),
                jnp.where(heights < 31, harmonic(k, up_z(k)), 0.0),
                jnp.where(heights > 0, harmonic(k, down_z(k)), 0.0),
            ]
            diag = functools.reduce(lambda a, b: a + b, faces, cbuf[t, tile_rows(i)])
            scale = (2.0 / 3.0) * inverse(jnp.maximum(diag, TINY))
            for d, face in enumerate(faces):
                wbuf[t, d, tile_rows(i)] = face * scale
            gbuf[t, tile_rows(i)] = 1.5 * diag


def core_bits():
    lanes = lane_index()
    j = lax.rem(lanes, 32)
    return jnp.where((j >= 8) & (j < 24), jnp.where(lax.rem(lanes // 32, 2) == 0, 0xFFFF, 0xFFFF00), 0)


def support_of(bits, by, bz, u):
    offset = height_of_lane() - 8 * bz
    valid = (offset >= 0) & (offset < (18, 24)[bz])
    lane_bit = jnp.where(valid, jnp.left_shift(1, jnp.clip(offset, 0, 23)), 0)
    index = 32 * (2 * by + bz) + 4 * u + 8 * (1 - by) + lane_index() // 32
    spread = jnp.take_along_axis(bits, index, axis=1, mode="promise_in_bounds")
    return jnp.where((spread & lane_bit) != 0, 1.0, 0.0)


def message_cells(ref):
    found = [{}, {}]
    for by in range(2):
        for u in range(USED):
            at = 3 * (by * USED + u)
            common, first_top, second_top = [ref[tile_rows(at + n)] for n in range(3)]
            found[0][by, 0, u], found[1][by, 0, u] = unshare(common, first_top, second_top)
            found[0][by, 1, u], found[1][by, 1, u] = first_top, second_top
    return found


def edge_cells(fetch):
    found = {}
    for by in range(2):
        base = by * (HALF + USED)
        for u in range(HALF):
            tops = [fetch(base + HALF + u), fetch(base + HALF + u + HALF)]
            found[by, 0, u], found[by, 0, u + HALF] = unshare(fetch(base + u), *tops)
            found[by, 1, u], found[by, 1, u + HALF] = tops
    return found


def put_cells(pbuf, sup, row, found, bits):
    for (by, bz, u), tile in found.items():
        s = support_of(bits, by, bz, u)
        sup[by, bz, u, row : row + 8] = s
        pbuf[by, bz, u, row : row + 8] = s * tile


def side_row(ring):
    return SIDE + 8 * ((ring - 2) % 5)


def tile_of(pbuf, by, bz, u, row):
    return pbuf[by, bz, u, row : row + 8] if 0 <= u < USED else zeros()


def stencil(pbuf, by, bz, u, row, v, w, beside_z=None):
    upper, lower = beside_z or (up_z(v), down_z(v))
    near = w[0] * pbuf[by, bz, u, row + 1 : row + 9] + w[1] * pbuf[by, bz, u, row - 1 : row + 7]
    near += w[2] * up_y(v, tile_of(pbuf, by, bz, u + 1, row)) + w[3] * down_y(v, tile_of(pbuf, by, bz, u - 1, row))
    return near + (w[4] * upper + w[5] * lower)


def relax(pbuf, qbuf, sup, wbuf, by, tiles, zbuf=None, shift=None, spans=()):
    if spans:
        count = sum(b - a for a, b in spans)
        v = jnp.concatenate([pbuf[by, :, :, a:b] for a, b in spans], axis=2).reshape(2 * USED * count, 128)
        high = v.astype(jnp.bfloat16)
        low = (v - high.astype(F32)).astype(jnp.bfloat16)
        parts = jnp.concatenate([high, low], axis=1)
        beside = jnp.dot(parts, shift[...], preferred_element_type=F32)
        zbuf[:, :, :count] = beside.reshape(2, USED, count, 256)
    places = {}
    for a, b in spans:
        for row in range(a, b, 8):
            places[row] = 8 * len(places)
    for u in range(USED):
        for bz in range(2):
            for row, i in tiles:
                v = tile_of(pbuf, by, bz, u, row)
                w = [wbuf[u + 2 * by, d, tile_rows(i)] for d in range(6)]
                beside_z = None
                if spans:
                    at = slice(places[row], places[row] + 8)
                    beside_z = zbuf[bz, u, at, 0:128], zbuf[bz, u, at, 128:256]
                near = stencil(pbuf, by, bz, u, row, v, w, beside_z)
                s = sup[by, bz, u, row : row + 8]
                qbuf[by, bz, u, row : row + 8] = s * jnp.maximum(v * (1.0 / 3.0) + near, 0.0)


def normalise(qbuf, pbuf, tiles, basis_ref=None):
    for t in range(LANE_TILES):
        blocks = [(by, bz, t - 2 * by) for by in range(2) for bz in range(2) if 0 <= t - 2 * by < USED]
        for i in sorted({ring for _, ring in tiles}):
            at = [(b, row) for b in blocks for row, ring in tiles if ring == i]
            kept = [qbuf[by, bz, u, row : row + 8] for (by, bz, u), row in at]
            total = functools.reduce(lambda a, b: a + b, kept)
            scale = inverse(jnp.maximum(total, SUM_FLOOR))
            for ((by, bz, u), row), v in zip(at, kept):
                v = v * scale
                pbuf[by, bz, u, row : row + 8] = v
                if basis_ref is not None and row < TWO:
                    basis_ref[0, by, bz, row - OWN : row - OWN + 8, lanes_of(box_tile(by, u))] = v


def halves(odd):
    return ((1, 0), (2, 3)) if odd else ((2, 3), (1, 0))


def by_parity(body):
    parity = lax.rem(lax.axis_index("gx"), 2)
    for odd in range(2):
        pl.when(parity == odd)(functools.partial(body, odd))


def begin_kernel(perm_ref, stor_ref, mask_ref, prev_ref, near_ref, rest_ref, first, second, sup, wbuf, gbuf, shift, kbuf, cbuf, qbuf):
    here = lax.axis_index("gx")
    last = lax.axis_size("gx") - 1
    deep = lax.broadcasted_iota(jnp.int32, (256, 256), 0) % 128
    wide = lax.broadcasted_iota(jnp.int32, (256, 256), 1)
    source = jnp.where(wide < 128, wide + 1, wide - 129)
    shift[...] = jnp.where(deep == source, 1.0, 0.0).astype(jnp.bfloat16)

    own_bits = [mask_ref[tile_rows(k)].astype(jnp.int32) for k in range(4)]
    own_bits[0] = jnp.where(here == 0, 0, own_bits[0])
    own_bits[1] |= core_bits()
    own_bits[2] |= core_bits()
    own_bits[3] = jnp.where(here == last, 0, own_bits[3])
    for by in range(2):
        for bz in range(2):
            for u in range(USED):
                for row in PADS:
                    first[by, bz, u, row : row + 8] = zeros()
                    second[by, bz, u, row : row + 8] = zeros()
    for k in range(4):
        found = {
            (by, bz, u): prev_ref[2 * by + bz, tile_rows(k), lanes_of(u)]
            for by in range(2)
            for bz in range(2)
            for u in range(USED)
        }
        put_cells(first, sup, OWN + 8 * k, found, own_bits[k])

    def body(odd):
        (inner, outer), _ = halves(odd)
        near = (near_ref, rest_ref, 0)
        sides = (near, None) if odd else (None, near)
        fill_coefficients((1, 2, outer, 4), kbuf, perm_ref, PERM_AT, CELLS, sides)
        fill_coefficients((inner, outer), cbuf, stor_ref, STOR_AT, CELLS + LANE_TILES, sides)
        fill_weights((inner, outer), kbuf, cbuf, wbuf, gbuf)
        found = message_cells(near_ref)
        for n in range(2):
            ring = n if odd else n + 2
            bits = near_ref[tile_rows(MASK_AT + n)].astype(jnp.int32)
            put_cells(first, sup, side_row(ring), found[n], bits | core_bits() if ring in (0, 3) else bits)

        def rest(index):
            return edges(rest_ref, 0, index, odd == 1)

        put_cells(first, sup, side_row(4), edge_cells(rest), rest(REST - 1).astype(jnp.int32) | core_bits())
        tiles = [(row, i) for row, i in TILES if i in (inner, outer)]
        for by in range(2):
            relax(first, qbuf, sup, wbuf, by, tiles)
        normalise(qbuf, second, tiles)

    by_parity(body)


def finish_kernel(
    far_ref, far2_ref, near2_ref, near_ref, rest_ref, perm_ref, stor_ref, shift, _first, _second, _sup, _wbuf, _gbuf,
    basis_ref, coarse_ref, first, second, sup, wbuf, gbuf,
    kbuf, cbuf, qbuf, sums, zbuf,
):
    here = lax.axis_index("gx")
    odd_chip = lax.rem(here // 2, 2) == 1
    rows = lax.broadcasted_iota(jnp.int32, (8, 128), 0)
    low_rows = rows < 4

    def thin(index):
        right = jnp.where(odd_chip, edges(near2_ref, 0, index, False), edges(far2_ref, 0, index, False))
        left = jnp.where(odd_chip, edges(far2_ref, 0, index, True), edges(near2_ref, 0, index, True))
        return jnp.where(low_rows, right, left)

    def body(odd):
        (_, near_outer), (inner, outer) = halves(odd)
        near, far = (near_ref, rest_ref, 0), (far_ref, far_ref, REST_AT)
        sides = (near, far) if odd else (far, near)
        fill_coefficients((1, 2, near_outer, outer, 4), kbuf, perm_ref, PERM_AT, CELLS, sides)
        fill_coefficients((inner, outer, 4), cbuf, stor_ref, STOR_AT, CELLS + LANE_TILES, sides)
        fill_weights((inner, outer, 4), kbuf, cbuf, wbuf, gbuf)
        found = message_cells(far_ref)
        for n in range(2):
            ring = n + 2 if odd else n
            bits = far_ref[tile_rows(MASK_AT + n)].astype(jnp.int32)
            put_cells(first, sup, side_row(ring), found[n], bits | core_bits() if ring in (0, 3) else bits)

        def rest(index):
            return jnp.where(low_rows, edges(*sides[1][1:], index, False), edges(*sides[0][1:], index, True))

        put_cells(first, sup, side_row(4), edge_cells(rest), rest(REST - 1).astype(jnp.int32) | core_bits())
        put_cells(first, sup, TWO, edge_cells(thin), thin(THIN - 1).astype(jnp.int32))
        tiles = [(row, i) for row, i in TILES if i in (inner, outer, 4)]
        own = OWN + 16 * odd
        side = SIDE + 16 * (1 - odd)
        spans = ((own, own + 16), (TWO, TWO + 8), (side, side + 24))
        for by in range(2):
            relax(first, qbuf, sup, wbuf, by, tiles, zbuf, shift, spans)
        normalise(qbuf, second, tiles)

    by_parity(body)

    pbuf, other = second, first
    for sweep in range(1, ITERS):
        for by in range(2):
            relax(pbuf, qbuf, sup, wbuf, by, TILES, zbuf, shift, ((OWN, OWN + SPAN),))
        normalise(qbuf, other, TILES, basis_ref if sweep == ITERS - 1 else None)
        pbuf, other = other, pbuf

    for by in range(2):
        for bz in range(2):
            at = 0 if by == 0 else 768
            basis_ref[0, by, bz, :, at : at + 256] = jnp.zeros((32, 256), F32)

    for by in range(2):
        acc = [[] for _ in range(24)]
        for t in range(by, by + USED + 1):
            u = t - 2 * by
            weights = [[wbuf[t, d, tile_rows(i)] for d in range(6)] for i in range(5)]
            scale = [gbuf[t, 8 * i : 8 * i + 8] for i in range(5)]
            images = []
            for bz in range(2):
                image = []
                for k in range(4):
                    row = OWN + 8 * k
                    if 0 <= u < USED:
                        v = tile_of(pbuf, by, bz, u, row)
                        image.append(scale[k] * (v * (2.0 / 3.0) - stencil(pbuf, by, bz, u, row, v, weights[k])))
                    elif u < 0:
                        image.append(-scale[k] * (weights[k][2] * up_y(zeros(), tile_of(pbuf, by, bz, u + 1, row))))
                    else:
                        image.append(-scale[k] * (weights[k][3] * down_y(zeros(), tile_of(pbuf, by, bz, u - 1, row))))
                before = beyond = None
                if 0 <= u < USED:
                    edge = pbuf[by, bz, u, OWN + 31 : OWN + 39]
                    beyond = -scale[4] * (weights[4][1] * edge)
                    edge = pbuf[by, bz, u, OWN - 7 : OWN + 1]
                    before = -scale[4] * (weights[4][0] * edge)
                images.append((image, before, beyond))
            for partner in range(BLOCKS):
                by2, bz2 = divmod(partner, 2)
                u2 = t - 2 * by2
                if not 0 <= u2 < USED:
                    continue
                own = [tile_of(pbuf, by2, bz2, u2, OWN + 8 * k) for k in range(4)]
                side = [tile_of(pbuf, by2, bz2, u2, SIDE + 8 * k) for k in range(5)]
                for bz in range(2):
                    image, before, beyond = images[bz]
                    at = bz * 12 + partner
                    acc[at] += [image[0] * side[3], image[1] * side[4]]
                    acc[at + 4] += [image[k] * own[k] for k in range(4)]
                    acc[at + 8] += [image[2] * side[0], image[3] * side[1]]
                    if before is not None:
                        acc[at] += [before * side[2]]
                        acc[at + 8] += [beyond * side[2]]
            acc = [[functools.reduce(lambda a, b: a + b, terms)] if terms else [] for terms in acc]
        for bz in range(2):
            for n in range(12):
                sums[2 * by + bz, n] = jnp.sum(acc[bz * 12 + n][0], axis=0)

    entry = lax.broadcasted_iota(jnp.int32, (16, 128), 0)
    column = lax.broadcasted_iota(jnp.int32, (16, 128), 1)
    for by in range(2):
        for bz in range(2):
            values = jnp.sum(sums[2 * by + bz], axis=1, keepdims=True)
            target = 9 * (entry // 4) + 3 * (lax.rem(entry // 2, 2) - by + 1) + (lax.rem(entry, 2) - bz + 1)
            placed = jnp.where((column == target) & (entry < 12), values, 0.0)
            coarse_ref[0, by, bz, :] = jnp.sum(placed, axis=0)[:27]


def shards(permeability, storage, support_mask, prev_basis):
    vmem = pl.BlockSpec(memory_space=pltpu.VMEM)
    far, far2, near2, near, rest, *own = pl.pallas_call(
        pack_kernel,
        in_specs=[pl.BlockSpec(memory_space=pl.ANY)] * 4,
        out_specs=[vmem] * 9,
        out_shape=[
            *[pltpu.VMEM((n, 128), F32) for n in (MESSAGE, THIN_MESSAGE, THIN_MESSAGE, REST_AT, MESSAGE - REST_AT)],
            pltpu.VMEM(permeability.shape, F32),
            pltpu.VMEM(storage.shape, F32),
            pltpu.VMEM((32, 128), F32),
            pltpu.VMEM((BLOCKS, 32, 128 * USED), F32),
        ],
        scratch_shapes=[
            pltpu.VMEM((BLOCKS, 32, 32), jnp.int32),
            pltpu.SemaphoreType.DMA((2 * BLOCKS + 2,)),
        ],
        name="pack",
    )(permeability, storage, support_mask, prev_basis)
    size = lax.axis_size("gx")

    def move(x, step, width):
        pairs = [(i, i + (-step if i // width % 2 else step)) for i in range(size)]
        return lax.ppermute(x, "gx", [(i, j) for i, j in pairs if 0 <= j < size])

    far = move(far, -1, 1)
    far2 = move(far2, 2, 2)
    near2 = move(near2, -2, 2)
    near = move(near, 1, 1)
    rest = move(rest, 1, 1)

    strips = (2, 2, USED, STRIP, 128)
    state = [
        pltpu.VMEM(strips, F32),
        pltpu.VMEM(strips, F32),
        pltpu.VMEM(strips, F32),
        pltpu.VMEM((LANE_TILES, 6, 40, 128), F32),
        pltpu.VMEM((LANE_TILES, 40, 128), F32),
    ]
    scratch = [
        pltpu.VMEM((LANE_TILES, 40, 128), F32),
        pltpu.VMEM((LANE_TILES, 40, 128), F32),
        pltpu.VMEM(strips, F32),
    ]
    limit = pltpu.CompilerParams(vmem_limit_bytes=32 * 1024 * 1024)
    *filled, shift = pl.pallas_call(
        begin_kernel,
        in_specs=[vmem] * 6,
        out_specs=[vmem] * 6,
        out_shape=[*state, pltpu.VMEM((256, 256), jnp.bfloat16)],
        scratch_shapes=scratch,
        compiler_params=limit,
        cost_estimate=pl.CostEstimate(flops=0, bytes_accessed=0, transcendentals=0),
        name="begin",
    )(*own, near, rest)
    return pl.pallas_call(
        finish_kernel,
        in_specs=[vmem] * 13,
        out_specs=[vmem] * 7,
        out_shape=[
            jax.ShapeDtypeStruct(prev_basis.shape, F32),
            jax.ShapeDtypeStruct((*prev_basis.shape[:3], 27), F32),
            *state,
        ],
        input_output_aliases={8 + n: 2 + n for n in range(5)},
        scratch_shapes=[
            *scratch,
            pltpu.VMEM((4, 16, 128), F32),
            pltpu.VMEM((2, USED, SPAN, 256), F32),
        ],
        compiler_params=limit,
        name="finish",
    )(far, far2, near2, near, rest, *own[:2], shift, *filled)[:2]


def solution(mesh):
    placed = (
        P(("groups", "gx"), None),
        P(("groups", "gx"), None),
        P(("groups", "gx"), None, None, None, None),
        P(("groups", "gx"), None, None, None, None),
    )
    return jax.shard_map(
        shards,
        mesh=mesh,
        in_specs=placed,
        out_specs=(
            P(("groups", "gx"), None, None, None, None),
            P(("groups", "gx"), None, None, None),
        ),
        check_vma=False,
    )
```

time: 19.5 us -> 18.2 us (0.933)
  waiting for transfers between devices: 4.91 us -> 3.61 us
    ppermute x4 -> x5, waiting for transfers between devices: 4.91 us -> 3.61 us  [move(): return lax.ppermute(x, 'gx', [(i, j) for i, j in pairs if 0 <= j < size])]
    ppermute x4 -> x5, starting transfers between devices: 7.41 us -> 7.49 us  [move(): return lax.ppermute(x, 'gx', [(i, j) for i, j in pairs if 0 <= j < size])]
    pallas_call x1 -> x2, Pallas kernels: 4.71 us -> 4.76 us  [the longest x1 3.57 us: shards(): pl.pallas_call(finish_kernel, in_specs=[vmem] * 13, out_specs=[vmem] * 7,...]
  transfers between devices with their start and end apart: 4 -> 5, of which waited for: 1 -> 1; matrix products, arithmetic and copies ran while one was open for 0% -> 0% of each run, Pallas kernels for 0% -> 7%
where the time goes in v6:
time: 18.2 us; the launch traced here: 18 us
  starting transfers between devices  7.49 us (41%)
  Pallas kernels  6.17 us (34%)
  waiting for transfers between devices  3.61 us (20%)
  between operations  0.68 us (4%)
    ppermute x5, starting transfers between devices, move(): return lax.ppermute(x, 'gx', [(i, j) for i, j in pairs if 0 <= j < size])  7.49 us
    ppermute x5, waiting for transfers between devices, move(): return lax.ppermute(x, 'gx', [(i, j) for i, j in pairs if 0 <= j < size])  3.61 us
    pallas_call x1, Pallas kernels, shards(): pl.pallas_call(finish_kernel, in_specs=[vmem] * 13, out_specs=[vmem] * 7,...  3.57 us
    pallas_call x1, Pallas kernels, shards(): pl.pallas_call(pack_kernel, in_specs=[pl.BlockSpec(memory_space=pl.ANY)]...  1.41 us
    pallas_call x1, Pallas kernels, shards(): pl.pallas_call(begin_kernel, in_specs=[vmem] * 6, out_specs=[vmem] * 6, o...  1.2 us
  transfers between devices with their start and end apart: 5, of which 1 were waited for; matrix products, arithmetic and copies ran while one was open for 0% of the time, Pallas kernels for 7%

profile of v6, /device:TPU:8, one launch (start us, length us, event | category | flops | bytes accessed | tf_op | source)
XLA Modules:
  0.0 18.0 jit_solution(6599071426509234049)
XLA Ops:
  0.6 1.4 %pack.1 = (f32[544,128]{1,0:T(8,128)S(1)}, f32[64,128]{1,0:T(8,128)S(1)}, f32[64,128]{1,0:T(8,128)S(1)}, f32[432,128]{1,0:T(8,128)S(1)}, f32[112,128]{1,0:T(8,12...) custom-call(f32[16,1024]{1,0:T(8,128)} %perm_ref.1, ...), custom_call_target="tpu_custom_call" | custom-call | tf_op jit(solution)/shard_map/pack/pallas_call | solution.py:536
  2.0 2.8 %collective-permute-start = (f32[544,128]{1,0:T(8,128)S(1)}, f32[544,128]{1,0:T(8,128)S(1)}, u32[]{:S(2)}, u32[]{:S(2)}) collective-permute-start(f32[544,128]{1,0:T(8,128)S(1)} %get-tuple-element.19), channel_id=1, source_target_pairs={{1,2},{2,1},{3,4},{4,3},{5,6},{6,5},{7,8},{8,7},{9,10},{10,9},{11,... | collective-permute-start | bytes 835592 | tf_op jit(solution)/shard_map/ppermute | solution.py:557
  4.8 0.9 %collective-permute-start.3 = (f32[432,128]{1,0:T(8,128)S(1)}, f32[432,128]{1,0:T(8,128)S(1)}, u32[]{:S(2)}, u32[]{:S(2)}) collective-permute-start(f32[432,128]{1,0:T(8,128)S(1)} %get-tuple-element.22), channel_id=1, source_target_pairs={{0,1},{1,0},{2,3},{3,2},{4,5},{5,4},{6,7},{7,6},{8,9},{9,8},{10,11... | collective-permute-start | bytes 663560 | tf_op jit(solution)/shard_map/ppermute | solution.py:557
  5.7 0.1 collective-permute-start.4
  5.7 1.5 %collective-permute-start.1 = (f32[64,128]{1,0:T(8,128)S(1)}, f32[64,128]{1,0:T(8,128)S(1)}, u32[]{:S(2)}, u32[]{:S(2)}) collective-permute-start(f32[64,128]{1,0:T(8,128)S(1)} %get-tuple-element.20), channel_id=1, source_target_pairs={{0,2},{1,3},{2,0},{3,1},{4,6},{5,7},{6,4},{7,5},{8,10},{9,11},{10,... | collective-permute-start | bytes 98312 | tf_op jit(solution)/shard_map/ppermute | solution.py:557
  7.3 2.3 %collective-permute-start.2 = (f32[64,128]{1,0:T(8,128)S(1)}, f32[64,128]{1,0:T(8,128)S(1)}, u32[]{:S(2)}, u32[]{:S(2)}) collective-permute-start(f32[64,128]{1,0:T(8,128)S(1)} %get-tuple-element.21), channel_id=1, source_target_pairs={{2,4},{3,5},{4,2},{5,3},{6,8},{7,9},{8,6},{9,7},{10,12},{11,13},{1... | collective-permute-start | bytes 98312 | tf_op jit(solution)/shard_map/ppermute | solution.py:557
  9.6 0.0 collective-permute-done.4.rest_ref
  9.6 0.0 collective-permute-done.3.near_ref
  9.6 1.2 %begin.1 = (f32[2,2,6,112,128]{4,3,2,1,0:T(8,128)S(1)}, f32[2,2,6,112,128]{4,3,2,1,0:T(8,128)S(1)}, f32[2,2,6,112,128]{4,3,2,1,0:T(8,128)S(1)}, f32[8,6,40,128]{...) custom-call(f32[16,1024]{1,0:T(8,128)S(1)} %get-tuple-element.24.perm_ref, ...), custom_call_target="tpu_custom_call" | custom-call | tf_op jit(solution)/shard_map/begin/pallas_call | solution.py:579
  10.8 3.6 %collective-permute-done.1.far2_ref = f32[64,128]{1,0:T(8,128)S(1)} collective-permute-done((f32[64,128]{1,0:T(8,128)S(1)}, f32[64,128]{1,0:T(8,128)S(1)}, u32[]{:S(2)}, u32[]{:S(2)}) %collective-permute-start.1) | collective-permute-done | bytes 32800 | tf_op jit(solution)/shard_map/ppermute | solution.py:557
  14.4 0.0 collective-permute-done.2.near2_ref
  14.4 0.0 collective-permute-done.far_ref
  14.4 3.6 %finish.1 = (f32[1,2,2,32,1024]{4,3,2,1,0:T(8,128)}, f32[1,2,2,27]{3,2,1,0:T(2,128)}, f32[2,2,6,112,128]{4,3,2,1,0:T(8,128)S(1)}, f32[2,2,6,112,128]{4,3,2,1,0:T...) custom-call(f32[544,128]{1,0:T(8,128)S(1)} %collective-permute-done., ...), custom_call_target="tpu_custom_call", output_to_operand_aliasing={{2}: (8, {}), {3}: (9, {}), {4}: (10, {}), {5}: (11, {}), {... | custom-call | tf_op jit(solution)/shard_map/finish/pallas_call | solution.py:589
Async XLA Ops:
  2.0 12.3 %collective-permute-start = (f32[544,128]{1,0:T(8,128)S(1)}, f32[544,128]{1,0:T(8,128)S(1)}, u32[]{:S(2)}, u32[]{:S(2)}) collective-permute-start(f32[544,128]{1,0:T(8,128)S(1)} %get-tuple-element.19), channel_id=1, source_target_pairs={{1,2},{2,1},{3,4},{4,3},{5,6},{6,5},{7,8},{8,7},{9,10},{10,9},{11,... | collective-permute-start | bytes 835592 | tf_op jit(solution)/shard_map/ppermute | solution.py:557
  4.8 4.8 %collective-permute-start.3 = (f32[432,128]{1,0:T(8,128)S(1)}, f32[432,128]{1,0:T(8,128)S(1)}, u32[]{:S(2)}, u32[]{:S(2)}) collective-permute-start(f32[432,128]{1,0:T(8,128)S(1)} %get-tuple-element.22), channel_id=1, source_target_pairs={{0,1},{1,0},{2,3},{3,2},{4,5},{5,4},{6,7},{7,6},{8,9},{9,8},{10,11... | collective-permute-start | bytes 663560 | tf_op jit(solution)/shard_map/ppermute | solution.py:557
  5.7 3.9 %collective-permute-start.4 = (f32[112,128]{1,0:T(8,128)S(1)}, f32[112,128]{1,0:T(8,128)S(1)}, u32[]{:S(2)}, u32[]{:S(2)}) collective-permute-start(f32[112,128]{1,0:T(8,128)S(1)} %get-tuple-element.23), channel_id=1, source_target_pairs={{0,1},{1,0},{2,3},{3,2},{4,5},{5,4},{6,7},{7,6},{8,9},{9,8},{10,11... | collective-permute-start | bytes 172040 | tf_op jit(solution)/shard_map/ppermute | solution.py:557
  5.7 8.6 %collective-permute-start.1 = (f32[64,128]{1,0:T(8,128)S(1)}, f32[64,128]{1,0:T(8,128)S(1)}, u32[]{:S(2)}, u32[]{:S(2)}) collective-permute-start(f32[64,128]{1,0:T(8,128)S(1)} %get-tuple-element.20), channel_id=1, source_target_pairs={{0,2},{1,3},{2,0},{3,1},{4,6},{5,7},{6,4},{7,5},{8,10},{9,11},{10,... | collective-permute-start | bytes 98312 | tf_op jit(solution)/shard_map/ppermute | solution.py:557
  7.3 7.1 %collective-permute-start.2 = (f32[64,128]{1,0:T(8,128)S(1)}, f32[64,128]{1,0:T(8,128)S(1)}, u32[]{:S(2)}, u32[]{:S(2)}) collective-permute-start(f32[64,128]{1,0:T(8,128)S(1)} %get-tuple-element.21), channel_id=1, source_target_pairs={{2,4},{3,5},{4,2},{5,3},{6,8},{7,9},{8,6},{9,7},{10,12},{11,13},{1... | collective-permute-start | bytes 98312 | tf_op jit(solution)/shard_map/ppermute | solution.py:557

commit v7 on v6

--- a/solution.py
+++ b/solution.py
@@ -7,7 +7,6 @@
 from jax.experimental.pallas import tpu as pltpu
 from jax.sharding import PartitionSpec as P
 
-ITERS = 2
 SUM_FLOOR = 0.5
 TINY = 1e-30
 F32 = jnp.float32
@@ -38,7 +37,7 @@
 THIN_MESSAGE = whole_tiles(EDGE * THIN + 8 - EDGE)
 
 OWN, TWO, SIDE, STRIP = 8, 48, 64, 112
-SPAN = 96
+SPAN = 48
 PADS = (0, 40, 56, 104)
 TILES = tuple((OWN + 8 * k, k) for k in range(4)) + ((TWO, 4),) + tuple((SIDE + 8 * n, (n + 2) % 5) for n in range(5))
 
@@ -308,14 +307,15 @@
     return pbuf[by, bz, u, row : row + 8] if 0 <= u < USED else zeros()
 
 
-def stencil(pbuf, by, bz, u, row, v, w, beside_z=None):
+def stencil(pbuf, by, bz, u, row, v, beside_y, w, beside_z=None):
+    before, after = beside_y
     upper, lower = beside_z or (up_z(v), down_z(v))
     near = w[0] * pbuf[by, bz, u, row + 1 : row + 9] + w[1] * pbuf[by, bz, u, row - 1 : row + 7]
-    near += w[2] * up_y(v, tile_of(pbuf, by, bz, u + 1, row)) + w[3] * down_y(v, tile_of(pbuf, by, bz, u - 1, row))
+    near += w[2] * up_y(v, after) + w[3] * down_y(v, before)
     return near + (w[4] * upper + w[5] * lower)
 
 
-def relax(pbuf, qbuf, sup, wbuf, by, tiles, zbuf=None, shift=None, spans=()):
+def relax(pbuf, qbuf, sup, wbuf, by, tiles, zbuf=None, shift=None, spans=(), unfinished=()):
     if spans:
         count = sum(b - a for a, b in spans)
         v = jnp.concatenate([pbuf[by, :, :, a:b] for a, b in spans], axis=2).reshape(2 * USED * count, 128)
@@ -328,18 +328,36 @@
     for a, b in spans:
         for row in range(a, b, 8):
             places[row] = 8 * len(places)
-    for u in range(USED):
-        for bz in range(2):
-            for row, i in tiles:
-                v = tile_of(pbuf, by, bz, u, row)
-                w = [wbuf[u + 2 * by, d, tile_rows(i)] for d in range(6)]
+    for i in sorted({ring for _, ring in tiles}):
+        lines = [(bz, row) for bz in range(2) for row, ring in tiles if ring == i]
+        before = [zeros()] * len(lines)
+        here = [pbuf[by, bz, 0, row : row + 8] for bz, row in lines]
+        for u in range(USED):
+            w = [wbuf[u + 2 * by, d, tile_rows(i)] for d in range(6)]
+            after = [tile_of(pbuf, by, bz, u + 1, row) for bz, row in lines]
+            for n, (bz, row) in enumerate(lines):
+                v = here[n]
                 beside_z = None
                 if spans:
                     at = slice(places[row], places[row] + 8)
                     beside_z = zbuf[bz, u, at, 0:128], zbuf[bz, u, at, 128:256]
-                near = stencil(pbuf, by, bz, u, row, v, w, beside_z)
-                s = sup[by, bz, u, row : row + 8]
-                qbuf[by, bz, u, row : row + 8] = s * jnp.maximum(v * (1.0 / 3.0) + near, 0.0)
+                near = stencil(pbuf, by, bz, u, row, v, (before[n], after[n]), w, beside_z)
+                kept = v * (1.0 / 3.0) + near
+                if row not in unfinished:
+                    kept = sup[by, bz, u, row : row + 8] * jnp.maximum(kept, 0.0)
+                qbuf[by, bz, u, row : row + 8] = kept
+            before, here = here, after
+
+
+def complete(pbuf, qbuf, sup, wbuf, row, ring, eastward):
+    edge = lax.broadcasted_iota(jnp.int32, (8, 128), 0) == (7 if eastward else 0)
+    at = row + 1 if eastward else row - 1
+    for by in range(2):
+        for u in range(USED):
+            w = jnp.where(edge, wbuf[u + 2 * by, 0 if eastward else 1, tile_rows(ring)], 0.0)
+            for bz in range(2):
+                kept = qbuf[by, bz, u, row : row + 8] + w * jnp.where(edge, pbuf[by, bz, u, at : at + 8], 0.0)
+                qbuf[by, bz, u, row : row + 8] = sup[by, bz, u, row : row + 8] * jnp.maximum(kept, 0.0)
 
 
 def normalise(qbuf, pbuf, tiles, basis_ref=None):
@@ -367,7 +385,7 @@
         pl.when(parity == odd)(functools.partial(body, odd))
 
 
-def begin_kernel(perm_ref, stor_ref, mask_ref, prev_ref, near_ref, rest_ref, first, second, sup, wbuf, gbuf, shift, kbuf, cbuf, qbuf):
+def begin_kernel(perm_ref, stor_ref, mask_ref, prev_ref, near_ref, rest_ref, first, second, sup, wbuf, gbuf, qbuf, shift, kbuf, cbuf):
     here = lax.axis_index("gx")
     last = lax.axis_size("gx") - 1
     deep = lax.broadcasted_iota(jnp.int32, (256, 256), 0) % 128
@@ -396,7 +414,7 @@
         put_cells(first, sup, OWN + 8 * k, found, own_bits[k])
 
     def body(odd):
-        (inner, outer), _ = halves(odd)
+        (inner, outer), (far_inner, _) = halves(odd)
         near = (near_ref, rest_ref, 0)
         sides = (near, None) if odd else (None, near)
         fill_coefficients((1, 2, outer, 4), kbuf, perm_ref, PERM_AT, CELLS, sides)
@@ -416,14 +434,21 @@
         for by in range(2):
             relax(first, qbuf, sup, wbuf, by, tiles)
         normalise(qbuf, second, tiles)
+        for by in range(2):
+            for bz in range(2):
+                for u in range(USED):
+                    for row in (OWN + 8 * far_inner, side_row(4)):
+                        second[by, bz, u, row : row + 8] = zeros()
+        for by in range(2):
+            relax(second, qbuf, sup, wbuf, by, tiles, unfinished=(OWN + 8 * inner, side_row(outer)))
 
     by_parity(body)
 
 
 def finish_kernel(
-    far_ref, far2_ref, near2_ref, near_ref, rest_ref, perm_ref, stor_ref, shift, _first, _second, _sup, _wbuf, _gbuf,
-    basis_ref, coarse_ref, first, second, sup, wbuf, gbuf,
-    kbuf, cbuf, qbuf, sums, zbuf,
+    far_ref, far2_ref, near2_ref, near_ref, rest_ref, perm_ref, stor_ref, shift, _first, _second, _sup, _wbuf, _gbuf, _qbuf,
+    basis_ref, coarse_ref, first, second, sup, wbuf, gbuf, qbuf,
+    kbuf, cbuf, sums, zbuf,
 ):
     here = lax.axis_index("gx")
     odd_chip = lax.rem(here // 2, 2) == 1
@@ -436,7 +461,7 @@
         return jnp.where(low_rows, right, left)
 
     def body(odd):
-        (_, near_outer), (inner, outer) = halves(odd)
+        (near_inner, near_outer), (inner, outer) = halves(odd)
         near, far = (near_ref, rest_ref, 0), (far_ref, far_ref, REST_AT)
         sides = (near, far) if odd else (far, near)
         fill_coefficients((1, 2, near_outer, outer, 4), kbuf, perm_ref, PERM_AT, CELLS, sides)
@@ -460,16 +485,15 @@
         for by in range(2):
             relax(first, qbuf, sup, wbuf, by, tiles, zbuf, shift, spans)
         normalise(qbuf, second, tiles)
+        for by in range(2):
+            relax(second, qbuf, sup, wbuf, by, tiles, zbuf, shift, spans)
+        complete(second, qbuf, sup, wbuf, OWN + 8 * near_inner, near_inner, odd == 1)
+        complete(second, qbuf, sup, wbuf, side_row(near_outer), near_outer, odd == 0)
 
     by_parity(body)
 
-    pbuf, other = second, first
-    for sweep in range(1, ITERS):
-        for by in range(2):
-            relax(pbuf, qbuf, sup, wbuf, by, TILES, zbuf, shift, ((OWN, OWN + SPAN),))
-        normalise(qbuf, other, TILES, basis_ref if sweep == ITERS - 1 else None)
-        pbuf, other = other, pbuf
-
+    pbuf = first
+    normalise(qbuf, pbuf, TILES, basis_ref)
     for by in range(2):
         for bz in range(2):
             at = 0 if by == 0 else 768
@@ -481,25 +505,25 @@
             u = t - 2 * by
             weights = [[wbuf[t, d, tile_rows(i)] for d in range(6)] for i in range(5)]
             scale = [gbuf[t, 8 * i : 8 * i + 8] for i in range(5)]
-            images = []
-            for bz in range(2):
-                image = []
-                for k in range(4):
-                    row = OWN + 8 * k
+            images = [[], []]
+            for k in range(4):
+                row = OWN + 8 * k
+                for bz in range(2):
+                    beside_y = tile_of(pbuf, by, bz, u - 1, row), tile_of(pbuf, by, bz, u + 1, row)
                     if 0 <= u < USED:
                         v = tile_of(pbuf, by, bz, u, row)
-                        image.append(scale[k] * (v * (2.0 / 3.0) - stencil(pbuf, by, bz, u, row, v, weights[k])))
+                        near = stencil(pbuf, by, bz, u, row, v, beside_y, weights[k])
+                        images[bz].append(scale[k] * (v * (2.0 / 3.0) - near))
                     elif u < 0:
-                        image.append(-scale[k] * (weights[k][2] * up_y(zeros(), tile_of(pbuf, by, bz, u + 1, row))))
+                        images[bz].append(-scale[k] * (weights[k][2] * up_y(zeros(), beside_y[1])))
                     else:
-                        image.append(-scale[k] * (weights[k][3] * down_y(zeros(), tile_of(pbuf, by, bz, u - 1, row))))
-                before = beyond = None
-                if 0 <= u < USED:
-                    edge = pbuf[by, bz, u, OWN + 31 : OWN + 39]
-                    beyond = -scale[4] * (weights[4][1] * edge)
-                    edge = pbuf[by, bz, u, OWN - 7 : OWN + 1]
-                    before = -scale[4] * (weights[4][0] * edge)
-                images.append((image, before, beyond))
+                        images[bz].append(-scale[k] * (weights[k][3] * down_y(zeros(), beside_y[0])))
+            ends = [None, None]
+            if 0 <= u < USED:
+                for bz in range(2):
+                    beyond = -scale[4] * (weights[4][1] * pbuf[by, bz, u, OWN + 31 : OWN + 39])
+                    before = -scale[4] * (weights[4][0] * pbuf[by, bz, u, OWN - 7 : OWN + 1])
+                    ends[bz] = before, beyond
             for partner in range(BLOCKS):
                 by2, bz2 = divmod(partner, 2)
                 u2 = t - 2 * by2
@@ -508,14 +532,14 @@
                 own = [tile_of(pbuf, by2, bz2, u2, OWN + 8 * k) for k in range(4)]
                 side = [tile_of(pbuf, by2, bz2, u2, SIDE + 8 * k) for k in range(5)]
                 for bz in range(2):
-                    image, before, beyond = images[bz]
+                    image = images[bz]
                     at = bz * 12 + partner
                     acc[at] += [image[0] * side[3], image[1] * side[4]]
                     acc[at + 4] += [image[k] * own[k] for k in range(4)]
                     acc[at + 8] += [image[2] * side[0], image[3] * side[1]]
-                    if before is not None:
-                        acc[at] += [before * side[2]]
-                        acc[at + 8] += [beyond * side[2]]
+                    if ends[bz] is not None:
+                        acc[at] += [ends[bz][0] * side[2]]
+                        acc[at + 8] += [ends[bz][1] * side[2]]
             acc = [[functools.reduce(lambda a, b: a + b, terms)] if terms else [] for terms in acc]
         for bz in range(2):
             for n in range(12):
@@ -569,17 +593,14 @@
         pltpu.VMEM(strips, F32),
         pltpu.VMEM((LANE_TILES, 6, 40, 128), F32),
         pltpu.VMEM((LANE_TILES, 40, 128), F32),
-    ]
-    scratch = [
-        pltpu.VMEM((LANE_TILES, 40, 128), F32),
-        pltpu.VMEM((LANE_TILES, 40, 128), F32),
         pltpu.VMEM(strips, F32),
     ]
+    scratch = [pltpu.VMEM((LANE_TILES, 40, 128), F32)] * 2
     limit = pltpu.CompilerParams(vmem_limit_bytes=32 * 1024 * 1024)
     *filled, shift = pl.pallas_call(
         begin_kernel,
         in_specs=[vmem] * 6,
-        out_specs=[vmem] * 6,
+        out_specs=[vmem] * 7,
         out_shape=[*state, pltpu.VMEM((256, 256), jnp.bfloat16)],
         scratch_shapes=scratch,
         compiler_params=limit,
@@ -588,14 +609,14 @@
     )(*own, near, rest)
     return pl.pallas_call(
         finish_kernel,
-        in_specs=[vmem] * 13,
-        out_specs=[vmem] * 7,
+        in_specs=[vmem] * 14,
+        out_specs=[vmem] * 8,
         out_shape=[
             jax.ShapeDtypeStruct(prev_basis.shape, F32),
             jax.ShapeDtypeStruct((*prev_basis.shape[:3], 27), F32),
             *state,
         ],
-        input_output_aliases={8 + n: 2 + n for n in range(5)},
+        input_output_aliases={8 + n: 2 + n for n in range(6)},
         scratch_shapes=[
             *scratch,
             pltpu.VMEM((4, 16, 128), F32),

time: 18.2 us -> 17.8 us (0.978)
  waiting for transfers between devices: 3.61 us -> 3.2 us
    ppermute x5, waiting for transfers between devices: 3.61 us -> 3.2 us  [move(): return lax.ppermute(x, 'gx', [(i, j) for i, j in pairs if 0 <= j < size])]
  transfers between devices with their start and end apart: 5 -> 5, of which waited for: 1 -> 1; matrix products, arithmetic and copies ran while one was open for 0% -> 0% of each run, Pallas kernels for 7% -> 9%
where the time goes in v7:
time: 17.8 us; the launch traced here: 17.6 us
  starting transfers between devices  7.49 us (42%)
  Pallas kernels  6.22 us (35%)
  waiting for transfers between devices  3.2 us (18%)
  between operations  0.68 us (4%)
    ppermute x5, starting transfers between devices, move(): return lax.ppermute(x, 'gx', [(i, j) for i, j in pairs if 0 <= j < size])  7.49 us
    pallas_call x1, Pallas kernels, shards(): pl.pallas_call(finish_kernel, in_specs=[vmem] * 14, out_specs=[vmem] * 8,...  3.21 us
    ppermute x5, waiting for transfers between devices, move(): return lax.ppermute(x, 'gx', [(i, j) for i, j in pairs if 0 <= j < size])  3.2 us
    pallas_call x1, Pallas kernels, shards(): pl.pallas_call(begin_kernel, in_specs=[vmem] * 6, out_specs=[vmem] * 7, o...  1.61 us
    pallas_call x1, Pallas kernels, shards(): pl.pallas_call(pack_kernel, in_specs=[pl.BlockSpec(memory_space=pl.ANY)]...  1.41 us
  transfers between devices with their start and end apart: 5, of which 1 were waited for; matrix products, arithmetic and copies ran while one was open for 0% of the time, Pallas kernels for 9%

profile of v7, /device:TPU:8, one launch (start us, length us, event | category | flops | bytes accessed | tf_op | source)
XLA Modules:
  0.0 17.6 jit_solution(5983674381269656525)
XLA Ops:
  0.6 1.4 %pack.1 = (f32[544,128]{1,0:T(8,128)S(1)}, f32[64,128]{1,0:T(8,128)S(1)}, f32[64,128]{1,0:T(8,128)S(1)}, f32[432,128]{1,0:T(8,128)S(1)}, f32[112,128]{1,0:T(8,12...) custom-call(f32[16,1024]{1,0:T(8,128)} %perm_ref.1, ...), custom_call_target="tpu_custom_call" | custom-call | tf_op jit(solution)/shard_map/pack/pallas_call | solution.py:560
  2.0 2.8 %collective-permute-start = (f32[544,128]{1,0:T(8,128)S(1)}, f32[544,128]{1,0:T(8,128)S(1)}, u32[]{:S(2)}, u32[]{:S(2)}) collective-permute-start(f32[544,128]{1,0:T(8,128)S(1)} %get-tuple-element.20), channel_id=1, source_target_pairs={{1,2},{2,1},{3,4},{4,3},{5,6},{6,5},{7,8},{8,7},{9,10},{10,9},{11,... | collective-permute-start | bytes 835592 | tf_op jit(solution)/shard_map/ppermute | solution.py:581
  4.8 0.9 %collective-permute-start.3 = (f32[432,128]{1,0:T(8,128)S(1)}, f32[432,128]{1,0:T(8,128)S(1)}, u32[]{:S(2)}, u32[]{:S(2)}) collective-permute-start(f32[432,128]{1,0:T(8,128)S(1)} %get-tuple-element.23), channel_id=1, source_target_pairs={{0,1},{1,0},{2,3},{3,2},{4,5},{5,4},{6,7},{7,6},{8,9},{9,8},{10,11... | collective-permute-start | bytes 663560 | tf_op jit(solution)/shard_map/ppermute | solution.py:581
  5.7 0.1 collective-permute-start.4
  5.7 1.5 %collective-permute-start.1 = (f32[64,128]{1,0:T(8,128)S(1)}, f32[64,128]{1,0:T(8,128)S(1)}, u32[]{:S(2)}, u32[]{:S(2)}) collective-permute-start(f32[64,128]{1,0:T(8,128)S(1)} %get-tuple-element.21), channel_id=1, source_target_pairs={{0,2},{1,3},{2,0},{3,1},{4,6},{5,7},{6,4},{7,5},{8,10},{9,11},{10,... | collective-permute-start | bytes 98312 | tf_op jit(solution)/shard_map/ppermute | solution.py:581
  7.3 2.3 %collective-permute-start.2 = (f32[64,128]{1,0:T(8,128)S(1)}, f32[64,128]{1,0:T(8,128)S(1)}, u32[]{:S(2)}, u32[]{:S(2)}) collective-permute-start(f32[64,128]{1,0:T(8,128)S(1)} %get-tuple-element.22), channel_id=1, source_target_pairs={{2,4},{3,5},{4,2},{5,3},{6,8},{7,9},{8,6},{9,7},{10,12},{11,13},{1... | collective-permute-start | bytes 98312 | tf_op jit(solution)/shard_map/ppermute | solution.py:581
  9.6 0.0 collective-permute-done.4.rest_ref
  9.6 0.0 collective-permute-done.3.near_ref
  9.6 1.6 %begin.1 = (f32[2,2,6,112,128]{4,3,2,1,0:T(8,128)S(1)}, f32[2,2,6,112,128]{4,3,2,1,0:T(8,128)S(1)}, f32[2,2,6,112,128]{4,3,2,1,0:T(8,128)S(1)}, f32[8,6,40,128]{...) custom-call(f32[16,1024]{1,0:T(8,128)S(1)} %get-tuple-element.25.per, ...), custom_call_target="tpu_custom_call" | custom-call | tf_op jit(solution)/shard_map/begin/pallas_call | solution.py:600
  11.2 3.2 %collective-permute-done.1.far2_ref = f32[64,128]{1,0:T(8,128)S(1)} collective-permute-done((f32[64,128]{1,0:T(8,128)S(1)}, f32[64,128]{1,0:T(8,128)S(1)}, u32[]{:S(2)}, u32[]{:S(2)}) %collective-permute-start.1) | collective-permute-done | bytes 32800 | tf_op jit(solution)/shard_map/ppermute | solution.py:581
  14.4 0.0 collective-permute-done.2.near2_ref
  14.4 0.0 collective-permute-done.far_ref
  14.4 3.2 %finish.1 = (f32[1,2,2,32,1024]{4,3,2,1,0:T(8,128)}, f32[1,2,2,27]{3,2,1,0:T(2,128)}, f32[2,2,6,112,128]{4,3,2,1,0:T(8,128)S(1)}, f32[2,2,6,112,128]{4,3,2,1,0:T...) custom-call(f32[544,128]{1,0:T(8,128)S(1)} %collective-permute-done., ...), custom_call_target="tpu_custom_call", output_to_operand_aliasing={{2}: (8, {}), {3}: (9, {}), {4}: (10, {}), {5}: (11, {}), {... | custom-call | tf_op jit(solution)/shard_map/finish/pallas_call | solution.py:610
Async XLA Ops:
  2.0 12.3 %collective-permute-start = (f32[544,128]{1,0:T(8,128)S(1)}, f32[544,128]{1,0:T(8,128)S(1)}, u32[]{:S(2)}, u32[]{:S(2)}) collective-permute-start(f32[544,128]{1,0:T(8,128)S(1)} %get-tuple-element.20), channel_id=1, source_target_pairs={{1,2},{2,1},{3,4},{4,3},{5,6},{6,5},{7,8},{8,7},{9,10},{10,9},{11,... | collective-permute-start | bytes 835592 | tf_op jit(solution)/shard_map/ppermute | solution.py:581
  4.8 4.8 %collective-permute-start.3 = (f32[432,128]{1,0:T(8,128)S(1)}, f32[432,128]{1,0:T(8,128)S(1)}, u32[]{:S(2)}, u32[]{:S(2)}) collective-permute-start(f32[432,128]{1,0:T(8,128)S(1)} %get-tuple-element.23), channel_id=1, source_target_pairs={{0,1},{1,0},{2,3},{3,2},{4,5},{5,4},{6,7},{7,6},{8,9},{9,8},{10,11... | collective-permute-start | bytes 663560 | tf_op jit(solution)/shard_map/ppermute | solution.py:581
  5.7 3.9 %collective-permute-start.4 = (f32[112,128]{1,0:T(8,128)S(1)}, f32[112,128]{1,0:T(8,128)S(1)}, u32[]{:S(2)}, u32[]{:S(2)}) collective-permute-start(f32[112,128]{1,0:T(8,128)S(1)} %get-tuple-element.24), channel_id=1, source_target_pairs={{0,1},{1,0},{2,3},{3,2},{4,5},{5,4},{6,7},{7,6},{8,9},{9,8},{10,11... | collective-permute-start | bytes 172040 | tf_op jit(solution)/shard_map/ppermute | solution.py:581
  5.7 8.6 %collective-permute-start.1 = (f32[64,128]{1,0:T(8,128)S(1)}, f32[64,128]{1,0:T(8,128)S(1)}, u32[]{:S(2)}, u32[]{:S(2)}) collective-permute-start(f32[64,128]{1,0:T(8,128)S(1)} %get-tuple-element.21), channel_id=1, source_target_pairs={{0,2},{1,3},{2,0},{3,1},{4,6},{5,7},{6,4},{7,5},{8,10},{9,11},{10,... | collective-permute-start | bytes 98312 | tf_op jit(solution)/shard_map/ppermute | solution.py:581
  7.3 7.1 %collective-permute-start.2 = (f32[64,128]{1,0:T(8,128)S(1)}, f32[64,128]{1,0:T(8,128)S(1)}, u32[]{:S(2)}, u32[]{:S(2)}) collective-permute-start(f32[64,128]{1,0:T(8,128)S(1)} %get-tuple-element.22), channel_id=1, source_target_pairs={{2,4},{3,5},{4,2},{5,3},{6,8},{7,9},{8,6},{9,7},{10,12},{11,13},{1... | collective-permute-start | bytes 98312 | tf_op jit(solution)/shard_map/ppermute | solution.py:581

commit v8 on v7

--- a/solution.py
+++ b/solution.py
@@ -106,9 +106,9 @@
     pieces += [perm_tile(leftward, t) for t in range(LANE_TILES)]
     pieces += [stor_tile(leftward, t) for t in range(LANE_TILES)]
     pieces += [mask_tile(2)]
+    end = rest_at + MESSAGE - REST_AT
+    rest_ref[end - 8 : end] = zeros()
     put_edges(rest_ref, rest_at, pieces, 1 - leftward)
-    tail, end = rest_at + EDGE * REST, rest_at + MESSAGE - REST_AT
-    rest_ref[tail:end] = jnp.zeros((end - tail, 128), F32)
 
 
 def eight(tile):
@@ -118,9 +118,8 @@
 def put_thin(out_ref, leftward, prev_tile, mask_tile):
     edge = 3 - 3 * leftward
     pieces = cells(functools.partial(prev_tile, edge)) + [mask_tile(edge)]
+    out_ref[THIN_MESSAGE - 8 : THIN_MESSAGE] = zeros()
     put_edges(out_ref, 0, pieces, 1 - leftward)
-    tail = EDGE * THIN
-    out_ref[tail:THIN_MESSAGE] = jnp.zeros((THIN_MESSAGE - tail, 128), F32)
 
 
 def pack_kernel(

time: 17.8 us -> 17.8 us (level)
  no operation moved by 1% of the time
where the time goes in v8:
time: 17.8 us; the launch traced here: 17.6 us
  starting transfers between devices  7.49 us (42%)
  Pallas kernels  6.22 us (35%)
  waiting for transfers between devices  3.2 us (18%)
  between operations  0.68 us (4%)
    ppermute x5, starting transfers between devices, move(): return lax.ppermute(x, 'gx', [(i, j) for i, j in pairs if 0 <= j < size])  7.49 us
    pallas_call x1, Pallas kernels, shards(): pl.pallas_call(finish_kernel, in_specs=[vmem] * 14, out_specs=[vmem] * 8,...  3.21 us
    ppermute x5, waiting for transfers between devices, move(): return lax.ppermute(x, 'gx', [(i, j) for i, j in pairs if 0 <= j < size])  3.2 us
    pallas_call x1, Pallas kernels, shards(): pl.pallas_call(begin_kernel, in_specs=[vmem] * 6, out_specs=[vmem] * 7, o...  1.61 us
    pallas_call x1, Pallas kernels, shards(): pl.pallas_call(pack_kernel, in_specs=[pl.BlockSpec(memory_space=pl.ANY)]...  1.4 us
  transfers between devices with their start and end apart: 5, of which 1 were waited for; matrix products, arithmetic and copies ran while one was open for 0% of the time, Pallas kernels for 9%

profile of v8, /device:TPU:8, one launch (start us, length us, event | category | flops | bytes accessed | tf_op | source)
XLA Modules:
  0.0 17.6 jit_solution(6233273808141153676)
XLA Ops:
  0.6 1.4 %pack.1 = (f32[544,128]{1,0:T(8,128)S(1)}, f32[64,128]{1,0:T(8,128)S(1)}, f32[64,128]{1,0:T(8,128)S(1)}, f32[432,128]{1,0:T(8,128)S(1)}, f32[112,128]{1,0:T(8,12...) custom-call(f32[16,1024]{1,0:T(8,128)} %perm_ref.1, ...), custom_call_target="tpu_custom_call" | custom-call | tf_op jit(solution)/shard_map/pack/pallas_call | solution.py:559
  2.0 2.8 %collective-permute-start = (f32[544,128]{1,0:T(8,128)S(1)}, f32[544,128]{1,0:T(8,128)S(1)}, u32[]{:S(2)}, u32[]{:S(2)}) collective-permute-start(f32[544,128]{1,0:T(8,128)S(1)} %get-tuple-element.20), channel_id=1, source_target_pairs={{1,2},{2,1},{3,4},{4,3},{5,6},{6,5},{7,8},{8,7},{9,10},{10,9},{11,... | collective-permute-start | bytes 835592 | tf_op jit(solution)/shard_map/ppermute | solution.py:580
  4.8 0.9 %collective-permute-start.3 = (f32[432,128]{1,0:T(8,128)S(1)}, f32[432,128]{1,0:T(8,128)S(1)}, u32[]{:S(2)}, u32[]{:S(2)}) collective-permute-start(f32[432,128]{1,0:T(8,128)S(1)} %get-tuple-element.23), channel_id=1, source_target_pairs={{0,1},{1,0},{2,3},{3,2},{4,5},{5,4},{6,7},{7,6},{8,9},{9,8},{10,11... | collective-permute-start | bytes 663560 | tf_op jit(solution)/shard_map/ppermute | solution.py:580
  5.7 0.1 collective-permute-start.4
  5.7 1.5 %collective-permute-start.1 = (f32[64,128]{1,0:T(8,128)S(1)}, f32[64,128]{1,0:T(8,128)S(1)}, u32[]{:S(2)}, u32[]{:S(2)}) collective-permute-start(f32[64,128]{1,0:T(8,128)S(1)} %get-tuple-element.21), channel_id=1, source_target_pairs={{0,2},{1,3},{2,0},{3,1},{4,6},{5,7},{6,4},{7,5},{8,10},{9,11},{10,... | collective-permute-start | bytes 98312 | tf_op jit(solution)/shard_map/ppermute | solution.py:580
  7.3 2.3 %collective-permute-start.2 = (f32[64,128]{1,0:T(8,128)S(1)}, f32[64,128]{1,0:T(8,128)S(1)}, u32[]{:S(2)}, u32[]{:S(2)}) collective-permute-start(f32[64,128]{1,0:T(8,128)S(1)} %get-tuple-element.22), channel_id=1, source_target_pairs={{2,4},{3,5},{4,2},{5,3},{6,8},{7,9},{8,6},{9,7},{10,12},{11,13},{1... | collective-permute-start | bytes 98312 | tf_op jit(solution)/shard_map/ppermute | solution.py:580
  9.6 0.0 collective-permute-done.4.rest_ref
  9.6 0.0 collective-permute-done.3.near_ref
  9.6 1.6 %begin.1 = (f32[2,2,6,112,128]{4,3,2,1,0:T(8,128)S(1)}, f32[2,2,6,112,128]{4,3,2,1,0:T(8,128)S(1)}, f32[2,2,6,112,128]{4,3,2,1,0:T(8,128)S(1)}, f32[8,6,40,128]{...) custom-call(f32[16,1024]{1,0:T(8,128)S(1)} %get-tuple-element.25.per, ...), custom_call_target="tpu_custom_call" | custom-call | tf_op jit(solution)/shard_map/begin/pallas_call | solution.py:599
  11.2 3.2 %collective-permute-done.1.far2_ref = f32[64,128]{1,0:T(8,128)S(1)} collective-permute-done((f32[64,128]{1,0:T(8,128)S(1)}, f32[64,128]{1,0:T(8,128)S(1)}, u32[]{:S(2)}, u32[]{:S(2)}) %collective-permute-start.1) | collective-permute-done | bytes 32800 | tf_op jit(solution)/shard_map/ppermute | solution.py:580
  14.4 0.0 collective-permute-done.2.near2_ref
  14.4 0.0 collective-permute-done.far_ref
  14.4 3.2 %finish.1 = (f32[1,2,2,32,1024]{4,3,2,1,0:T(8,128)}, f32[1,2,2,27]{3,2,1,0:T(2,128)}, f32[2,2,6,112,128]{4,3,2,1,0:T(8,128)S(1)}, f32[2,2,6,112,128]{4,3,2,1,0:T...) custom-call(f32[544,128]{1,0:T(8,128)S(1)} %collective-permute-done., ...), custom_call_target="tpu_custom_call", output_to_operand_aliasing={{2}: (8, {}), {3}: (9, {}), {4}: (10, {}), {5}: (11, {}), {... | custom-call | tf_op jit(solution)/shard_map/finish/pallas_call | solution.py:609
Async XLA Ops:
  2.0 12.3 %collective-permute-start = (f32[544,128]{1,0:T(8,128)S(1)}, f32[544,128]{1,0:T(8,128)S(1)}, u32[]{:S(2)}, u32[]{:S(2)}) collective-permute-start(f32[544,128]{1,0:T(8,128)S(1)} %get-tuple-element.20), channel_id=1, source_target_pairs={{1,2},{2,1},{3,4},{4,3},{5,6},{6,5},{7,8},{8,7},{9,10},{10,9},{11,... | collective-permute-start | bytes 835592 | tf_op jit(solution)/shard_map/ppermute | solution.py:580
  4.8 4.8 %collective-permute-start.3 = (f32[432,128]{1,0:T(8,128)S(1)}, f32[432,128]{1,0:T(8,128)S(1)}, u32[]{:S(2)}, u32[]{:S(2)}) collective-permute-start(f32[432,128]{1,0:T(8,128)S(1)} %get-tuple-element.23), channel_id=1, source_target_pairs={{0,1},{1,0},{2,3},{3,2},{4,5},{5,4},{6,7},{7,6},{8,9},{9,8},{10,11... | collective-permute-start | bytes 663560 | tf_op jit(solution)/shard_map/ppermute | solution.py:580
  5.7 3.9 %collective-permute-start.4 = (f32[112,128]{1,0:T(8,128)S(1)}, f32[112,128]{1,0:T(8,128)S(1)}, u32[]{:S(2)}, u32[]{:S(2)}) collective-permute-start(f32[112,128]{1,0:T(8,128)S(1)} %get-tuple-element.24), channel_id=1, source_target_pairs={{0,1},{1,0},{2,3},{3,2},{4,5},{5,4},{6,7},{7,6},{8,9},{9,8},{10,11... | collective-permute-start | bytes 172040 | tf_op jit(solution)/shard_map/ppermute | solution.py:580
  5.7 8.6 %collective-permute-start.1 = (f32[64,128]{1,0:T(8,128)S(1)}, f32[64,128]{1,0:T(8,128)S(1)}, u32[]{:S(2)}, u32[]{:S(2)}) collective-permute-start(f32[64,128]{1,0:T(8,128)S(1)} %get-tuple-element.21), channel_id=1, source_target_pairs={{0,2},{1,3},{2,0},{3,1},{4,6},{5,7},{6,4},{7,5},{8,10},{9,11},{10,... | collective-permute-start | bytes 98312 | tf_op jit(solution)/shard_map/ppermute | solution.py:580
  7.3 7.1 %collective-permute-start.2 = (f32[64,128]{1,0:T(8,128)S(1)}, f32[64,128]{1,0:T(8,128)S(1)}, u32[]{:S(2)}, u32[]{:S(2)}) collective-permute-start(f32[64,128]{1,0:T(8,128)S(1)} %get-tuple-element.22), channel_id=1, source_target_pairs={{2,4},{3,5},{4,2},{5,3},{6,8},{7,9},{8,6},{9,7},{10,12},{11,13},{1... | collective-permute-start | bytes 98312 | tf_op jit(solution)/shard_map/ppermute | solution.py:580

commit v9 on v8

--- a/solution.py
+++ b/solution.py
@@ -130,18 +130,15 @@
     odd_chip = lax.rem(lax.axis_index("gx") // 2, 2)
     copies = []
     for by in range(2):
-        for bz in range(2):
-            blk = 2 * by + bz
-            lanes = pl.ds(128 * box_tile(by, 0), 128 * USED)
-            copies.append((prev_ref.at[0, by, bz, :, lanes], prev.at[blk]))
-            copies.append((mask_ref.at[0, by, bz], mask.at[blk]))
-    copies += [(perm_ref, perm), (stor_ref, stor)]
+        lanes = pl.ds(128 * box_tile(by, 0), 128 * USED)
+        copies.append((prev_ref.at[0, by, :, :, lanes], prev.at[pl.ds(2 * by, 2)]))
+    copies += [(mask_ref.at[0], mask), (perm_ref, perm), (stor_ref, stor)]
     copies = [pltpu.make_async_copy(src, dst, sems.at[n]) for n, (src, dst) in enumerate(copies)]
     for copy in copies:
         copy.start()
     for copy in copies:
         copy.wait()
-    mask_buf[...] = jnp.concatenate([mask[blk] for blk in range(BLOCKS)], axis=1).astype(F32)
+    mask_buf[...] = jnp.concatenate([mask[blk // 2, blk % 2] for blk in range(BLOCKS)], axis=1).astype(F32)
 
     def prev_tile(tile, by, bz, u):
         return prev[2 * by + bz, eight(tile), lanes_of(u)]
@@ -568,8 +565,8 @@
             pltpu.VMEM((BLOCKS, 32, 128 * USED), F32),
         ],
         scratch_shapes=[
-            pltpu.VMEM((BLOCKS, 32, 32), jnp.int32),
-            pltpu.SemaphoreType.DMA((2 * BLOCKS + 2,)),
+            pltpu.VMEM((2, 2, 32, 32), jnp.int32),
+            pltpu.SemaphoreType.DMA((5,)),
         ],
         name="pack",
     )(permeability, storage, support_mask, prev_basis)

time: 17.8 us -> 17.8 us (level)
  no operation moved by 1% of the time
where the time goes in v9:
time: 17.8 us; the launch traced here: 17.5 us
  starting transfers between devices  7.49 us (42%)
  Pallas kernels  6.14 us (34%)
  waiting for transfers between devices  3.2 us (18%)
  between operations  0.68 us (4%)
    ppermute x5, starting transfers between devices, move(): return lax.ppermute(x, 'gx', [(i, j) for i, j in pairs if 0 <= j < size])  7.49 us
    pallas_call x1, Pallas kernels, shards(): pl.pallas_call(finish_kernel, in_specs=[vmem] * 14, out_specs=[vmem] * 8,...  3.21 us
    ppermute x5, waiting for transfers between devices, move(): return lax.ppermute(x, 'gx', [(i, j) for i, j in pairs if 0 <= j < size])  3.2 us
    pallas_call x1, Pallas kernels, shards(): pl.pallas_call(begin_kernel, in_specs=[vmem] * 6, out_specs=[vmem] * 7, o...  1.61 us
    pallas_call x1, Pallas kernels, shards(): pl.pallas_call(pack_kernel, in_specs=[pl.BlockSpec(memory_space=pl.ANY)]...  1.33 us
  transfers between devices with their start and end apart: 5, of which 1 were waited for; matrix products, arithmetic and copies ran while one was open for 0% of the time, Pallas kernels for 9%

profile of v9, /device:TPU:8, one launch (start us, length us, event | category | flops | bytes accessed | tf_op | source)
XLA Modules:
  0.0 17.5 jit_solution(5607989121579584003)
XLA Ops:
  0.6 1.3 %pack.1 = (f32[544,128]{1,0:T(8,128)S(1)}, f32[64,128]{1,0:T(8,128)S(1)}, f32[64,128]{1,0:T(8,128)S(1)}, f32[432,128]{1,0:T(8,128)S(1)}, f32[112,128]{1,0:T(8,12...) custom-call(f32[16,1024]{1,0:T(8,128)} %perm_ref.1, ...), custom_call_target="tpu_custom_call" | custom-call | tf_op jit(solution)/shard_map/pack/pallas_call | solution.py:556
  2.0 2.8 %collective-permute-start = (f32[544,128]{1,0:T(8,128)S(1)}, f32[544,128]{1,0:T(8,128)S(1)}, u32[]{:S(2)}, u32[]{:S(2)}) collective-permute-start(f32[544,128]{1,0:T(8,128)S(1)} %get-tuple-element.20), channel_id=1, source_target_pairs={{1,2},{2,1},{3,4},{4,3},{5,6},{6,5},{7,8},{8,7},{9,10},{10,9},{11,... | collective-permute-start | bytes 835592 | tf_op jit(solution)/shard_map/ppermute | solution.py:577
  4.7 0.9 %collective-permute-start.3 = (f32[432,128]{1,0:T(8,128)S(1)}, f32[432,128]{1,0:T(8,128)S(1)}, u32[]{:S(2)}, u32[]{:S(2)}) collective-permute-start(f32[432,128]{1,0:T(8,128)S(1)} %get-tuple-element.23), channel_id=1, source_target_pairs={{0,1},{1,0},{2,3},{3,2},{4,5},{5,4},{6,7},{7,6},{8,9},{9,8},{10,11... | collective-permute-start | bytes 663560 | tf_op jit(solution)/shard_map/ppermute | solution.py:577
  5.6 0.1 collective-permute-start.4
  5.7 1.5 %collective-permute-start.1 = (f32[64,128]{1,0:T(8,128)S(1)}, f32[64,128]{1,0:T(8,128)S(1)}, u32[]{:S(2)}, u32[]{:S(2)}) collective-permute-start(f32[64,128]{1,0:T(8,128)S(1)} %get-tuple-element.21), channel_id=1, source_target_pairs={{0,2},{1,3},{2,0},{3,1},{4,6},{5,7},{6,4},{7,5},{8,10},{9,11},{10,... | collective-permute-start | bytes 98312 | tf_op jit(solution)/shard_map/ppermute | solution.py:577
  7.2 2.3 %collective-permute-start.2 = (f32[64,128]{1,0:T(8,128)S(1)}, f32[64,128]{1,0:T(8,128)S(1)}, u32[]{:S(2)}, u32[]{:S(2)}) collective-permute-start(f32[64,128]{1,0:T(8,128)S(1)} %get-tuple-element.22), channel_id=1, source_target_pairs={{2,4},{3,5},{4,2},{5,3},{6,8},{7,9},{8,6},{9,7},{10,12},{11,13},{1... | collective-permute-start | bytes 98312 | tf_op jit(solution)/shard_map/ppermute | solution.py:577
  9.5 0.0 collective-permute-done.4.rest_ref
  9.5 0.0 collective-permute-done.3.near_ref
  9.5 1.6 %begin.1 = (f32[2,2,6,112,128]{4,3,2,1,0:T(8,128)S(1)}, f32[2,2,6,112,128]{4,3,2,1,0:T(8,128)S(1)}, f32[2,2,6,112,128]{4,3,2,1,0:T(8,128)S(1)}, f32[8,6,40,128]{...) custom-call(f32[16,1024]{1,0:T(8,128)S(1)} %get-tuple-element.25.per, ...), custom_call_target="tpu_custom_call" | custom-call | tf_op jit(solution)/shard_map/begin/pallas_call | solution.py:596
  11.1 3.2 %collective-permute-done.1.far2_ref = f32[64,128]{1,0:T(8,128)S(1)} collective-permute-done((f32[64,128]{1,0:T(8,128)S(1)}, f32[64,128]{1,0:T(8,128)S(1)}, u32[]{:S(2)}, u32[]{:S(2)}) %collective-permute-start.1) | collective-permute-done | bytes 32800 | tf_op jit(solution)/shard_map/ppermute | solution.py:577
  14.3 0.0 collective-permute-done.2.near2_ref
  14.3 0.0 collective-permute-done.far_ref
  14.3 3.2 %finish.1 = (f32[1,2,2,32,1024]{4,3,2,1,0:T(8,128)}, f32[1,2,2,27]{3,2,1,0:T(2,128)}, f32[2,2,6,112,128]{4,3,2,1,0:T(8,128)S(1)}, f32[2,2,6,112,128]{4,3,2,1,0:T...) custom-call(f32[544,128]{1,0:T(8,128)S(1)} %collective-permute-done., ...), custom_call_target="tpu_custom_call", output_to_operand_aliasing={{2}: (8, {}), {3}: (9, {}), {4}: (10, {}), {5}: (11, {}), {... | custom-call | tf_op jit(solution)/shard_map/finish/pallas_call | solution.py:606
Async XLA Ops:
  2.0 12.3 %collective-permute-start = (f32[544,128]{1,0:T(8,128)S(1)}, f32[544,128]{1,0:T(8,128)S(1)}, u32[]{:S(2)}, u32[]{:S(2)}) collective-permute-start(f32[544,128]{1,0:T(8,128)S(1)} %get-tuple-element.20), channel_id=1, source_target_pairs={{1,2},{2,1},{3,4},{4,3},{5,6},{6,5},{7,8},{8,7},{9,10},{10,9},{11,... | collective-permute-start | bytes 835592 | tf_op jit(solution)/shard_map/ppermute | solution.py:577
  4.7 4.8 %collective-permute-start.3 = (f32[432,128]{1,0:T(8,128)S(1)}, f32[432,128]{1,0:T(8,128)S(1)}, u32[]{:S(2)}, u32[]{:S(2)}) collective-permute-start(f32[432,128]{1,0:T(8,128)S(1)} %get-tuple-element.23), channel_id=1, source_target_pairs={{0,1},{1,0},{2,3},{3,2},{4,5},{5,4},{6,7},{7,6},{8,9},{9,8},{10,11... | collective-permute-start | bytes 663560 | tf_op jit(solution)/shard_map/ppermute | solution.py:577
  5.6 3.9 %collective-permute-start.4 = (f32[112,128]{1,0:T(8,128)S(1)}, f32[112,128]{1,0:T(8,128)S(1)}, u32[]{:S(2)}, u32[]{:S(2)}) collective-permute-start(f32[112,128]{1,0:T(8,128)S(1)} %get-tuple-element.24), channel_id=1, source_target_pairs={{0,1},{1,0},{2,3},{3,2},{4,5},{5,4},{6,7},{7,6},{8,9},{9,8},{10,11... | collective-permute-start | bytes 172040 | tf_op jit(solution)/shard_map/ppermute | solution.py:577
  5.7 8.6 %collective-permute-start.1 = (f32[64,128]{1,0:T(8,128)S(1)}, f32[64,128]{1,0:T(8,128)S(1)}, u32[]{:S(2)}, u32[]{:S(2)}) collective-permute-start(f32[64,128]{1,0:T(8,128)S(1)} %get-tuple-element.21), channel_id=1, source_target_pairs={{0,2},{1,3},{2,0},{3,1},{4,6},{5,7},{6,4},{7,5},{8,10},{9,11},{10,... | collective-permute-start | bytes 98312 | tf_op jit(solution)/shard_map/ppermute | solution.py:577
  7.2 7.1 %collective-permute-start.2 = (f32[64,128]{1,0:T(8,128)S(1)}, f32[64,128]{1,0:T(8,128)S(1)}, u32[]{:S(2)}, u32[]{:S(2)}) collective-permute-start(f32[64,128]{1,0:T(8,128)S(1)} %get-tuple-element.22), channel_id=1, source_target_pairs={{2,4},{3,5},{4,2},{5,3},{6,8},{7,9},{8,6},{9,7},{10,12},{11,13},{1... | collective-permute-start | bytes 98312 | tf_op jit(solution)/shard_map/ppermute | solution.py:577
